TPU v7x, 32 devices: a whole 2x2x4 slice. The times are simulated.
32 devices in a mesh: dp: 4 (over y, core), tensor: 8 (over z, x).
Axes of the slice: x: 2, y: 2, z: 4, core: 2. Of those that a mesh axis runs over, the one named last changes fastest.
Arguments:
- tokens: bfloat16 [1024, 24, 1152], P('tensor', 'dp'), may hold values from -6 to 6
- condition: bfloat16 [24, 1152], P('dp'), may hold values from -6 to 6
- counts: int32 [4], P('dp'), may hold values from 1 to 6, as said below
- ada_weight: bfloat16 [1152, 6912], P(None, 'tensor'), may hold values from -0.1875 to 0.1875
- ada_bias: bfloat16 [6912], P('tensor'), may hold values from -3 to 3
- qkv_weight: bfloat16 [1152, 3, 1152], P(None, None, 'tensor'), may hold values from -0.1875 to 0.1875
- qkv_bias: bfloat16 [2, 1152], P(None, 'tensor'), may hold values from -3 to 3
- out_weight: bfloat16 [1152, 1152], P('tensor'), may hold values from -3 to 3
- out_bias: bfloat16 [1152], replicated, may hold values from -3 to 3
- fc1_weight: bfloat16 [1152, 4608], P(None, 'tensor'), may hold values from -0.1875 to 0.1875
- fc1_bias: bfloat16 [4608], P('tensor'), may hold values from -3 to 3
- fc2_weight: bfloat16 [4608, 1152], P('tensor'), may hold values from -0.25 to 0.25
- fc2_bias: bfloat16 [1152], replicated, may hold values from -3 to 3
- out_grad: bfloat16 [1024, 24, 1152], P('tensor', 'dp'), may hold values from -6 to 6
Outputs:
- output: bfloat16 [1024, 24, 1152], P('tensor', 'dp')
- tokens_grad: float32 [1024, 24, 1152], P('tensor', 'dp')
- condition_grad: float32 [24, 1152], P('dp')
- ada_weight_grad: float32 [1152, 6912], P(None, 'tensor')
- ada_bias_grad: float32 [6912], P('tensor')
- qkv_weight_grad: float32 [1152, 3, 1152], P(None, None, 'tensor')
- qkv_bias_grad: float32 [2, 1152], P(None, 'tensor')
- out_weight_grad: float32 [1152, 1152], P('tensor')
- out_bias_grad: float32 [1152], replicated
- fc1_weight_grad: float32 [1152, 4608], P(None, 'tensor')
- fc1_bias_grad: float32 [4608], P('tensor')
- fc2_weight_grad: float32 [4608, 1152], P('tensor')
- fc2_bias_grad: float32 [1152], replicated
Inputs may be any that keep to these rules, and one draw needn't show every extreme that they name: `counts`: slots of a dp index below its count hold latents, the rest are empty; some dp index holds 6 latents and some holds 1.
All inputs are finite; a program needn't handle non-finite values.
Results may differ from a plain program's by a relative error of at most 0.01145.
The roundings to bfloat16 on the way count: a program that leaves them out, or rounds other values in their place, can miss the bound.
Values may be sent and summed in bfloat16 or wider, within the bound.
No kernel may reach another device: no remote copies, remote signals or barrier semaphores. Data moves between devices by JAX's collectives and lax.ppermute only.
A program may use at most 320 MiB of HBM per device.

v0:
```python
import jax
import jax.numpy as jnp
from jax import lax
from jax.sharding import PartitionSpec as P

HDIM = 72


def layer_norm(values):
    average = jnp.mean(values, axis=-1, keepdims=True)
    centred = values - average
    variance = jnp.mean(centred * centred, axis=-1, keepdims=True)
    return centred * lax.rsqrt(variance + 1e-06)


def gelu_tanh(values):
    return jax.nn.gelu(values, approximate=True)


def attend_forward(query_rows, key_rows, value_rows, block_rows):
    score_scale = query_rows.shape[-1] ** (-0.5)
    starts = jnp.arange(query_rows.shape[0] // block_rows) * block_rows

    def one_block(first_row):
        query_block = lax.dynamic_slice_in_dim(query_rows, first_row, block_rows, 0)
        scores = (
            jnp.einsum("qshe,kshe->shqk", query_block, key_rows, preferred_element_type=jnp.float32)
            * score_scale
        )
        row_peak = jnp.max(scores, axis=-1, keepdims=True)
        raised = jnp.exp(scores - row_peak)
        row_total = jnp.sum(raised, axis=-1, keepdims=True)
        soft_low = (raised / row_total).astype(jnp.bfloat16)
        attended = jnp.einsum(
            "shqk,kshe->qshe", soft_low, value_rows, preferred_element_type=jnp.float32
        )
        return (attended, (row_peak + jnp.log(row_total))[..., 0])

    attended, log_total = lax.map(one_block, starts)
    return (attended.reshape(query_rows.shape), log_total)


def attend_backward(query_rows, key_rows, value_rows, attended_grad, log_total, block_rows):
    score_scale = query_rows.shape[-1] ** (-0.5)
    starts = jnp.arange(query_rows.shape[0] // block_rows) * block_rows

    def one_block(totals, inputs):
        key_total, value_total = totals
        first_row, block_lse = inputs
        query_block = lax.dynamic_slice_in_dim(query_rows, first_row, block_rows, 0)
        grad_block = lax.dynamic_slice_in_dim(attended_grad, first_row, block_rows, 0)
        scores = (
            jnp.einsum("qshe,kshe->shqk", query_block, key_rows, preferred_element_type=jnp.float32)
            * score_scale
        )
        soft = jnp.exp(scores - block_lse[..., None])
        soft_grad = jnp.einsum(
            "qshe,kshe->shqk", grad_block, value_rows, preferred_element_type=jnp.float32
        )
        row_dot = jnp.sum(soft * soft_grad, axis=-1, keepdims=True)
        score_grad = (soft * (soft_grad - row_dot)).astype(jnp.bfloat16)
        query_grad = (
            jnp.einsum("shqk,kshe->qshe", score_grad, key_rows, preferred_element_type=jnp.float32)
            * score_scale
        )
        key_total = (
            key_total
            + jnp.einsum(
                "shqk,qshe->kshe", score_grad, query_block, preferred_element_type=jnp.float32
            )
            * score_scale
        )
        value_total = value_total + jnp.einsum(
            "shqk,qshe->kshe",
            soft.astype(jnp.bfloat16),
            grad_block,
            preferred_element_type=jnp.float32,
        )
        return ((key_total, value_total), query_grad)

    empty = jnp.zeros(key_rows.shape, jnp.float32)
    (key_grad, value_grad), query_grad = lax.scan(one_block, (empty, empty), (starts, log_total))
    return (query_grad.reshape(query_rows.shape), key_grad, value_grad)


def on_device(
    tokens,
    condition,
    counts,
    ada_weight,
    ada_bias,
    qkv_weight,
    qkv_bias,
    out_weight,
    out_bias,
    fc1_weight,
    fc1_bias,
    fc2_weight,
    fc2_bias,
    out_grad,
):
    local_rows, slot_count, model_width = tokens.shape
    groups = lax.axis_size("tensor")
    seq_len = local_rows * groups
    local_width = qkv_weight.shape[2]
    head_local = local_width // HDIM
    block_rows = min(512, seq_len)
    live_mask = (jnp.arange(slot_count) < counts[0]).astype(jnp.float32)[None, :, None]
    silu_value, silu_back = jax.vjp(jax.nn.silu, condition.astype(jnp.float32))
    activated = silu_value.astype(jnp.bfloat16)
    mod_local = jnp.dot(
        activated, ada_weight, preferred_element_type=jnp.float32
    ) + ada_bias.astype(jnp.float32)
    modulation = lax.all_gather(mod_local, "tensor", axis=1, tiled=True)
    shift_attn, scale_attn, gate_attn, shift_mlp, scale_mlp, gate_mlp = [
        modulation[None, :, column * model_width : (column + 1) * model_width]
        for column in range(6)
    ]
    inputs = tokens.astype(jnp.float32)
    normed_attn, attn_norm_back = jax.vjp(layer_norm, inputs)
    hidden_attn = (normed_attn * (1.0 + scale_attn) + shift_attn).astype(jnp.bfloat16)
    hidden_full = lax.all_gather(hidden_attn, "tensor", axis=0, tiled=True)
    bias_three = jnp.stack([qkv_bias[0], jnp.zeros_like(qkv_bias[0]), qkv_bias[1]]).astype(
        jnp.float32
    )
    projected = (
        jnp.einsum("tsd,dcf->tscf", hidden_full, qkv_weight, preferred_element_type=jnp.float32)
        + bias_three
    ).astype(jnp.bfloat16)
    head_shape = (seq_len, slot_count, head_local, HDIM)
    query_rows = projected[:, :, 0].reshape(head_shape)
    key_rows = projected[:, :, 1].reshape(head_shape)
    value_rows = projected[:, :, 2].reshape(head_shape)
    attended, log_total = attend_forward(query_rows, key_rows, value_rows, block_rows)
    attended = attended.reshape(seq_len, slot_count, local_width).astype(jnp.bfloat16)
    picked = attended
    attn_branch = lax.psum_scatter(
        jnp.einsum("tsf,fd->tsd", picked, out_weight, preferred_element_type=jnp.float32),
        "tensor",
        scatter_dimension=0,
        tiled=True,
    ) + out_bias.astype(jnp.float32)
    mixed = inputs + gate_attn * attn_branch
    normed_mlp, mlp_norm_back = jax.vjp(layer_norm, mixed)
    hidden_mlp = (normed_mlp * (1.0 + scale_mlp) + shift_mlp).astype(jnp.bfloat16)
    hidden_mlp_full = lax.all_gather(hidden_mlp, "tensor", axis=0, tiled=True)
    pre_act = jnp.einsum(
        "tsd,df->tsf", hidden_mlp_full, fc1_weight, preferred_element_type=jnp.float32
    ) + fc1_bias.astype(jnp.float32)
    activ_value, gelu_back = jax.vjp(gelu_tanh, pre_act)
    activ = activ_value.astype(jnp.bfloat16)
    picked = activ
    mlp_branch = lax.psum_scatter(
        jnp.einsum("tsf,fd->tsd", picked, fc2_weight, preferred_element_type=jnp.float32),
        "tensor",
        scatter_dimension=0,
        tiled=True,
    ) + fc2_bias.astype(jnp.float32)
    output = (live_mask * (mixed + gate_mlp * mlp_branch)).astype(jnp.bfloat16)
    upstream = live_mask * out_grad.astype(jnp.float32)
    branch_grad = (gate_mlp * upstream).astype(jnp.bfloat16)
    gate_mlp_grad = jnp.sum(upstream * mlp_branch, axis=0)
    fc2_bias_part = jnp.sum(branch_grad, axis=(0, 1), dtype=jnp.float32)
    branch_full = lax.all_gather(branch_grad, "tensor", axis=0, tiled=True)
    activ_grad = jnp.einsum(
        "tsd,fd->tsf", branch_full, fc2_weight, preferred_element_type=jnp.float32
    )
    pre_grad = gelu_back(activ_grad)[0].astype(jnp.bfloat16)
    fc2_weight_grad = jnp.einsum(
        "tsf,tsd->fd", activ, branch_full, preferred_element_type=jnp.float32
    )
    fc1_weight_grad = jnp.einsum(
        "tsd,tsf->df", hidden_mlp_full, pre_grad, preferred_element_type=jnp.float32
    )
    fc1_bias_grad = jnp.sum(pre_grad, axis=(0, 1), dtype=jnp.float32)
    picked = pre_grad
    hidden_mlp_grad = lax.psum_scatter(
        jnp.einsum("tsf,df->tsd", picked, fc1_weight, preferred_element_type=jnp.float32),
        "tensor",
        scatter_dimension=0,
        tiled=True,
    )
    shift_mlp_grad = jnp.sum(hidden_mlp_grad, axis=0)
    scale_mlp_grad = jnp.sum(hidden_mlp_grad * normed_mlp, axis=0)
    mixed_grad = upstream + mlp_norm_back(hidden_mlp_grad * (1.0 + scale_mlp))[0]
    gate_attn_grad = jnp.sum(mixed_grad * attn_branch, axis=0)
    attn_grad = (gate_attn * mixed_grad).astype(jnp.bfloat16)
    out_bias_part = jnp.sum(attn_grad, axis=(0, 1), dtype=jnp.float32)
    attn_grad_full = lax.all_gather(attn_grad, "tensor", axis=0, tiled=True)
    out_weight_grad = jnp.einsum(
        "tsf,tsd->fd", attended, attn_grad_full, preferred_element_type=jnp.float32
    )
    attended_grad = jnp.einsum(
        "tsd,fd->tsf", attn_grad_full, out_weight, preferred_element_type=jnp.float32
    ).astype(jnp.bfloat16)
    query_grad, key_grad, value_grad = attend_backward(
        query_rows, key_rows, value_rows, attended_grad.reshape(head_shape), log_total, block_rows
    )
    projected_grad = (
        jnp.stack([query_grad, key_grad, value_grad], axis=2)
        .reshape(seq_len, slot_count, 3, local_width)
        .astype(jnp.bfloat16)
    )
    qkv_weight_grad = jnp.einsum(
        "tsd,tscf->dcf", hidden_full, projected_grad, preferred_element_type=jnp.float32
    )
    qkv_bias_grad = jnp.stack(
        [
            jnp.sum(projected_grad[:, :, 0], axis=(0, 1), dtype=jnp.float32),
            jnp.sum(projected_grad[:, :, 2], axis=(0, 1), dtype=jnp.float32),
        ]
    )
    picked = projected_grad
    hidden_attn_grad = lax.psum_scatter(
        jnp.einsum("tscf,dcf->tsd", picked, qkv_weight, preferred_element_type=jnp.float32),
        "tensor",
        scatter_dimension=0,
        tiled=True,
    )
    shift_attn_grad = jnp.sum(hidden_attn_grad, axis=0)
    scale_attn_grad = jnp.sum(hidden_attn_grad * normed_attn, axis=0)
    tokens_grad = mixed_grad + attn_norm_back(hidden_attn_grad * (1.0 + scale_attn))[0]
    mod_part = jnp.concatenate(
        [
            shift_attn_grad,
            scale_attn_grad,
            gate_attn_grad,
            shift_mlp_grad,
            scale_mlp_grad,
            gate_mlp_grad,
        ],
        axis=1,
    )
    mod_grad = lax.psum_scatter(mod_part, "tensor", scatter_dimension=1, tiled=True).astype(
        jnp.bfloat16
    )
    ada_weight_grad = jnp.dot(activated.T, mod_grad, preferred_element_type=jnp.float32)
    ada_bias_grad = jnp.sum(mod_grad, axis=0, dtype=jnp.float32)
    cond_part = jnp.dot(mod_grad, ada_weight.T, preferred_element_type=jnp.float32)
    cond_sum, out_bias_sum, fc2_bias_sum = lax.psum(
        (cond_part, out_bias_part, fc2_bias_part), "tensor"
    )
    condition_grad = silu_back(cond_sum)[0]
    summed = lax.psum(
        (
            ada_weight_grad,
            ada_bias_grad,
            qkv_weight_grad,
            qkv_bias_grad,
            out_weight_grad,
            out_bias_sum,
            fc1_weight_grad,
            fc1_bias_grad,
            fc2_weight_grad,
            fc2_bias_sum,
        ),
        "dp",
    )
    return (
        output,
        tokens_grad,
        condition_grad,
        summed[0],
        summed[1],
        summed[2],
        summed[3],
        summed[4],
        summed[5],
        summed[6],
        summed[7],
        summed[8],
        summed[9],
    )


def solution(mesh):
    return jax.shard_map(
        on_device,
        mesh=mesh,
        in_specs=(
            P("tensor", "dp", None),
            P("dp", None),
            P("dp"),
            P(None, "tensor"),
            P("tensor"),
            P(None, None, "tensor"),
            P(None, "tensor"),
            P("tensor", None),
            P(),
            P(None, "tensor"),
            P("tensor"),
            P("tensor", None),
            P(),
            P("tensor", "dp", None),
        ),
        out_specs=(
            P("tensor", "dp", None),
            P("tensor", "dp", None),
            P("dp", None),
            P(None, "tensor"),
            P("tensor"),
            P(None, None, "tensor"),
            P(None, "tensor"),
            P("tensor", None),
            P(),
            P(None, "tensor"),
            P("tensor"),
            P("tensor", None),
            P(),
        ),
        check_vma=False,
    )
```

profile of v0, /device:TPU:0, one launch (start us, length us, event | category | flops | bytes accessed | tf_op | source)
XLA Modules:
  0.0 3350.8 jit_solution(16556652899242488160)
XLA Ops:
  13.2 32.6 all-gather
  51.6 196.3 %all-gather.6.cloned.1.call-done = bf16[1024,6,1152]{2,0,1:T(8,128)(2,1)} async-done(((bf16[128,6,1152]{2,0,1:T(8,128)(2,1)}), bf16[1024,6,1152]{2,0,1:T(8,128)(2,1)}) %all-gather.6.cloned.1.call-update) | async-done | bytes 14155792 | tf_op jit(solution)/shard_map/all_gather | solution.py:122
  247.9 14.6 add_convert_fusion
  266.5 79.8 %while.27 = (s32[]{:T(128)}, bf16[2,512,6,2,72]{1,4,3,2,0:T(8,128)(2,1)}, f32[2,6,2,512]{3,2,1,0:T(2,128)S(1)}, s32[2]{0:T(128)S(1)}, bf16[1024,6,2,72]{0,3,2,1:...) while((s32[]{:T(128)}, ...), condition=%wide.region_5.6_spmd, body=%wide.region_2.5_spmd.sunk | while | flops 1868556288 | bytes 103121144 | solution.py:39
  269.0 13.8 multiply_reduce_fusion.9
  282.9 11.3 fusion.123
  294.2 10.9 bitcast_dynamic-update-slice_fusion.6
  308.9 13.8 multiply_reduce_fusion.9
  322.7 11.3 fusion.123
  334.0 10.9 bitcast_dynamic-update-slice_fusion.6
  350.9 5.3 convert_element_type.113
  356.2 12.7 fusion.64
  369.6 446.5 %reduce-scatter.8.cloned.1.call-done = f32[128,6,1152]{2,0,1:T(8,128)} async-done(((f32[1024,6,1152]{2,0,1:T(8,128)}), f32[128,6,1152]{2,0,1:T(8,128)}) %reduce-scatter.8.cloned.1.call-update) | async-done | bytes 3538960 | tf_op jit(solution)/shard_map/reduce_scatter | solution.py:137
  828.3 190.1 %all-gather.8.cloned.1.call-done = bf16[1024,6,1152]{2,0,1:T(8,128)(2,1)} async-done(((bf16[128,6,1152]{2,0,1:T(8,128)(2,1)}), bf16[1024,6,1152]{2,0,1:T(8,128)(2,1)}) %all-gather.8.cloned.1.call-update) | async-done | bytes 14155792 | tf_op jit(solution)/shard_map/all_gather | solution.py:146
  1018.4 16.1 fusion.54
  1034.5 180.5 %all-gather.10.cloned.1.call-done = bf16[1024,6,1152]{2,0,1:T(8,128)(2,1)} async-done(((bf16[128,6,1152]{2,0,1:T(8,128)(2,1)}), bf16[1024,6,1152]{2,0,1:T(8,128)(2,1)}) %all-gather.10.cloned.1.call-update) | async-done | bytes 14155792 | tf_op jit(solution)/shard_map/all_gather | solution.py:164
  1215.1 24.1 convert_reduce_fusion
  1239.2 18.7 fusion.52
  1258.0 23.3 fusion.57
  1282.0 423.1 %reduce-scatter.12.cloned.1.call-done = f32[128,6,1152]{2,0,1:T(8,128)} async-done(((f32[1024,6,1152]{2,0,1:T(8,128)}), f32[128,6,1152]{2,0,1:T(8,128)}) %reduce-scatter.12.cloned.1.call-update) | async-done | bytes 3538960 | tf_op jit(solution)/shard_map/reduce_scatter | solution.py:177
  1712.5 444.2 %reduce-scatter.10.cloned.1.call-done = f32[128,6,1152]{2,0,1:T(8,128)} async-done(((f32[1024,6,1152]{2,0,1:T(8,128)}), f32[128,6,1152]{2,0,1:T(8,128)}) %reduce-scatter.10.cloned.1.call-update) | async-done | bytes 3538960 | tf_op jit(solution)/shard_map/reduce_scatter | solution.py:153
  2156.7 8.4 multiply_reduce_fusion.2
  2165.2 194.8 %all-gather.12.cloned.1.call-done = bf16[1024,6,1152]{2,0,1:T(8,128)(2,1)} async-done(((bf16[128,6,1152]{2,0,1:T(8,128)(2,1)}), bf16[1024,6,1152]{2,0,1:T(8,128)(2,1)}) %all-gather.12.cloned.1.call-update) | async-done | bytes 14155792 | tf_op jit(solution)/shard_map/all_gather | solution.py:189
  2359.9 11.0 convolution_convert_fusion
  2372.3 177.0 %while.28 = (s32[]{:T(128)}, f32[1024,6,2,72]{0,3,2,1:T(8,128)}, f32[1024,6,2,72]{0,3,2,1:T(8,128)}, bf16[2,512,6,2,72]{1,4,3,2,0:T(8,128)(2,1)}, s32[2]{0:T(128...) while((s32[]{:T(128)}, f32[1024,6,2,72]{0,3,2,1:T(8,128)}, ...), condition=%wide.region_15.16_spmd.clone, body=%wide.region_13.15_spmd.clone.sunk | while | flops 4610205696 | bytes 220766448 | solution.py:82
  2375.4 13.9 fusion.133
  2389.3 12.9 bitcast_add_fusion.5
  2402.2 17.2 multiply_reduce_fusion.10
  2419.4 21.5 multiply_convert_fusion.10
  2440.9 9.9 bitcast_dynamic-update-slice_fusion.8
  2450.8 9.2 bitcast_add_fusion.4
  2462.7 13.8 fusion.133
  2476.5 13.9 bitcast_add_fusion.5
  2490.4 17.2 multiply_reduce_fusion.10
  2507.6 21.5 multiply_convert_fusion.10
  2529.1 9.9 bitcast_dynamic-update-slice_fusion.8
  2539.1 10.1 bitcast_add_fusion.4
  2553.8 5.3 stack.24
  2564.7 13.2 convolution_bitcast_fusion
  2578.0 15.1 convolution_bitcast_fusion.1
  2593.1 20.9 convolution_bitcast_fusion.2
  2614.0 11.1 fusion.48
  2625.1 400.0 %reduce-scatter.14.cloned.1.call-done = f32[128,6,1152]{2,0,1:T(8,128)} async-done(((f32[1024,6,1152]{2,0,1:T(8,128)}), f32[128,6,1152]{2,0,1:T(8,128)}) %reduce-scatter.14.cloned.1.call-update) | async-done | bytes 3538960 | tf_op jit(solution)/shard_map/reduce_scatter | solution.py:214
  3038.5 8.9 convolution_bitcast_fusion.3
  3047.4 69.5 %reduce-scatter.16.cloned.1.call-done = f32[864,6]{1,0:T(8,128)} async-done(((f32[6912,6]{1,0:T(8,128)}), f32[864,6]{1,0:T(8,128)}) %reduce-scatter.16.cloned.1.call-update) | async-done | bytes 20752
  3124.8 36.2 %all-reduce = (f32[6,1152]{1,0:T(8,128)S(1)}, f32[1152]{0:T(1024)S(1)}, f32[1152]{0:T(1024)S(1)}) all-reduce(f32[6,1152]{1,0:T(8,128)S(1)} %fusion.86, f32[1152]{0:T(1024)S(1)} %copy-done.42, f32[1152]{0:T(1024)S(1)} %copy-done.43), channel_id=1, replica_groups=mesh['dp'=4,'tensor'=8] {'tensor'}, use_global_device_ids=true, to_apply=%region_26.27 | all-reduce | flops 9216 | bytes 73728 | tf_op jit(solution)/shard_map/psum | solution.py:240
  3161.0 12.9 all-reduce.1
  3174.6 158.7 %all-reduce.5.cloned.1.call-done = (f32[1152,864]{0,1:T(8,128)}, f32[1152,3,144]{0,2,1:T(8,128)}, f32[144,1152]{1,0:T(8,128)}, f32[1152,576]{0,1:T(8,128)}, f32[576,1152]{1,0:T(8,128)}) async-done(((f32[1152,864]{0,1:T(8,128)}, f32[1152,3,144]{0,2,1:T(8,128)}, f32[144,1152]{1,0:T(8,128)}, f32[1152,576]{0,1:T(8,128)}, f32[576,1152]{1,0:T(8,128)}), (f32[1152,864]{0,1:T(8,128)}, f32[1152,3,144]{0,2,1:T(8,128)}, ...) | async-done | bytes 11943952 | tf_op jit(solution)/shard_map/psum | solution.py:244
  (207 shorter events, 89.2 us)
Async XLA Ops:
  7.2 5.4 copy-start
  7.2 5.4 copy-start.28
  7.2 240.7 %all-gather.6.cloned.1.call-start = ((), (), s32[]{:S(2)}) async-start(), calls=%async_computation.5 | async-start | bytes 15925248 | tf_op jit(solution)/shard_map/all_gather | solution.py:122
  9.9 41.3 %copy-start.34 = (f32[128,6]{0,1:T(8,128)}, f32[128,6]{0,1:T(8,128)S(1)}, u32[]{:S(2)}) copy-start(f32[128,6]{0,1:T(8,128)S(1)} %broadcast_multiply_fusion.1) | copy-start | bytes 9220
  12.6 38.6 %copy-start.38 = (f32[128,6]{0,1:T(8,128)}, f32[128,6]{0,1:T(8,128)S(1)}, u32[]{:S(2)}) copy-start(f32[128,6]{0,1:T(8,128)S(1)} %fusion.72) | copy-start | bytes 9220
  13.2 38.3 %copy-start.48 = (bf16[2,144]{1,0:T(2,128)(2,1)S(1)}, bf16[2,144]{1,0:T(2,128)(2,1)}, u32[]{:S(2)}) copy-start(bf16[2,144]{1,0:T(2,128)(2,1)} %param.24) | copy-start | bytes 1732
  13.2 234.7 %copy-start.52 = (bf16[1152,3,144]{0,2,1:T(8,128)(2,1)S(1)}, bf16[1152,3,144]{0,2,1:T(8,128)(2,1)}, u32[]{:S(2)}) copy-start(bf16[1152,3,144]{0,2,1:T(8,128)(2,1)} %param.23) | copy-start | bytes 2985988
  51.2 764.9 %reduce-scatter.8.cloned.1.call-start = ((), (), s32[]{:S(2)}) async-start(), calls=%async_computation.6 | async-start | bytes 31850496 | tf_op jit(solution)/shard_map/reduce_scatter | solution.py:137
  282.9 11.3 copy-start.5
  282.9 11.3 copy-start.12
  322.6 11.3 copy-start.5
  322.7 11.3 copy-start.12
  346.3 9.9 copy-start.25
  368.9 447.2 %copy-start.27 = (f32[6,1152]{1,0:T(8,128)S(1)}, f32[6,1152]{1,0:T(8,128)}, u32[]{:S(2)}) copy-start(f32[6,1152]{1,0:T(8,128)} %get-tuple-element.222) | copy-start | bytes 82948
  368.9 649.5 %all-gather.8.cloned.1.call-start = ((), (), s32[]{:S(2)}) async-start(), calls=%async_computation.7 | async-start | bytes 15925248 | tf_op jit(solution)/shard_map/all_gather | solution.py:146
  369.6 446.5 %copy-start.36 = (f32[1152]{0:T(1024)}, f32[1152]{0:T(1024)S(1)}, u32[]{:S(2)}) copy-start(f32[1152]{0:T(1024)S(1)} %convert_element_type.114) | copy-start | bytes 13828
  823.5 4.7 copy-start.50
  823.6 391.5 %all-gather.10.cloned.1.call-start = ((), (), s32[]{:S(2)}) async-start(), calls=%async_computation.9 | async-start | bytes 15925248 | tf_op jit(solution)/shard_map/all_gather | solution.py:164
  828.2 876.9 %reduce-scatter.12.cloned.1.call-start = ((), (), s32[]{:S(2)}) async-start(), calls=%async_computation.10 | async-start | bytes 31850496 | tf_op jit(solution)/shard_map/reduce_scatter | solution.py:177
  828.3 429.8 %copy-start.46 = (f32[576]{0:T(1024)}, f32[576]{0:T(1024)S(1)}, u32[]{:S(2)}) copy-start(f32[576]{0:T(1024)S(1)} %convert_element_type.116) | copy-start | bytes 6916
  1215.1 24.1 copy-start.51
  1258.0 898.7 %reduce-scatter.10.cloned.1.call-start = ((), (), s32[]{:S(2)}) async-start(), calls=%async_computation.8 | async-start | bytes 31850496 | tf_op jit(solution)/shard_map/reduce_scatter | solution.py:153
  1281.3 1078.6 %all-gather.12.cloned.1.call-start = ((), (), s32[]{:S(2)}) async-start(), calls=%async_computation.11 | async-start | bytes 15925248 | tf_op jit(solution)/shard_map/all_gather | solution.py:189
  1705.1 4.1 copy-start.2
  1705.1 5.1 copy-start.7
  2165.1 860.0 %reduce-scatter.14.cloned.1.call-start = ((), (), s32[]{:S(2)}) async-start(), calls=%async_computation.12 | async-start | bytes 31850496 | tf_op jit(solution)/shard_map/reduce_scatter | solution.py:214
  2375.4 13.9 copy-start.6
  2462.7 13.8 copy-start.6
  2577.9 15.1 copy-start.47
  2577.9 538.9 %reduce-scatter.16.cloned.1.call-start = ((), (), s32[]{:S(2)}) async-start(), calls=%async_computation.13 | async-start | bytes 3981312
  2593.1 21.0 copy-start.11
  2593.1 21.0 copy-start.15
  2593.1 21.0 copy-start.20
  2614.0 411.1 %copy-start.23 = (f32[6,1152]{1,0:T(8,128)S(1)}, f32[6,1152]{1,0:T(8,128)}, u32[]{:S(2)}) copy-start(f32[6,1152]{1,0:T(8,128)} %copy-done.22) | copy-start | bytes 82948
  2614.0 411.1 %copy-start.35 = (f32[128,6]{0,1:T(8,128)S(1)}, f32[128,6]{0,1:T(8,128)}, u32[]{:S(2)}) copy-start(f32[128,6]{0,1:T(8,128)} %copy-done.34) | copy-start | bytes 9220
  2625.1 403.4 %copy-start.41 = (f32[128,6]{0,1:T(8,128)S(1)}, f32[128,6]{0,1:T(8,128)}, u32[]{:S(2)}) copy-start(f32[128,6]{0,1:T(8,128)} %copy-done.40) | copy-start | bytes 9220
  2625.1 403.5 %copy-start.39 = (f32[128,6]{0,1:T(8,128)S(1)}, f32[128,6]{0,1:T(8,128)}, u32[]{:S(2)}) copy-start(f32[128,6]{0,1:T(8,128)} %copy-done.38) | copy-start | bytes 9220
  3025.1 3.5 copy-start.4
  3025.1 4.1 copy-start.8
  3031.2 4.7 copy-start.31
  3031.3 4.7 copy-start.30
  3031.3 4.7 copy-start.32
  3038.4 79.6 %copy-start.29 = (bf16[6,1152]{1,0:T(8,128)(2,1)S(1)}, bf16[6,1152]{1,0:T(8,128)(2,1)}, u32[]{:S(2)}) copy-start(bf16[6,1152]{1,0:T(8,128)(2,1)} %param.19) | copy-start | bytes 41476
  3038.5 294.8 %all-reduce.5.cloned.1.call-start = ((), (), s32[]{:S(2)}) async-start(), calls=%async_computation.14 | async-start | bytes 23887872 | tf_op jit(solution)/shard_map/psum | solution.py:244
  3120.7 4.1 copy-start.42
  3120.7 4.0 copy-start.43
  3120.8 40.3 %copy-start.49 = (f32[576]{0:T(1024)S(1)}, f32[576]{0:T(1024)}, u32[]{:S(2)}) copy-start(f32[576]{0:T(1024)} %get-tuple-element.225) | copy-start | bytes 6916
  3333.3 4.5 copy-start.18
  (20 other events, 37.7 us)
Sparse Core Ops, SparseCore 0:
  51.3 196.5 all-gather.5
  369.0 446.9 reduce-scatter.7
  823.7 194.6 all-gather.7
  1021.3 193.7 all-gather.9
  1258.1 446.9 reduce-scatter.11
  1708.9 447.7 reduce-scatter.9
  2165.2 194.6 all-gather.11
  2578.0 447.0 reduce-scatter.13
  3038.6 78.2 reduce-scatter.15
  3120.9 212.3 all-reduce.4
where the time goes:
time: 3350 us
  waiting for transfers between devices  2700 us (81%)
  matrix products  371 us (11%)
  other arithmetic  117 us (3%)
  blocking collectives  81.7 us (2%)
  local copies, waits for them, and re-layouts  52.7 us (2%)
    reduce_scatter x1, waiting for transfers between devices, on_device(): lax.psum_scatter(jnp.einsum('tsf,fd->tsd', picked, out_weight, preferred_...  446 us
    reduce_scatter x1, waiting for transfers between devices, on_device(): lax.psum_scatter(jnp.einsum('tsf,fd->tsd', picked, fc2_weight, preferred_...  444 us
    reduce_scatter x1, waiting for transfers between devices, on_device(): lax.psum_scatter(jnp.einsum('tsf,df->tsd', picked, fc1_weight, preferred_...  423 us
    reduce_scatter x1, waiting for transfers between devices, on_device(): lax.psum_scatter(jnp.einsum('tscf,dcf->tsd', picked, qkv_weight, preferre...  400 us
    all_gather x1, waiting for transfers between devices, on_device(): hidden_full = lax.all_gather(hidden_attn, 'tensor', axis=0, tiled=True)  196 us
    all_gather x1, waiting for transfers between devices, on_device(): attn_grad_full = lax.all_gather(attn_grad, 'tensor', axis=0, tiled=True)  195 us
    all_gather x1, waiting for transfers between devices, on_device(): hidden_mlp_full = lax.all_gather(hidden_mlp, 'tensor', axis=0, tiled=True)  190 us
    all_gather x1, waiting for transfers between devices, on_device(): branch_full = lax.all_gather(branch_grad, 'tensor', axis=0, tiled=True)  181 us
  transfers between devices with their start and end apart: 10, of which 10 were waited for; matrix products, arithmetic and copies ran while one was open for 3% of the time, Pallas kernels for 0%

commit v1 on v0

v1 whole, which is shorter than its diff:
```python
import functools

import jax
import jax.numpy as jnp
from jax import lax
from jax.experimental import pallas as pl
from jax.experimental.pallas import tpu as pltpu
from jax.sharding import PartitionSpec as P

HDIM = 72
LOW = jnp.bfloat16
FULL = jnp.float32
LAST = (((1,), (1,)), ((), ()))
FIRST = (((0,), (0,)), ((), ()))
PLAIN = (((1,), (0,)), ((), ()))
ROWS = 256


def dot(left, right, dims=PLAIN):
    return lax.dot_general(left, right, dims, preferred_element_type=FULL)


def layer_norm(values):
    average = jnp.mean(values, axis=-1, keepdims=True)
    centred = values - average
    variance = jnp.mean(centred * centred, axis=-1, keepdims=True)
    scale = lax.rsqrt(variance + 1e-06)
    return centred * scale, scale


def norm_back(normed, scale, grad):
    first = jnp.mean(grad, axis=-1, keepdims=True)
    second = jnp.mean(grad * normed, axis=-1, keepdims=True)
    return (grad - first - normed * second) * scale


def gelu_tanh(values):
    return jax.nn.gelu(values, approximate=True)


def soft_rows(query_block, keys):
    scores = dot(query_block, keys, LAST)
    peak = jnp.max(scores, axis=-1, keepdims=True)
    raised = jnp.exp((scores - peak) * (HDIM**-0.5))
    return raised * (1.0 / jnp.sum(raised, axis=-1, keepdims=True))


def column(head, part):
    return (head * 3 + part) * HDIM


def attend_kernel(heads, base, projected, attended, queries, keys, values, results):
    seq = projected.shape[0]
    block = min(ROWS, seq)
    for head in range(heads):
        for part, held in enumerate((queries, keys, values)):
            at = base + column(head, part)
            held[head] = projected[:, at : at + HDIM]

    def one_head(head, carry):
        key_rows, value_rows = keys[head], values[head]
        for start in range(0, seq, block):
            soft = soft_rows(queries[head, start : start + block], key_rows)
            results[head, start : start + block] = dot(soft.astype(LOW), value_rows).astype(LOW)
        return carry

    lax.fori_loop(0, heads, one_head, 0)
    for head in range(heads):
        attended[:, head * HDIM : (head + 1) * HDIM] = results[head]


def attend(projected, heads, chunk):
    seq = projected.shape[0]
    held = pltpu.VMEM((heads, seq, HDIM), LOW)
    return pl.pallas_call(
        functools.partial(attend_kernel, heads, chunk * column(heads, 0)),
        out_shape=jax.ShapeDtypeStruct((seq, heads * HDIM), LOW),
        in_specs=[pl.BlockSpec(memory_space=pltpu.VMEM)],
        out_specs=pl.BlockSpec(memory_space=pltpu.VMEM),
        scratch_shapes=[held, held, held, held],
        compiler_params=pltpu.CompilerParams(vmem_limit_bytes=48 * 1024 * 1024),
        cost_estimate=pl.CostEstimate(
            flops=heads * seq * seq * 2048,
            bytes_accessed=8 * heads * HDIM * seq,
            transcendentals=heads * seq * seq,
        ),
    )(projected)


def attend_back_kernel(
    heads, base, projected, attended_grad, projected_grad, queries, keys, values, grads
):
    seq = projected.shape[0]
    block = min(ROWS, seq)
    score_scale = HDIM**-0.5
    first = base // 3
    for head in range(heads):
        for part, held in enumerate((queries, keys, values)):
            at = base + column(head, part)
            held[head] = projected[:, at : at + HDIM]
        at = first + head * HDIM
        grads[head] = attended_grad[:, at : at + HDIM]

    def one_head(head, carry):
        key_rows, value_rows = keys[head], values[head]
        key_total = value_total = None
        for start in range(0, seq, block):
            query_block = queries[head, start : start + block]
            grad_block = grads[head, start : start + block]
            soft = soft_rows(query_block, key_rows)
            soft_grad = dot(grad_block, value_rows, LAST)
            row_dot = jnp.sum(soft * soft_grad, axis=-1, keepdims=True)
            score_grad = (soft * (soft_grad - row_dot)).astype(LOW)
            queries[head, start : start + block] = (
                dot(score_grad, key_rows) * score_scale
            ).astype(LOW)
            key_part = dot(query_block, score_grad, FIRST)
            value_part = dot(grad_block, soft.astype(LOW), FIRST)
            key_total = key_part if key_total is None else key_total + key_part
            value_total = value_part if value_total is None else value_total + value_part
        keys[head] = (key_total * score_scale).T.astype(LOW)
        values[head] = value_total.T.astype(LOW)
        return carry

    lax.fori_loop(0, heads, one_head, 0)
    for head in range(heads):
        for part, held in enumerate((queries, keys, values)):
            at = column(head, part)
            projected_grad[:, at : at + HDIM] = held[head]


def attend_back(projected, attended_grad, heads, chunk):
    seq = projected.shape[0]
    held = pltpu.VMEM((heads, seq, HDIM), LOW)
    whole = pl.BlockSpec(memory_space=pltpu.VMEM)
    return pl.pallas_call(
        functools.partial(attend_back_kernel, heads, chunk * column(heads, 0)),
        out_shape=jax.ShapeDtypeStruct((seq, column(heads, 0)), LOW),
        in_specs=[whole, whole],
        out_specs=whole,
        scratch_shapes=[held, held, held, held],
        compiler_params=pltpu.CompilerParams(vmem_limit_bytes=48 * 1024 * 1024),
        cost_estimate=pl.CostEstimate(
            flops=heads * seq * seq * 4096,
            bytes_accessed=14 * heads * HDIM * seq,
            transcendentals=heads * seq * seq,
        ),
    )(projected, attended_grad)


def low(values):
    return lax.optimization_barrier(values.astype(LOW))


def add(*terms):
    total = terms[0].astype(FULL)
    for term in terms[1:]:
        total = total + term.astype(FULL)
    return total


def partner(values, axis, bit):
    return lax.ppermute(values, axis, [(i, i ^ bit) for i in range(lax.axis_size(axis))])


def bits_of(axis, start=1):
    found, bit = [], start
    while bit < lax.axis_size(axis):
        found.append(bit)
        bit *= 2
    return found


def order_by(flag, one, two, axis):
    return jnp.concatenate([jnp.where(flag, two, one), jnp.where(flag, one, two)], axis=axis)


def pair_sum(values, axis, start=1):
    for bit in bits_of(axis, start):
        values = values + partner(values, axis, bit)
    return values


def pair_gather(values, axis):
    here = lax.axis_index(axis)
    held = values[None]
    for bit in bits_of(axis):
        held = order_by((here & bit) != 0, held, partner(held, axis, bit), 0)
    return held


def after(value, *others):
    return lax.optimization_barrier((value, *others))[0]


def gather_weight(shard):
    share = shard.shape[0] // lax.axis_size("dp")
    mine = lax.dynamic_slice_in_dim(shard, lax.axis_index("dp") * share, share, 0)
    return lax.all_gather(mine, ("tensor", "dp"), axis=0, tiled=True)


def reduce_weight(grad):
    mine = lax.psum_scatter(grad, ("tensor", "dp"), scatter_dimension=0, tiled=True)
    return pair_gather(mine, "dp").reshape(-1, grad.shape[1])


def slot_start(slots):
    return (lax.axis_size("tensor") - slots) // 2


def to_slots(pieces):
    slots, rows, width = pieces.shape
    groups, here = lax.axis_size("tensor"), lax.axis_index("tensor")
    start = slot_start(slots)
    parts = []
    for step in range(groups):
        slot = jnp.clip(lax.rem(here + step, groups) - start, 0, slots - 1)
        piece = lax.dynamic_index_in_dim(pieces, slot, 0, False)
        if step:
            pairs = [(i, (i + step) % groups) for i in range(groups)]
            pairs = [pair for pair in pairs if start <= pair[1] < start + slots]
            piece = lax.ppermute(piece, "tensor", pairs)
        parts.append(piece)
    return jnp.concatenate(parts, axis=0)


def from_slots(values, slots):
    groups, here = lax.axis_size("tensor"), lax.axis_index("tensor")
    start = slot_start(slots)
    rows = values.shape[0] // groups
    parts = []
    for step in range(groups):
        piece = values[step * rows : (step + 1) * rows]
        if step:
            pairs = [((i + step) % groups, i) for i in range(groups)]
            pairs = [pair for pair in pairs if start <= pair[0] < start + slots]
            piece = lax.ppermute(piece, "tensor", pairs)
        parts.append(piece)
    twice = jnp.stack(parts + parts, axis=0)
    return lax.dynamic_slice_in_dim(twice, lax.rem(groups + start - here, groups), slots, 0)


def on_device(
    tokens,
    condition,
    counts,
    ada_weight,
    ada_bias,
    qkv_weight,
    qkv_bias,
    out_weight,
    out_bias,
    fc1_weight,
    fc1_bias,
    fc2_weight,
    fc2_bias,
    out_grad,
):
    local_rows, slots, width = tokens.shape
    groups, here = lax.axis_size("tensor"), lax.axis_index("tensor")
    assert slots <= groups
    seq = local_rows * groups
    local_width = qkv_weight.shape[2]
    local = local_width // HDIM
    three = 3 * HDIM
    unit = 4 * HDIM
    start = slot_start(slots)
    hidden_local = fc1_weight.shape[1]
    live = ((here >= start) & (here - start < counts[0])).astype(FULL)

    qkv_rows = jnp.transpose(qkv_weight, (1, 2, 0)).reshape(3, local, HDIM, width)
    out_rows = out_weight.reshape(1, local, HDIM, width)
    first = jnp.transpose(jnp.concatenate([qkv_rows, out_rows]), (1, 0, 2, 3))
    first = gather_weight(first.reshape(local * unit, width)).reshape(groups, local, unit, width)
    fc1_full = gather_weight(fc1_weight.T)
    fc2_full = gather_weight(fc2_weight)
    first = jnp.transpose(first, (1, 0, 2, 3))
    qkv_full = first[:, :, :three].reshape(-1, width)
    out_full = first[:, :, three:].reshape(-1, width)

    silu_value, silu_back = jax.vjp(jax.nn.silu, condition.astype(FULL))
    activated = silu_value.astype(LOW)
    mod_local = dot(activated, ada_weight) + ada_bias.astype(FULL)
    mod_width = mod_local.shape[1]
    qkv_three = jnp.stack([qkv_bias[0], jnp.zeros_like(qkv_bias[0]), qkv_bias[1]])
    qkv_three = jnp.transpose(qkv_three.reshape(3, local, HDIM), (1, 0, 2)).reshape(-1).astype(FULL)
    small = jnp.concatenate([mod_local.reshape(-1), qkv_three, fc1_bias.astype(FULL)])
    small = pair_gather(small, "tensor")
    slot = jnp.clip(here - start, 0, slots - 1)
    modulation = small[:, : slots * mod_width].reshape(groups, slots, mod_width)
    modulation = lax.dynamic_index_in_dim(modulation, slot, 1, False).reshape(6, 1, width)
    shift_attn, scale_attn, gate_attn, shift_mlp, scale_mlp, gate_mlp = modulation
    qkv_bias_full = small[:, slots * mod_width : slots * mod_width + local * three]
    qkv_bias_full = jnp.transpose(qkv_bias_full.reshape(groups, local, three), (1, 0, 2)).reshape(-1)
    fc1_bias_full = small[:, slots * mod_width + local * three :].reshape(-1)

    inputs = to_slots(jnp.transpose(tokens, (1, 0, 2))).astype(FULL)
    normed_attn, attn_scale = layer_norm(inputs)
    hidden_attn = (normed_attn * (1.0 + scale_attn) + shift_attn).astype(LOW)
    projected = (dot(hidden_attn, qkv_full, LAST) + qkv_bias_full).astype(LOW)
    attended = [attend(projected, groups, chunk) for chunk in range(local)]
    attended = jnp.concatenate(attended, axis=1)
    attn_branch = dot(attended, out_full) + out_bias.astype(FULL)
    mixed = inputs + gate_attn * attn_branch
    normed_mlp, mlp_scale = layer_norm(mixed)
    hidden_mlp = (normed_mlp * (1.0 + scale_mlp) + shift_mlp).astype(LOW)
    pre_act = dot(hidden_mlp, fc1_full, LAST) + fc1_bias_full
    activ_value, gelu_back = jax.vjp(gelu_tanh, pre_act)
    activ = activ_value.astype(LOW)
    mlp_branch = dot(activ, fc2_full) + fc2_bias.astype(FULL)
    output = (live * (mixed + gate_mlp * mlp_branch)).astype(LOW)
    output = jnp.transpose(from_slots(output, slots), (1, 0, 2))

    out_grad, _ = lax.optimization_barrier((out_grad, projected))
    upstream = live * to_slots(jnp.transpose(out_grad, (1, 0, 2))).astype(FULL)
    branch_grad = (gate_mlp * upstream).astype(LOW)
    gate_mlp_grad = jnp.sum(upstream * mlp_branch, axis=0)
    fc2_bias_part = jnp.sum(branch_grad, axis=0, dtype=FULL)
    fc2_weight_part = dot(activ, branch_grad, FIRST).astype(LOW)
    fc2_weight_part, branch_grad = lax.optimization_barrier((fc2_weight_part, branch_grad))
    fc2_weight_grad = reduce_weight(fc2_weight_part)
    activ_grad = dot(branch_grad, fc2_full, LAST)
    pre_grad = gelu_back(activ_grad)[0].astype(LOW)
    fc1_weight_part = dot(pre_grad, hidden_mlp, FIRST).astype(LOW)
    fc1_weight_part, pre_grad = lax.optimization_barrier((fc1_weight_part, pre_grad))
    fc1_weight_grad = reduce_weight(fc1_weight_part)
    fc1_bias_part = jnp.sum(pre_grad, axis=0, dtype=FULL)
    hidden_mlp_grad = dot(pre_grad, fc1_full)
    shift_mlp_grad = jnp.sum(hidden_mlp_grad, axis=0)
    scale_mlp_grad = jnp.sum(hidden_mlp_grad * normed_mlp, axis=0)
    mixed_grad = upstream + norm_back(normed_mlp, mlp_scale, hidden_mlp_grad * (1.0 + scale_mlp))
    gate_attn_grad = jnp.sum(mixed_grad * attn_branch, axis=0)
    attn_grad = (gate_attn * mixed_grad).astype(LOW)
    out_bias_part = jnp.sum(attn_grad, axis=0, dtype=FULL)
    out_weight_part = dot(attended, attn_grad, FIRST).astype(LOW)
    attended_grad = dot(attn_grad, out_full, LAST).astype(LOW)
    out_weight_part = out_weight_part.reshape(local, groups, HDIM, width)
    first_parts, projected_grad = [], []
    for chunk in range(local):
        if chunk:
            attended_grad = after(attended_grad, projected_grad[0], fc2_weight_grad)
        part_grad = attend_back(projected, attended_grad, groups, chunk)
        weight_part = dot(part_grad, hidden_attn, FIRST).astype(LOW)
        first_parts.append(weight_part.reshape(groups, three, width))
        first_parts.append(out_weight_part[chunk])
        projected_grad.append(part_grad)
    first_part = jnp.concatenate(first_parts, axis=1).reshape(-1, width)
    projected_grad = after(tuple(projected_grad), first_part, fc1_weight_grad)
    first_grad = reduce_weight(first_part).astype(FULL)
    first_grad = jnp.transpose(first_grad.reshape(local, 4, HDIM, width), (1, 0, 2, 3))
    first_grad = first_grad.reshape(4, local_width, width)
    qkv_weight_grad = jnp.transpose(first_grad[:3], (2, 0, 1))
    out_weight_grad = first_grad[3]
    fc1_weight_grad = fc1_weight_grad.astype(FULL).T
    fc2_weight_grad = fc2_weight_grad.astype(FULL)
    hidden_attn_grad = dot(jnp.concatenate(projected_grad, axis=1), qkv_full)
    qkv_bias_part = jnp.concatenate([jnp.sum(part, axis=0, dtype=FULL) for part in projected_grad])
    shift_attn_grad = jnp.sum(hidden_attn_grad, axis=0)
    scale_attn_grad = jnp.sum(hidden_attn_grad * normed_attn, axis=0)
    tokens_grad = mixed_grad + norm_back(
        normed_attn, attn_scale, hidden_attn_grad * (1.0 + scale_attn)
    )
    tokens_grad = from_slots(tokens_grad.astype(LOW), slots).astype(FULL)
    tokens_grad = jnp.transpose(tokens_grad, (1, 0, 2))

    mod_row = jnp.concatenate(
        [
            shift_attn_grad,
            scale_attn_grad,
            gate_attn_grad,
            shift_mlp_grad,
            scale_mlp_grad,
            gate_mlp_grad,
        ]
    ).astype(LOW)
    mod_mine = pair_gather(mod_row.reshape(groups, mod_width), "tensor")
    mod_mine = lax.dynamic_index_in_dim(mod_mine, here, 1, False)
    mod_grad = pair_gather(mod_mine, "dp").reshape(-1, mod_width)
    activated_all = pair_gather(jnp.pad(activated, ((start, groups - slots - start), (0, 0))), "dp")
    ada_weight_grad = dot(activated_all.reshape(-1, width), mod_grad, FIRST)
    ada_bias_grad = jnp.sum(mod_grad, axis=0, dtype=FULL)
    cond_sum = pair_sum(dot(mod_mine[start : start + slots], ada_weight, LAST), "tensor")
    condition_grad = silu_back(cond_sum)[0]
    bias_sum = jnp.concatenate([out_bias_part, fc2_bias_part, fc1_bias_part, qkv_bias_part])
    bias_sum = pair_sum(pair_sum(bias_sum, "tensor"), "dp")
    out_bias_grad, fc2_bias_grad = bias_sum[:width], bias_sum[width : 2 * width]
    fc1_bias_grad = lax.dynamic_slice_in_dim(bias_sum, 2 * width + here * hidden_local, hidden_local, 0)
    qkv_start = 2 * width + groups * hidden_local
    qkv_bias_sum = bias_sum[qkv_start:].reshape(local, groups, three)
    qkv_bias_sum = lax.dynamic_index_in_dim(qkv_bias_sum, here, 1, False).reshape(local, 3, HDIM)
    qkv_bias_sum = jnp.transpose(qkv_bias_sum, (1, 0, 2)).reshape(3, local_width)
    qkv_bias_grad = jnp.stack([qkv_bias_sum[0], qkv_bias_sum[2]])
    return (
        output,
        tokens_grad,
        condition_grad,
        ada_weight_grad,
        ada_bias_grad,
        qkv_weight_grad,
        qkv_bias_grad,
        out_weight_grad,
        out_bias_grad,
        fc1_weight_grad,
        fc1_bias_grad,
        fc2_weight_grad,
        fc2_bias_grad,
    )


def solution(mesh):
    return jax.shard_map(
        on_device,
        mesh=mesh,
        in_specs=(
            P("tensor", "dp", None),
            P("dp", None),
            P("dp"),
            P(None, "tensor"),
            P("tensor"),
            P(None, None, "tensor"),
            P(None, "tensor"),
            P("tensor", None),
            P(),
            P(None, "tensor"),
            P("tensor"),
            P("tensor", None),
            P(),
            P("tensor", "dp", None),
        ),
        out_specs=(
            P("tensor", "dp", None),
            P("tensor", "dp", None),
            P("dp", None),
            P(None, "tensor"),
            P("tensor"),
            P(None, None, "tensor"),
            P(None, "tensor"),
            P("tensor", None),
            P(),
            P(None, "tensor"),
            P("tensor"),
            P("tensor", None),
            P(),
        ),
        check_vma=False,
    )
```

time: 3350 us -> 928 us (0.28)
  waiting for transfers between devices: 2700 us -> 267 us
  matrix products: 371 us -> 202 us
  Pallas kernels: 0 us -> 148 us
  starting transfers between devices: 0.59 us -> 138 us
  blocking collectives: 81.7 us -> 0 us
  other arithmetic: 117 us -> 46.3 us
  local copies, waits for them, and re-layouts: 52.7 us -> 101 us
    reduce_scatter x4 -> x3, waiting for transfers between devices: 1710 us -> 36.3 us  [reduce_weight(): lax.psum_scatter(grad, ('tensor', 'dp'), scatter_dimension=0, tiled=True)]
    all_gather x4 -> x3, waiting for transfers between devices: 762 us -> 39.3 us  [gather_weight(): return lax.all_gather(mine, ('tensor', 'dp'), axis=0, tiled=True)]
    ppermute x0 -> x52, waiting for transfers between devices: none -> 191 us  [the longest x24 98.2 us: partner(): lax.ppermute(values, axis, [(i, i ^ bit) for i in range(lax.axis_size(axi...]
    dot_general x29 -> x16, matrix products: 371 us -> 202 us  [dot(): return lax.dot_general(left, right, dims, preferred_element_type=FULL)]
    psum x1 -> x0, waiting for transfers between devices: 159 us -> none  [on_device(): lax.psum((ada_weight_grad, ada_bias_grad, qkv_weight_grad, qkv_bias_grad,...]
    pallas_call x0 -> x4, Pallas kernels: none -> 148 us  [the longest x2 89.2 us: attend_back(): pl.pallas_call(functools.partial(attend_back_kernel, heads, chunk * colum...]
    ppermute x0 -> x52, starting transfers between devices: none -> 137 us  [the longest x14 66.9 us: to_slots(): piece = lax.ppermute(piece, 'tensor', pairs)]
    unnamed x11 -> x6, waiting for transfers between devices: 69.6 us -> 0.1 us
  transfers between devices with their start and end apart: 10 -> 58, of which waited for: 10 -> 24; matrix products, arithmetic and copies ran while one was open for 3% -> 36% of each run, Pallas kernels for 0% -> 16%
where the time goes in v1:
time: 928 us; the launch traced here: 918 us
  waiting for transfers between devices  267 us (29%)
  matrix products  202 us (22%)
  Pallas kernels  148 us (16%)
  starting transfers between devices  138 us (15%)
  local copies, waits for them, and re-layouts  101 us (11%)
  other arithmetic  46.3 us (5%)
  between operations  16.5 us (2%)
    dot_general x16, matrix products, dot(): return lax.dot_general(left, right, dims, preferred_element_type=FULL)  202 us
    ppermute x24, waiting for transfers between devices, partner(): lax.ppermute(values, axis, [(i, i ^ bit) for i in range(lax.axis_size(axi...  98.2 us
    pallas_call x2, Pallas kernels, attend_back(): pl.pallas_call(functools.partial(attend_back_kernel, heads, chunk * colum...  89.2 us
    ppermute x14, waiting for transfers between devices, from_slots(): piece = lax.ppermute(piece, 'tensor', pairs)  73 us
    ppermute x14, starting transfers between devices, to_slots(): piece = lax.ppermute(piece, 'tensor', pairs)  66.9 us
    pallas_call x2, Pallas kernels, attend(): pl.pallas_call(functools.partial(attend_kernel, heads, chunk * column(hea...  58.7 us
    ppermute x24, starting transfers between devices, partner(): lax.ppermute(values, axis, [(i, i ^ bit) for i in range(lax.axis_size(axi...  53.6 us
    unnamed x182, local copies, waits for them, and re-layouts  53.3 us
  transfers between devices with their start and end apart: 58, of which 24 were waited for; matrix products, arithmetic and copies ran while one was open for 36% of the time, Pallas kernels for 16%

profile of v1, /device:TPU:0, one launch (start us, length us, event | category | flops | bytes accessed | tf_op | source)
XLA Modules:
  0.0 918.4 jit_solution(12281389279749760228)
XLA Ops:
  12.8 3.0 collective-permute-start.7
  21.0 4.0 collective-permute-start.1
  25.0 5.4 collective-permute-start.2
  36.5 14.3 %collective-permute-done.8 = f32[2,6192]{1,0:T(2,128)S(1)} collective-permute-done((f32[2,6192]{1,0:T(2,128)S(1)}, f32[2,6192]{1,0:T(2,128)S(1)}, u32[]{:S(2)}, u32[]{:S(2)}) %collective-permute-start.8) | collective-permute-done | bytes 49568 | tf_op jit(solution)/shard_map/ppermute | solution.py:163
  54.6 4.1 collective-permute-done.9
  59.3 10.2 %collective-permute-start.4 = (bf16[128,1152]{1,0:T(8,128)(2,1)S(1)}, bf16[128,1152]{1,0:T(8,128)(2,1)}, u32[]{:S(2)}, u32[]{:S(2)}) collective-permute-start(bf16[128,1152]{1,0:T(8,128)(2,1)S(1)} %get-tuple-element.83), channel_id=1, source_target_pairs={{0,5},{1,6},{4,1},{5,2},{6,3},{7,4},{8,13},{9,14},{12,9},{13,10},{... | collective-permute-start | bytes 884744 | tf_op jit(solution)/shard_map/ppermute | solution.py:222
  74.2 24.7 %collective-permute-start.5 = (bf16[128,1152]{1,0:T(8,128)(2,1)S(1)}, bf16[128,1152]{1,0:T(8,128)(2,1)S(1)}, u32[]{:S(2)}, u32[]{:S(2)}) collective-permute-start(bf16[128,1152]{1,0:T(8,128)(2,1)S(1)} %get-tuple-element.88), channel_id=1, source_target_pairs={{0,6},{3,1},{4,2},{5,3},{6,4},{7,5},{8,14},{11,9},{12,10},{13,11},... | collective-permute-start | bytes 884744 | tf_op jit(solution)/shard_map/ppermute | solution.py:222
  115.4 19.5 %all-gather.4.cloned.1.call-done = bf16[4608,1152]{1,0:T(8,128)(2,1)} async-done(((bf16[144,1152]{1,0:T(8,128)(2,1)}), bf16[4608,1152]{1,0:T(8,128)(2,1)}) %all-gather.4.cloned.1.call-update) | async-done | bytes 10616848 | tf_op jit(solution)/shard_map/all_gather | solution.py:199
  134.9 9.4 %copy.47 = bf16[8,2,288,1152]{3,2,0,1:T(8,128)(2,1)} copy(bf16[8,2,288,1152]{3,2,1,0:T(8,128)(2,1)} %bitcast.178) | data formatting | bytes 21233664 | tf_op jit(solution)/shard_map/reshape | solution.py:274
  144.4 7.1 slice.164
  154.0 16.0 %add_convert_fusion.projected = bf16[1024,3456]{1,0:T(8,128)(2,1)} fusion(bf16[3456,1152]{1,0:T(8,128)(2,1)} %bitcast.179, f32[3456]{0:T(1024)S(1)} %add.252, bf16[1024,1152]{1,0:T(8,128)(2,1)S(1)} %copy-done.10, f32[1152]{0:T(1024)S(1)} %get-tuple-element.40, f32[1152]{0:T(1024)S(1)} %get-tuple-element.41, f32[1024]{0:T(1024)S(1)} %add_rsqrt_fusion.1, ...), kind=kOutput, calls=%fused_computation.13 | convolution fusion | flops 8167882752 | bytes 17431040 | tf_op jit(solution)/shard_map/dot_general | solution.py:20
  176.0 29.2 %shard_map.237 = bf16[1024,576]{1,0:T(8,128)(2,1)S(1)} custom-call(bf16[1024,3456]{1,0:T(8,128)(2,1)} %add_convert_fusion.projected), custom_call_target="tpu_custom_call" | custom-call | flops 17179869184 | bytes 4718592 | tf_op jit(solution)/shard_map/pallas_call | solution.py:75
  205.2 29.5 %shard_map.238 = bf16[1024,576]{1,0:T(8,128)(2,1)S(1)} custom-call(bf16[1024,3456]{1,0:T(8,128)(2,1)} %add_convert_fusion.projected), custom_call_target="tpu_custom_call" | custom-call | flops 17179869184 | bytes 4718592 | tf_op jit(solution)/shard_map/pallas_call | solution.py:75
  234.8 5.5 fusion.57
  243.0 20.9 %fusion.53 = f32[1024,4608]{1,0:T(8,128)} fusion(bf16[4608,1152]{1,0:T(8,128)(2,1)} %all-gather.6.cloned.1.call-done, f32[1024,1152]{1,0:T(8,128)} %copy-done.15, f32[1152]{0:T(1024)S(1)} %copy-done.53, f32[1152]{0:T(1024)S(1)} %copy-done.50, f32[1024]{0:T(1024)S(1)} %add_rsqrt_fusion, f32[1024]{0:T(1024)S(1)} %broadcast_multiply_fusion.4), kind=kOutput, calls=%fused_computation.240 | convolution fusion | flops 10877534208 | bytes 34227200 | tf_op jit(solution)/shard_map/dot_general | solution.py:20
  268.2 5.5 collective-permute-start.21
  279.9 6.3 collective-permute-done.20
  286.2 6.3 collective-permute-done.21
  292.5 5.6 collective-permute-done.22
  302.4 23.2 %convolution_convert_fusion.1 = bf16[4608,1152]{1,0:T(8,128)(2,1)} fusion(bf16[1024,1152]{1,0:T(8,128)(2,1)S(1)} %get-tuple-element.22, f32[1024,4608]{1,0:T(8,128)} %fusion.53, f32[4608]{0:T(1024)S(1)} %copy-done.44), kind=kOutput, calls=%fused_computation.3 | convolution fusion | flops 10924130304 | bytes 31868928 | tf_op jit(solution)/shard_map/dot_general | solution.py:20
  325.6 19.7 %all-gather.8.cloned.1.call-done = bf16[4608,1152]{1,0:T(8,128)(2,1)} async-done(((bf16[144,1152]{1,0:T(8,128)(2,1)}), bf16[4608,1152]{1,0:T(8,128)(2,1)}) %all-gather.8.cloned.1.call-update) | async-done | bytes 10616848 | tf_op jit(solution)/shard_map/all_gather | solution.py:199
  345.4 27.5 %fusion.6 = bf16[1024,4608]{1,0:T(8,128)(2,1)S(1)} fusion(f32[1024,4608]{1,0:T(8,128)} %fusion.53, f32[4608]{0:T(1024)S(1)} %copy-done.44, bf16[1024,1152]{1,0:T(8,128)(2,1)} %copy-done.22, bf16[4608,1152]{1,0:T(8,128)(2,1)} %all-gather.8.cloned.1.call-done), kind=kOutput, calls=%fused_computation.10 | convolution fusion | flops 10970726400 | bytes 41306112 | tf_op jit(solution)/shard_map/dot_general | solution.py:20
  372.9 3.7 copy-done.13
  376.6 18.3 %convolution_convert_fusion = bf16[4608,1152]{1,0:T(8,128)(2,1)} fusion(bf16[1024,4608]{1,0:T(8,128)(2,1)S(1)} %fusion.6, f32[1024,1152]{1,0:T(8,128)} %copy-done.15, f32[1152]{0:T(1024)S(1)} %copy-done.53, f32[1152]{0:T(1024)S(1)} %copy-done.50, f32[1024]{0:T(1024)S(1)} %add_rsqrt_fusion, f32[1024]{0:T(1024)S(1)} %broadcast_multiply_fusion.4), kind=kOutput, calls=%fused_computation.2 | convolution fusion | flops 10882842624 | bytes 24790016 | tf_op jit(solution)/shard_map/dot_general | solution.py:20
  394.9 22.5 %multiply_reduce_fusion.1 = (bf16[1152]{0:T(1024)(128)(2,1)}, f32[1024]{0:T(1024)S(1)}, f32[1024]{0:T(1024)S(1)}, bf16[1152]{0:T(1024)(128)(2,1)}, f32[1024,1152]{1,0:T(8,128)}) fusion(f32[1024,1152]{1,0:T(8,128)} %copy-done.15, f32[1024]{0:T(1024)S(1)} %add_rsqrt_fusion, f32[1024]{0:T(1024)S(1)} %broadcast_multiply_fusion.4, f32[1152]{0:T(1024)S(1)} %copy-done.50, ...), kind=kOutput, calls=%fused_computation.47 | convolution fusion | flops 10882248704 | bytes 29516800 | tf_op jit(solution)/shard_map/dot_general | solution.py:20
  417.4 25.1 %multiply_reduce_fusion = (bf16[1152]{0:T(1024)(128)(2,1)S(1)}, bf16[1024,1152]{1,0:T(8,128)(2,1)}, f32[1152]{0:T(1024)S(1)}, bf16[1024,1152]{1,0:T(8,128)(2,1)}, f32[1024,1152]{1,0:T(8,128)}) fusion(bf16[1024,1152]{1,0:T(8,128)(2,1)S(1)} %copy-done.19, f32[]{:T(128)S(6)} %convert_element_type.126, f32[1024,1152]{1,0:T(8,128)S(1)} %bitcast.185, ...), kind=kOutput, calls=%fused_computation.46 | convolution fusion | flops 10943592448 | bytes 50785028 | tf_op jit(solution)/shard_map/dot_general | solution.py:20
  442.5 6.2 convolution_convert_fusion.5.attended_grad
  448.7 45.0 %shard_map.239 = bf16[1024,1728]{1,0:T(8,128)(2,1)S(1)} custom-call(bf16[1024,3456]{1,0:T(8,128)(2,1)} %add_convert_fusion.projected, bf16[1024,1152]{1,0:T(8,128)(2,1)S(1)} %convolution_convert_fusion.5.attended_grad), custom_call_target="tpu_custom_call" | custom-call | flops 34359738368 | bytes 8257536 | tf_op jit(solution)/shard_map/pallas_call | solution.py:136
  493.8 3.5 convolution_convert_fusion.4
  499.6 7.0 convolution_convert_fusion.3
  508.3 44.2 %shard_map.240 = bf16[1024,1728]{1,0:T(8,128)(2,1)S(1)} custom-call(bf16[1024,3456]{1,0:T(8,128)(2,1)} %add_convert_fusion.projected, bf16[1024,1152]{1,0:T(8,128)(2,1)S(1)} %copy-done.5), custom_call_target="tpu_custom_call" | custom-call | flops 34359738368 | bytes 8257536 | tf_op jit(solution)/shard_map/pallas_call | solution.py:136
  552.5 5.9 convolution_convert_fusion.2
  558.4 5.2 pad_maximum_fusion
  567.8 5.1 convert_reduce_fusion
  573.0 16.5 %fusion.24 = (bf16[1152]{0:T(1024)(128)(2,1)S(1)}, f32[1024]{0:T(1024)S(1)}, f32[1024]{0:T(1024)S(1)}, bf16[1152]{0:T(1024)(128)(2,1)S(1)}, f32[1024,1152]{1,0:T(8,128)}) fusion(bf16[1024,1152]{1,0:T(8,128)(2,1)} %constant_dynamic-update-slice_fusion, f32[1024]{0:T(1024)S(1)} %copy-done.46, f32[1024]{0:T(1024)S(1)} %copy-done.38, f32[1152]{0:T(1024)S(1)} %copy-done.40, ...), kind=kOutput, calls=%fused_computation.42 | convolution fusion | flops 8179675136 | bytes 22144000 | tf_op jit(solution)/shard_map/dot_general | solution.py:20
  590.1 8.6 multiply_reduce_fusion.2
  604.6 20.3 %collective-permute-start.36 = (bf16[2,8,864]{2,1,0:T(8,128)(2,1)S(1)}, bf16[2,8,864]{2,1,0:T(8,128)(2,1)S(1)}, u32[]{:S(2)}, u32[]{:S(2)}) collective-permute-start(bf16[2,8,864]{2,1,0:T(8,128)(2,1)S(1)} %pad_maximum_fusion.16), channel_id=1, source_target_pairs={{0,2},{1,3},{2,0},{3,1},{4,6},{5,7},{6,4},{7,5},{8,10},{9,11},{10,... | collective-permute-start | bytes 82952 | tf_op jit(solution)/shard_map/ppermute | solution.py:163
  630.7 4.1 collective-permute-done.37
  640.9 6.3 collective-permute-start.49
  649.3 11.7 %collective-permute-done.39 = f32[6,1152]{1,0:T(8,128)S(1)} collective-permute-done((f32[6,1152]{1,0:T(8,128)S(1)}, f32[6,1152]{1,0:T(8,128)S(1)}, u32[]{:S(2)}, u32[]{:S(2)}) %collective-permute-start.39) | collective-permute-done | bytes 27680 | tf_op jit(solution)/shard_map/ppermute | solution.py:163
  660.9 8.4 collective-permute-start.40
  669.4 20.5 %collective-permute-done.49 = f32[10368]{0:T(1024)S(1)} collective-permute-done((f32[10368]{0:T(1024)S(1)}, f32[10368]{0:T(1024)S(1)}, u32[]{:S(2)}, u32[]{:S(2)}) %collective-permute-start.49) | collective-permute-done | bytes 41504 | tf_op jit(solution)/shard_map/ppermute | solution.py:163
  732.1 6.3 collective-permute-done.11
  742.5 61.3 %collective-permute-done.13 = bf16[128,1152]{1,0:T(8,128)(2,1)S(1)} collective-permute-done((bf16[128,1152]{1,0:T(8,128)(2,1)S(1)}, bf16[128,1152]{1,0:T(8,128)(2,1)S(1)}, u32[]{:S(2)}, u32[]{:S(2)}) %collective-permute-start.13) | collective-permute-done | bytes 294944 | tf_op jit(solution)/shard_map/ppermute | solution.py:237
  818.8 3.6 convert_bitcast_fusion
  825.7 36.3 %reduce-scatter.8.cloned.1.call-done = bf16[144,1152]{1,0:T(8,128)(2,1)} async-done(((bf16[4608,1152]{1,0:T(8,128)(2,1)}), bf16[144,1152]{1,0:T(8,128)(2,1)}) %reduce-scatter.8.cloned.1.call-update) | async-done | bytes 331792 | tf_op jit(solution)/shard_map/reduce_scatter | solution.py:203
  867.3 26.9 %collective-permute-done.46 = bf16[2,144,1152]{2,1,0:T(8,128)(2,1)S(1)} collective-permute-done((bf16[2,144,1152]{2,1,0:T(8,128)(2,1)S(1)}, bf16[2,144,1152]{2,1,0:T(8,128)(2,1)S(1)}, u32[]{:S(2)}, u32[]{:S(2)}) %collective-permute-start.46) | collective-permute-done | bytes 663584 | tf_op jit(solution)/shard_map/ppermute | solution.py:163
  897.3 10.6 %collective-permute-done.27 = bf16[2,144,1152]{2,1,0:T(8,128)(2,1)S(1)} collective-permute-done((bf16[2,144,1152]{2,1,0:T(8,128)(2,1)S(1)}, bf16[2,144,1152]{2,1,0:T(8,128)(2,1)S(1)}, u32[]{:S(2)}, u32[]{:S(2)}) %collective-permute-start.27) | collective-permute-done | bytes 663584 | tf_op jit(solution)/shard_map/ppermute | solution.py:163
  (394 shorter events, 172.1 us)
Async XLA Ops:
  7.2 127.7 %all-gather.4.cloned.1.call-start = ((), (), s32[]{:S(2)}) async-start(), calls=%async_computation.3 | async-start | bytes 10948608 | tf_op jit(solution)/shard_map/all_gather | solution.py:199
  9.8 233.2 %all-gather.6.cloned.1.call-start = ((), (), s32[]{:S(2)}) async-start(), calls=%async_computation.4 | async-start | bytes 10948608 | tf_op jit(solution)/shard_map/all_gather | solution.py:199
  11.6 333.8 %all-gather.8.cloned.1.call-start = ((), (), s32[]{:S(2)}) async-start(), calls=%async_computation.5 | async-start | bytes 10948608 | tf_op jit(solution)/shard_map/all_gather | solution.py:199
  12.8 19.6 %collective-permute-start.7 = (f32[1,6192]{1,0:T(1,128)S(1)}, f32[1,6192]{1,0:T(1,128)S(1)}, u32[]{:S(2)}, u32[]{:S(2)}) collective-permute-start(f32[1,6192]{1,0:T(1,128)S(1)} %broadcast_in_dim.12), channel_id=1, source_target_pairs={{0,1},{1,0},{2,3},{3,2},{4,5},{5,4},{6,7},{7,6},{8,9},{9,8},{10,11... | collective-permute-start | bytes 74312 | tf_op jit(solution)/shard_map/ppermute | solution.py:163
  18.3 55.9 %collective-permute-start = (bf16[128,1152]{1,0:T(8,128)(2,1)}, bf16[128,1152]{1,0:T(8,128)(2,1)}, u32[]{:S(2)}, u32[]{:S(2)}) collective-permute-start(bf16[128,1152]{1,0:T(8,128)(2,1)} %get-tuple-element.87), channel_id=1, source_target_pairs={{0,1},{1,2},{2,3},{3,4},{4,5},{5,6},{8,9},{9,10},{10,11},{11,12},{... | collective-permute-start | bytes 884744 | tf_op jit(solution)/shard_map/ppermute | solution.py:222
  21.0 79.6 %collective-permute-start.1 = (bf16[128,1152]{1,0:T(8,128)(2,1)}, bf16[128,1152]{1,0:T(8,128)(2,1)}, u32[]{:S(2)}, u32[]{:S(2)}) collective-permute-start(bf16[128,1152]{1,0:T(8,128)(2,1)} %get-tuple-element.86), channel_id=1, source_target_pairs={{0,2},{1,3},{2,4},{3,5},{4,6},{7,1},{8,10},{9,11},{10,12},{11,13},... | collective-permute-start | bytes 884744 | tf_op jit(solution)/shard_map/ppermute | solution.py:222
  25.0 78.0 %collective-permute-start.2 = (bf16[128,1152]{1,0:T(8,128)(2,1)}, bf16[128,1152]{1,0:T(8,128)(2,1)}, u32[]{:S(2)}, u32[]{:S(2)}) collective-permute-start(bf16[128,1152]{1,0:T(8,128)(2,1)} %get-tuple-element.85), channel_id=1, source_target_pairs={{0,3},{1,4},{2,5},{3,6},{6,1},{7,2},{8,11},{9,12},{10,13},{11,14},... | collective-permute-start | bytes 884744 | tf_op jit(solution)/shard_map/ppermute | solution.py:222
  30.4 74.3 %collective-permute-start.3 = (bf16[128,1152]{1,0:T(8,128)(2,1)S(1)}, bf16[128,1152]{1,0:T(8,128)(2,1)}, u32[]{:S(2)}, u32[]{:S(2)}) collective-permute-start(bf16[128,1152]{1,0:T(8,128)(2,1)S(1)} %get-tuple-element.84), channel_id=1, source_target_pairs={{0,4},{1,5},{2,6},{5,1},{6,2},{7,3},{8,12},{9,13},{10,14},{13,9},{... | collective-permute-start | bytes 884744 | tf_op jit(solution)/shard_map/ppermute | solution.py:222
  32.5 18.3 %collective-permute-start.8 = (f32[2,6192]{1,0:T(2,128)S(1)}, f32[2,6192]{1,0:T(2,128)S(1)}, u32[]{:S(2)}, u32[]{:S(2)}) collective-permute-start(f32[2,6192]{1,0:T(2,128)S(1)} %pad_maximum_fusion.13), channel_id=1, source_target_pairs={{0,2},{1,3},{2,0},{3,1},{4,6},{5,7},{6,4},{7,5},{8,10},{9,11},{10,... | collective-permute-start | bytes 148616 | tf_op jit(solution)/shard_map/ppermute | solution.py:163
  36.4 782.4 %reduce-scatter.4.cloned.1.call-start = ((), (), s32[]{:S(2)}) async-start(), calls=%async_computation.6 | async-start | bytes 10948608 | tf_op jit(solution)/shard_map/reduce_scatter | solution.py:203
  59.3 47.1 %collective-permute-start.4 = (bf16[128,1152]{1,0:T(8,128)(2,1)S(1)}, bf16[128,1152]{1,0:T(8,128)(2,1)}, u32[]{:S(2)}, u32[]{:S(2)}) collective-permute-start(bf16[128,1152]{1,0:T(8,128)(2,1)S(1)} %get-tuple-element.83), channel_id=1, source_target_pairs={{0,5},{1,6},{4,1},{5,2},{6,3},{7,4},{8,13},{9,14},{12,9},{13,10},{... | collective-permute-start | bytes 884744 | tf_op jit(solution)/shard_map/ppermute | solution.py:222
  74.2 35.2 %collective-permute-start.5 = (bf16[128,1152]{1,0:T(8,128)(2,1)S(1)}, bf16[128,1152]{1,0:T(8,128)(2,1)S(1)}, u32[]{:S(2)}, u32[]{:S(2)}) collective-permute-start(bf16[128,1152]{1,0:T(8,128)(2,1)S(1)} %get-tuple-element.88), channel_id=1, source_target_pairs={{0,6},{3,1},{4,2},{5,3},{6,4},{7,5},{8,14},{11,9},{12,10},{13,11},... | collective-permute-start | bytes 884744 | tf_op jit(solution)/shard_map/ppermute | solution.py:222
  100.6 9.5 %collective-permute-start.6 = (bf16[128,1152]{1,0:T(8,128)(2,1)S(1)}, bf16[128,1152]{1,0:T(8,128)(2,1)S(1)}, u32[]{:S(2)}, u32[]{:S(2)}) collective-permute-start(bf16[128,1152]{1,0:T(8,128)(2,1)S(1)} %get-tuple-element.82), channel_id=1, source_target_pairs={{2,1},{3,2},{4,3},{5,4},{6,5},{7,6},{10,9},{11,10},{12,11},{13,12}... | collective-permute-start | bytes 884744 | tf_op jit(solution)/shard_map/ppermute | solution.py:222
  171.0 102.7 %collective-permute-start.17 = (bf16[128,1152]{1,0:T(8,128)(2,1)}, bf16[128,1152]{1,0:T(8,128)(2,1)}, u32[]{:S(2)}, u32[]{:S(2)}) collective-permute-start(bf16[128,1152]{1,0:T(8,128)(2,1)} %get-tuple-element.81), channel_id=1, source_target_pairs={{0,1},{1,2},{2,3},{3,4},{4,5},{5,6},{8,9},{9,10},{10,11},{11,12},{... | collective-permute-start | bytes 884744 | tf_op jit(solution)/shard_map/ppermute | solution.py:222
  174.0 103.5 %collective-permute-start.18 = (bf16[128,1152]{1,0:T(8,128)(2,1)}, bf16[128,1152]{1,0:T(8,128)(2,1)}, u32[]{:S(2)}, u32[]{:S(2)}) collective-permute-start(bf16[128,1152]{1,0:T(8,128)(2,1)} %get-tuple-element.80), channel_id=1, source_target_pairs={{0,2},{1,3},{2,4},{3,5},{4,6},{7,1},{8,10},{9,11},{10,12},{11,13},... | collective-permute-start | bytes 884744 | tf_op jit(solution)/shard_map/ppermute | solution.py:222
  264.9 14.9 %collective-permute-start.19 = (bf16[128,1152]{1,0:T(8,128)(2,1)S(1)}, bf16[128,1152]{1,0:T(8,128)(2,1)S(1)}, u32[]{:S(2)}, u32[]{:S(2)}) collective-permute-start(bf16[128,1152]{1,0:T(8,128)(2,1)S(1)} %get-tuple-element.79), channel_id=1, source_target_pairs={{0,3},{1,4},{2,5},{3,6},{6,1},{7,2},{8,11},{9,12},{10,13},{11,14},... | collective-permute-start | bytes 884744 | tf_op jit(solution)/shard_map/ppermute | solution.py:222
  266.9 19.3 %collective-permute-start.20 = (bf16[128,1152]{1,0:T(8,128)(2,1)S(1)}, bf16[128,1152]{1,0:T(8,128)(2,1)S(1)}, u32[]{:S(2)}, u32[]{:S(2)}) collective-permute-start(bf16[128,1152]{1,0:T(8,128)(2,1)S(1)} %get-tuple-element.78), channel_id=1, source_target_pairs={{0,4},{1,5},{2,6},{5,1},{6,2},{7,3},{8,12},{9,13},{10,14},{13,9},{... | collective-permute-start | bytes 884744 | tf_op jit(solution)/shard_map/ppermute | solution.py:222
  268.2 24.3 %collective-permute-start.21 = (bf16[128,1152]{1,0:T(8,128)(2,1)S(1)}, bf16[128,1152]{1,0:T(8,128)(2,1)S(1)}, u32[]{:S(2)}, u32[]{:S(2)}) collective-permute-start(bf16[128,1152]{1,0:T(8,128)(2,1)S(1)} %get-tuple-element.77), channel_id=1, source_target_pairs={{0,5},{1,6},{4,1},{5,2},{6,3},{7,4},{8,13},{9,14},{12,9},{13,10},{... | collective-permute-start | bytes 884744 | tf_op jit(solution)/shard_map/ppermute | solution.py:222
  273.7 24.4 %collective-permute-start.22 = (bf16[128,1152]{1,0:T(8,128)(2,1)S(1)}, bf16[128,1152]{1,0:T(8,128)(2,1)S(1)}, u32[]{:S(2)}, u32[]{:S(2)}) collective-permute-start(bf16[128,1152]{1,0:T(8,128)(2,1)S(1)} %get-tuple-element.76), channel_id=1, source_target_pairs={{0,6},{3,1},{4,2},{5,3},{6,4},{7,5},{8,14},{11,9},{12,10},{13,11},... | collective-permute-start | bytes 884744 | tf_op jit(solution)/shard_map/ppermute | solution.py:222
  277.5 20.6 %collective-permute-start.23 = (bf16[128,1152]{1,0:T(8,128)(2,1)S(1)}, bf16[128,1152]{1,0:T(8,128)(2,1)S(1)}, u32[]{:S(2)}, u32[]{:S(2)}) collective-permute-start(bf16[128,1152]{1,0:T(8,128)(2,1)S(1)} %get-tuple-element.75), channel_id=1, source_target_pairs={{2,1},{3,2},{4,3},{5,4},{6,5},{7,6},{10,9},{11,10},{12,11},{13,12}... | collective-permute-start | bytes 884744 | tf_op jit(solution)/shard_map/ppermute | solution.py:222
  325.6 499.6 %reduce-scatter.6.cloned.1.call-start = ((), (), s32[]{:S(2)}) async-start(), calls=%async_computation.7 | async-start | bytes 10948608 | tf_op jit(solution)/shard_map/reduce_scatter | solution.py:203
  506.6 355.4 %reduce-scatter.8.cloned.1.call-start = ((), (), s32[]{:S(2)}) async-start(), calls=%async_computation.8 | async-start | bytes 10948608 | tf_op jit(solution)/shard_map/reduce_scatter | solution.py:203
  573.0 56.4 %collective-permute-start.47 = (f32[10368]{0:T(1024)S(1)}, f32[10368]{0:T(1024)S(1)}, u32[]{:S(2)}, u32[]{:S(2)}) collective-permute-start(f32[10368]{0:T(1024)S(1)} %concatenate.100), channel_id=1, source_target_pairs={{0,1},{1,0},{2,3},{3,2},{4,5},{5,4},{6,7},{7,6},{8,9},{9,8},{10,11... | collective-permute-start | bytes 124424 | tf_op jit(solution)/shard_map/ppermute | solution.py:163
  604.6 22.1 %collective-permute-start.36 = (bf16[2,8,864]{2,1,0:T(8,128)(2,1)S(1)}, bf16[2,8,864]{2,1,0:T(8,128)(2,1)S(1)}, u32[]{:S(2)}, u32[]{:S(2)}) collective-permute-start(bf16[2,8,864]{2,1,0:T(8,128)(2,1)S(1)} %pad_maximum_fusion.16), channel_id=1, source_target_pairs={{0,2},{1,3},{2,0},{3,1},{4,6},{5,7},{6,4},{7,5},{8,10},{9,11},{10,... | collective-permute-start | bytes 82952 | tf_op jit(solution)/shard_map/ppermute | solution.py:163
  629.4 10.1 %collective-permute-start.48 = (f32[10368]{0:T(1024)S(1)}, f32[10368]{0:T(1024)S(1)}, u32[]{:S(2)}, u32[]{:S(2)}) collective-permute-start(f32[10368]{0:T(1024)S(1)} %add.279), channel_id=1, source_target_pairs={{0,2},{1,3},{2,0},{3,1},{4,6},{5,7},{6,4},{7,5},{8,10},{9,11},{10,... | collective-permute-start | bytes 124424 | tf_op jit(solution)/shard_map/ppermute | solution.py:163
  634.9 12.3 %collective-permute-start.43 = (bf16[1,8,864]{2,1,0:T(8,128)(2,1)S(1)}, bf16[1,8,864]{2,1,0:T(8,128)(2,1)S(1)}, u32[]{:S(2)}, u32[]{:S(2)}) collective-permute-start(bf16[1,8,864]{2,1,0:T(8,128)(2,1)S(1)} %bitcast.200), channel_id=1, source_target_pairs={{0,8},{8,0},{16,24},{24,16},{1,9},{9,1},{17,25},{25,17},{2,10},{10... | collective-permute-start | bytes 41480 | tf_op jit(solution)/shard_map/ppermute | solution.py:163
  636.9 74.3 %collective-permute-start.28 = (bf16[128,1152]{1,0:T(8,128)(2,1)}, bf16[128,1152]{1,0:T(8,128)(2,1)S(1)}, u32[]{:S(2)}, u32[]{:S(2)}) collective-permute-start(bf16[128,1152]{1,0:T(8,128)(2,1)} %get-tuple-element.67), channel_id=1, source_target_pairs={{1,0},{2,1},{3,2},{4,3},{5,4},{6,5},{9,8},{10,9},{11,10},{12,11},{... | collective-permute-start | bytes 884744 | tf_op jit(solution)/shard_map/ppermute | solution.py:237
  638.2 75.1 %collective-permute-start.29 = (bf16[128,1152]{1,0:T(8,128)(2,1)}, bf16[128,1152]{1,0:T(8,128)(2,1)S(1)}, u32[]{:S(2)}, u32[]{:S(2)}) collective-permute-start(bf16[128,1152]{1,0:T(8,128)(2,1)} %get-tuple-element.66), channel_id=1, source_target_pairs={{2,0},{3,1},{4,2},{5,3},{6,4},{1,7},{10,8},{11,9},{12,10},{13,11},... | collective-permute-start | bytes 884744 | tf_op jit(solution)/shard_map/ppermute | solution.py:237
  639.5 75.2 %collective-permute-start.30 = (bf16[128,1152]{1,0:T(8,128)(2,1)}, bf16[128,1152]{1,0:T(8,128)(2,1)S(1)}, u32[]{:S(2)}, u32[]{:S(2)}) collective-permute-start(bf16[128,1152]{1,0:T(8,128)(2,1)} %get-tuple-element.65), channel_id=1, source_target_pairs={{3,0},{4,1},{5,2},{6,3},{1,6},{2,7},{11,8},{12,9},{13,10},{14,11},... | collective-permute-start | bytes 884744 | tf_op jit(solution)/shard_map/ppermute | solution.py:237
  640.9 49.1 %collective-permute-start.49 = (f32[10368]{0:T(1024)S(1)}, f32[10368]{0:T(1024)S(1)}, u32[]{:S(2)}, u32[]{:S(2)}) collective-permute-start(f32[10368]{0:T(1024)S(1)} %add.280), channel_id=1, source_target_pairs={{0,4},{1,5},{2,6},{3,7},{4,0},{5,1},{6,2},{7,3},{8,12},{9,13},{10,... | collective-permute-start | bytes 124424 | tf_op jit(solution)/shard_map/ppermute | solution.py:163
  647.2 13.7 %collective-permute-start.39 = (f32[6,1152]{1,0:T(8,128)S(1)}, f32[6,1152]{1,0:T(8,128)S(1)}, u32[]{:S(2)}, u32[]{:S(2)}) collective-permute-start(f32[6,1152]{1,0:T(8,128)S(1)} %add.276), channel_id=1, source_target_pairs={{0,2},{1,3},{2,0},{3,1},{4,6},{5,7},{6,4},{7,5},{8,10},{9,11},{10,... | collective-permute-start | bytes 82952 | tf_op jit(solution)/shard_map/ppermute | solution.py:163
  660.9 29.6 %collective-permute-start.40 = (f32[6,1152]{1,0:T(8,128)S(1)}, f32[6,1152]{1,0:T(8,128)S(1)}, u32[]{:S(2)}, u32[]{:S(2)}) collective-permute-start(f32[6,1152]{1,0:T(8,128)S(1)} %add.277), channel_id=1, source_target_pairs={{0,4},{1,5},{2,6},{3,7},{4,0},{5,1},{6,2},{7,3},{8,12},{9,13},{10,... | collective-permute-start | bytes 82952 | tf_op jit(solution)/shard_map/ppermute | solution.py:163
  694.4 22.3 %collective-permute-start.31 = (bf16[128,1152]{1,0:T(8,128)(2,1)}, bf16[128,1152]{1,0:T(8,128)(2,1)S(1)}, u32[]{:S(2)}, u32[]{:S(2)}) collective-permute-start(bf16[128,1152]{1,0:T(8,128)(2,1)} %get-tuple-element.64), channel_id=1, source_target_pairs={{4,0},{5,1},{6,2},{1,5},{2,6},{3,7},{12,8},{13,9},{14,10},{9,13},{... | collective-permute-start | bytes 884744 | tf_op jit(solution)/shard_map/ppermute | solution.py:237
  706.5 12.3 %collective-permute-start.32 = (bf16[128,1152]{1,0:T(8,128)(2,1)}, bf16[128,1152]{1,0:T(8,128)(2,1)S(1)}, u32[]{:S(2)}, u32[]{:S(2)}) collective-permute-start(bf16[128,1152]{1,0:T(8,128)(2,1)} %get-tuple-element.63), channel_id=1, source_target_pairs={{5,0},{6,1},{1,4},{2,5},{3,6},{4,7},{13,8},{14,9},{9,12},{10,13},{... | collective-permute-start | bytes 884744 | tf_op jit(solution)/shard_map/ppermute | solution.py:237
  711.3 12.3 %collective-permute-start.33 = (bf16[128,1152]{1,0:T(8,128)(2,1)}, bf16[128,1152]{1,0:T(8,128)(2,1)S(1)}, u32[]{:S(2)}, u32[]{:S(2)}) collective-permute-start(bf16[128,1152]{1,0:T(8,128)(2,1)} %get-tuple-element.62), channel_id=1, source_target_pairs={{6,0},{1,3},{2,4},{3,5},{4,6},{5,7},{14,8},{9,11},{10,12},{11,13},... | collective-permute-start | bytes 884744 | tf_op jit(solution)/shard_map/ppermute | solution.py:237
  713.3 12.3 %collective-permute-start.34 = (bf16[128,1152]{1,0:T(8,128)(2,1)S(1)}, bf16[128,1152]{1,0:T(8,128)(2,1)S(1)}, u32[]{:S(2)}, u32[]{:S(2)}) collective-permute-start(bf16[128,1152]{1,0:T(8,128)(2,1)S(1)} %copy-done.30), channel_id=1, source_target_pairs={{1,2},{2,3},{3,4},{4,5},{5,6},{6,7},{9,10},{10,11},{11,12},{12,13}... | collective-permute-start | bytes 884744 | tf_op jit(solution)/shard_map/ppermute | solution.py:237
  714.7 15.4 %collective-permute-start.10 = (bf16[128,1152]{1,0:T(8,128)(2,1)S(1)}, bf16[128,1152]{1,0:T(8,128)(2,1)S(1)}, u32[]{:S(2)}, u32[]{:S(2)}) collective-permute-start(bf16[128,1152]{1,0:T(8,128)(2,1)S(1)} %copy-done.31), channel_id=1, source_target_pairs={{1,0},{2,1},{3,2},{4,3},{5,4},{6,5},{9,8},{10,9},{11,10},{12,11},{... | collective-permute-start | bytes 884744 | tf_op jit(solution)/shard_map/ppermute | solution.py:237
  716.7 21.7 %collective-permute-start.11 = (bf16[128,1152]{1,0:T(8,128)(2,1)S(1)}, bf16[128,1152]{1,0:T(8,128)(2,1)S(1)}, u32[]{:S(2)}, u32[]{:S(2)}) collective-permute-start(bf16[128,1152]{1,0:T(8,128)(2,1)S(1)} %copy-done.29), channel_id=1, source_target_pairs={{2,0},{3,1},{4,2},{5,3},{6,4},{1,7},{10,8},{11,9},{12,10},{13,11},... | collective-permute-start | bytes 884744 | tf_op jit(solution)/shard_map/ppermute | solution.py:237
  718.8 23.0 %collective-permute-start.12 = (bf16[128,1152]{1,0:T(8,128)(2,1)S(1)}, bf16[128,1152]{1,0:T(8,128)(2,1)S(1)}, u32[]{:S(2)}, u32[]{:S(2)}) collective-permute-start(bf16[128,1152]{1,0:T(8,128)(2,1)S(1)} %copy-done.28), channel_id=1, source_target_pairs={{3,0},{4,1},{5,2},{6,3},{1,6},{2,7},{11,8},{12,9},{13,10},{14,11},... | collective-permute-start | bytes 884744 | tf_op jit(solution)/shard_map/ppermute | solution.py:237
  723.5 80.3 %collective-permute-start.13 = (bf16[128,1152]{1,0:T(8,128)(2,1)S(1)}, bf16[128,1152]{1,0:T(8,128)(2,1)S(1)}, u32[]{:S(2)}, u32[]{:S(2)}) collective-permute-start(bf16[128,1152]{1,0:T(8,128)(2,1)S(1)} %copy-done.27), channel_id=1, source_target_pairs={{4,0},{5,1},{6,2},{1,5},{2,6},{3,7},{12,8},{13,9},{14,10},{9,13},{... | collective-permute-start | bytes 884744 | tf_op jit(solution)/shard_map/ppermute | solution.py:237
  725.6 79.0 %collective-permute-start.14 = (bf16[128,1152]{1,0:T(8,128)(2,1)S(1)}, bf16[128,1152]{1,0:T(8,128)(2,1)S(1)}, u32[]{:S(2)}, u32[]{:S(2)}) collective-permute-start(bf16[128,1152]{1,0:T(8,128)(2,1)S(1)} %copy-done.26), channel_id=1, source_target_pairs={{5,0},{6,1},{1,4},{2,5},{3,6},{4,7},{13,8},{14,9},{9,12},{10,13},{... | collective-permute-start | bytes 884744 | tf_op jit(solution)/shard_map/ppermute | solution.py:237
  730.1 75.2 %collective-permute-start.15 = (bf16[128,1152]{1,0:T(8,128)(2,1)S(1)}, bf16[128,1152]{1,0:T(8,128)(2,1)S(1)}, u32[]{:S(2)}, u32[]{:S(2)}) collective-permute-start(bf16[128,1152]{1,0:T(8,128)(2,1)S(1)} %copy-done.25), channel_id=1, source_target_pairs={{6,0},{1,3},{2,4},{3,5},{4,6},{5,7},{14,8},{9,11},{10,12},{11,13},... | collective-permute-start | bytes 884744 | tf_op jit(solution)/shard_map/ppermute | solution.py:237
  738.4 67.6 %collective-permute-start.16 = (bf16[128,1152]{1,0:T(8,128)(2,1)S(1)}, bf16[128,1152]{1,0:T(8,128)(2,1)S(1)}, u32[]{:S(2)}, u32[]{:S(2)}) collective-permute-start(bf16[128,1152]{1,0:T(8,128)(2,1)S(1)} %get-tuple-element.68), channel_id=1, source_target_pairs={{1,2},{2,3},{3,4},{4,5},{5,6},{6,7},{9,10},{10,11},{11,12},{12,13}... | collective-permute-start | bytes 884744 | tf_op jit(solution)/shard_map/ppermute | solution.py:237
  818.8 43.1 %collective-permute-start.24 = (bf16[1,144,1152]{2,1,0:T(8,128)(2,1)}, bf16[1,144,1152]{2,1,0:T(8,128)(2,1)S(1)}, u32[]{:S(2)}, u32[]{:S(2)}) collective-permute-start(bf16[1,144,1152]{2,1,0:T(8,128)(2,1)} %bitcast.194), channel_id=1, source_target_pairs={{0,8},{8,0},{16,24},{24,16},{1,9},{9,1},{17,25},{25,17},{2,10},{10... | collective-permute-start | bytes 995336 | tf_op jit(solution)/shard_map/ppermute | solution.py:163
  825.2 41.3 %collective-permute-start.26 = (bf16[1,144,1152]{2,1,0:T(8,128)(2,1)}, bf16[1,144,1152]{2,1,0:T(8,128)(2,1)S(1)}, u32[]{:S(2)}, u32[]{:S(2)}) collective-permute-start(bf16[1,144,1152]{2,1,0:T(8,128)(2,1)} %bitcast.195), channel_id=1, source_target_pairs={{0,8},{8,0},{16,24},{24,16},{1,9},{9,1},{17,25},{25,17},{2,10},{10... | collective-permute-start | bytes 995336 | tf_op jit(solution)/shard_map/ppermute | solution.py:163
  862.1 34.9 %collective-permute-start.25 = (bf16[2,144,1152]{2,1,0:T(8,128)(2,1)S(1)}, bf16[2,144,1152]{2,1,0:T(8,128)(2,1)S(1)}, u32[]{:S(2)}, u32[]{:S(2)}) collective-permute-start(bf16[2,144,1152]{2,1,0:T(8,128)(2,1)S(1)} %pad_maximum_fusion.7), channel_id=1, source_target_pairs={{0,16},{8,24},{16,0},{24,8},{1,17},{9,25},{17,1},{25,9},{2,18},{10... | collective-permute-start | bytes 1990664 | tf_op jit(solution)/shard_map/ppermute | solution.py:163
  864.9 29.2 %collective-permute-start.46 = (bf16[2,144,1152]{2,1,0:T(8,128)(2,1)S(1)}, bf16[2,144,1152]{2,1,0:T(8,128)(2,1)S(1)}, u32[]{:S(2)}, u32[]{:S(2)}) collective-permute-start(bf16[2,144,1152]{2,1,0:T(8,128)(2,1)S(1)} %pad_maximum_fusion.9), channel_id=1, source_target_pairs={{0,16},{8,24},{16,0},{24,8},{1,17},{9,25},{17,1},{25,9},{2,18},{10... | collective-permute-start | bytes 1990664 | tf_op jit(solution)/shard_map/ppermute | solution.py:163
  866.7 41.3 %collective-permute-start.27 = (bf16[2,144,1152]{2,1,0:T(8,128)(2,1)S(1)}, bf16[2,144,1152]{2,1,0:T(8,128)(2,1)S(1)}, u32[]{:S(2)}, u32[]{:S(2)}) collective-permute-start(bf16[2,144,1152]{2,1,0:T(8,128)(2,1)S(1)} %pad_maximum_fusion.8), channel_id=1, source_target_pairs={{0,16},{8,24},{16,0},{24,8},{1,17},{9,25},{17,1},{25,9},{2,18},{10... | collective-permute-start | bytes 1990664 | tf_op jit(solution)/shard_map/ppermute | solution.py:163
  (76 other events, 1603.5 us)
Sparse Core Ops, SparseCore 0:
  11.5 123.3 all-gather.3
  138.4 90.6 all-gather.5
  232.0 113.3 all-gather.7
  351.3 155.1 reduce-scatter.3
  512.4 177.1 reduce-scatter.5
  695.6 166.3 reduce-scatter.7

commit v2 on v1

--- a/solution.py
+++ b/solution.py
@@ -14,6 +14,8 @@
 FIRST = (((0,), (0,)), ((), ()))
 PLAIN = (((1,), (0,)), ((), ()))
 ROWS = 256
+CORE = 1
+SIDE = 2
 
 
 def dot(left, right, dims=PLAIN):
@@ -199,9 +201,30 @@
     return lax.all_gather(mine, ("tensor", "dp"), axis=0, tiled=True)
 
 
-def reduce_weight(grad):
-    mine = lax.psum_scatter(grad, ("tensor", "dp"), scatter_dimension=0, tiled=True)
-    return pair_gather(mine, "dp").reshape(-1, grad.shape[1])
+def halves(values, flag):
+    size = values.shape[1] // 2
+    return (
+        lax.dynamic_slice_in_dim(values, flag * size, size, 1),
+        lax.dynamic_slice_in_dim(values, (1 - flag) * size, size, 1),
+    )
+
+
+def pair_reduce(terms, bit):
+    keep, send = halves(terms, (lax.axis_index("dp") & bit) // bit)
+    return add(keep, partner(send, "dp", bit)).astype(LOW)
+
+
+def scatter(terms):
+    held = terms.reshape(-1, terms.shape[2])
+    return lax.psum_scatter(held, "tensor", scatter_dimension=0, tiled=True)
+
+
+def spread(held):
+    for bit in bits_of("dp", 4):
+        held = low(add(held, partner(held, "dp", bit)))
+    for bit in (SIDE, CORE):
+        held = order_by((lax.axis_index("dp") & bit) != 0, held, partner(held, "dp", bit), 0)
+    return held
 
 
 def slot_start(slots):
@@ -224,18 +247,24 @@
     return jnp.concatenate(parts, axis=0)
 
 
-def from_slots(values, slots):
-    groups, here = lax.axis_size("tensor"), lax.axis_index("tensor")
+def send_back(values, slots, steps):
+    groups = lax.axis_size("tensor")
     start = slot_start(slots)
     rows = values.shape[0] // groups
     parts = []
-    for step in range(groups):
+    for step in steps:
         piece = values[step * rows : (step + 1) * rows]
         if step:
             pairs = [((i + step) % groups, i) for i in range(groups)]
             pairs = [pair for pair in pairs if start <= pair[0] < start + slots]
             piece = lax.ppermute(piece, "tensor", pairs)
         parts.append(piece)
+    return parts
+
+
+def from_slots(parts, slots):
+    groups, here = lax.axis_size("tensor"), lax.axis_index("tensor")
+    start = slot_start(slots)
     twice = jnp.stack(parts + parts, axis=0)
     return lax.dynamic_slice_in_dim(twice, lax.rem(groups + start - here, groups), slots, 0)
 
@@ -309,21 +338,22 @@
     activ = activ_value.astype(LOW)
     mlp_branch = dot(activ, fc2_full) + fc2_bias.astype(FULL)
     output = (live * (mixed + gate_mlp * mlp_branch)).astype(LOW)
-    output = jnp.transpose(from_slots(output, slots), (1, 0, 2))
 
     out_grad, _ = lax.optimization_barrier((out_grad, projected))
     upstream = live * to_slots(jnp.transpose(out_grad, (1, 0, 2))).astype(FULL)
     branch_grad = (gate_mlp * upstream).astype(LOW)
     gate_mlp_grad = jnp.sum(upstream * mlp_branch, axis=0)
     fc2_bias_part = jnp.sum(branch_grad, axis=0, dtype=FULL)
-    fc2_weight_part = dot(activ, branch_grad, FIRST).astype(LOW)
-    fc2_weight_part, branch_grad = lax.optimization_barrier((fc2_weight_part, branch_grad))
-    fc2_weight_grad = reduce_weight(fc2_weight_part)
+    fc2_part = dot(activ, branch_grad, FIRST).astype(LOW)
+    fc2_part = pair_reduce(fc2_part.reshape(groups, hidden_local, width), CORE)
+    branch_grad = after(branch_grad, fc2_part)
+    fc2_part = pair_reduce(fc2_part, SIDE)
     activ_grad = dot(branch_grad, fc2_full, LAST)
     pre_grad = gelu_back(activ_grad)[0].astype(LOW)
-    fc1_weight_part = dot(pre_grad, hidden_mlp, FIRST).astype(LOW)
-    fc1_weight_part, pre_grad = lax.optimization_barrier((fc1_weight_part, pre_grad))
-    fc1_weight_grad = reduce_weight(fc1_weight_part)
+    fc1_part = dot(pre_grad, hidden_mlp, FIRST).astype(LOW)
+    pre_grad = after(pre_grad, fc1_part, fc2_part)
+    fc2_part = scatter(fc2_part)
+    fc1_part = pair_reduce(fc1_part.reshape(groups, hidden_local, width), CORE)
     fc1_bias_part = jnp.sum(pre_grad, axis=0, dtype=FULL)
     hidden_mlp_grad = dot(pre_grad, fc1_full)
     shift_mlp_grad = jnp.sum(hidden_mlp_grad, axis=0)
@@ -335,24 +365,35 @@
     out_weight_part = dot(attended, attn_grad, FIRST).astype(LOW)
     attended_grad = dot(attn_grad, out_full, LAST).astype(LOW)
     out_weight_part = out_weight_part.reshape(local, groups, HDIM, width)
+    attended_grad = after(attended_grad, fc1_part, fc2_part)
+    fc1_part = pair_reduce(fc1_part, SIDE)
+    output = after(output, attended_grad)
+    early = send_back(output, slots, range(groups // 2))
     first_parts, projected_grad = [], []
     for chunk in range(local):
-        if chunk:
-            attended_grad = after(attended_grad, projected_grad[0], fc2_weight_grad)
         part_grad = attend_back(projected, attended_grad, groups, chunk)
         weight_part = dot(part_grad, hidden_attn, FIRST).astype(LOW)
-        first_parts.append(weight_part.reshape(groups, three, width))
-        first_parts.append(out_weight_part[chunk])
+        weight_part = weight_part.reshape(groups, three, width)
+        part = pair_reduce(jnp.concatenate([weight_part, out_weight_part[chunk]], axis=1), CORE)
         projected_grad.append(part_grad)
-    first_part = jnp.concatenate(first_parts, axis=1).reshape(-1, width)
-    projected_grad = after(tuple(projected_grad), first_part, fc1_weight_grad)
-    first_grad = reduce_weight(first_part).astype(FULL)
+        if not chunk:
+            attended_grad = after(attended_grad, part, fc1_part, *early)
+            fc1_part = scatter(fc1_part)
+            output = after(output, attended_grad)
+            late = send_back(output, slots, range(groups // 2, groups))
+        else:
+            projected_grad = after(projected_grad, part)
+        first_parts.append(pair_reduce(part, SIDE))
+    output = jnp.transpose(from_slots(early + late, slots), (1, 0, 2))
+    first_part = scatter(jnp.concatenate(first_parts, axis=1))
+    fc2_weight_grad = spread(fc2_part).astype(FULL)
+    fc1_weight_grad = spread(fc1_part).astype(FULL).T
+    first_grad = spread(first_part).reshape(4, local, -1, width)
+    first_grad = jnp.transpose(first_grad, (1, 0, 2, 3)).astype(FULL)
     first_grad = jnp.transpose(first_grad.reshape(local, 4, HDIM, width), (1, 0, 2, 3))
     first_grad = first_grad.reshape(4, local_width, width)
     qkv_weight_grad = jnp.transpose(first_grad[:3], (2, 0, 1))
     out_weight_grad = first_grad[3]
-    fc1_weight_grad = fc1_weight_grad.astype(FULL).T
-    fc2_weight_grad = fc2_weight_grad.astype(FULL)
     hidden_attn_grad = dot(jnp.concatenate(projected_grad, axis=1), qkv_full)
     qkv_bias_part = jnp.concatenate([jnp.sum(part, axis=0, dtype=FULL) for part in projected_grad])
     shift_attn_grad = jnp.sum(hidden_attn_grad, axis=0)
@@ -360,7 +401,12 @@
     tokens_grad = mixed_grad + norm_back(
         normed_attn, attn_scale, hidden_attn_grad * (1.0 + scale_attn)
     )
-    tokens_grad = from_slots(tokens_grad.astype(LOW), slots).astype(FULL)
+    tokens_grad = after(tokens_grad.astype(LOW), fc1_part, *late)
+    cut = groups - 2
+    early = send_back(tokens_grad, slots, range(cut))
+    tokens_grad = after(tokens_grad, first_part)
+    late = send_back(tokens_grad, slots, range(cut, groups))
+    tokens_grad = from_slots(early + late, slots).astype(FULL)
     tokens_grad = jnp.transpose(tokens_grad, (1, 0, 2))
 
     mod_row = jnp.concatenate(

time: 928 us -> 918 us (0.989)
  waiting for transfers between devices: 267 us -> 217 us
  local copies, waits for them, and re-layouts: 101 us -> 134 us
  other arithmetic: 46.3 us -> 69.1 us
  starting transfers between devices: 138 us -> 120 us
    ppermute x24 -> x32, waiting for transfers between devices: 98.2 us -> 60.7 us  [partner(): lax.ppermute(values, axis, [(i, i ^ bit) for i in range(lax.axis_size(axi...]
    convert_element_type x0 -> x10, other arithmetic: none -> 26.9 us  [the longest x8 25 us: pair_reduce(): return add(keep, partner(send, 'dp', bit)).astype(LOW)]
    unnamed x182 -> x200, local copies, waits for them, and re-layouts: 53.3 us -> 75.2 us
    ppermute x14, starting transfers between devices: 66.9 us -> 50.2 us  [to_slots(): piece = lax.ppermute(piece, 'tensor', pairs)]
    ppermute x14, waiting for transfers between devices: 73 us -> 57.3 us  [send_back(): piece = lax.ppermute(piece, 'tensor', pairs)]
    dynamic_slice x0 -> x6, local copies, waits for them, and re-layouts: none -> 12 us  [halves(): lax.dynamic_slice_in_dim(values, (1 - flag) * size, size, 1)]
    reduce_scatter x3, waiting for transfers between devices: 36.3 us -> 48.1 us  [scatter(): return lax.psum_scatter(held, 'tensor', scatter_dimension=0, tiled=True)]
    ppermute x24 -> x32, starting transfers between devices: 53.6 us -> 51.8 us  [partner(): lax.ppermute(values, axis, [(i, i ^ bit) for i in range(lax.axis_size(axi...]
  transfers between devices with their start and end apart: 58 -> 66, of which waited for: 24 -> 24; matrix products, arithmetic and copies ran while one was open for 36% -> 42% of each run, Pallas kernels for 16% -> 16%
where the time goes in v2:
time: 918 us; the launch traced here: 905 us
  waiting for transfers between devices  217 us (24%)
  matrix products  202 us (22%)
  Pallas kernels  147 us (16%)
  local copies, waits for them, and re-layouts  134 us (15%)
  starting transfers between devices  120 us (13%)
  other arithmetic  69.1 us (8%)
  between operations  16.7 us (2%)
    dot_general x16, matrix products, dot(): return lax.dot_general(left, right, dims, preferred_element_type=FULL)  202 us
    pallas_call x2, Pallas kernels, attend_back(): pl.pallas_call(functools.partial(attend_back_kernel, heads, chunk * colum...  88.1 us
    unnamed x200, local copies, waits for them, and re-layouts  75.2 us
    ppermute x32, waiting for transfers between devices, partner(): lax.ppermute(values, axis, [(i, i ^ bit) for i in range(lax.axis_size(axi...  60.7 us
    pallas_call x2, Pallas kernels, attend(): pl.pallas_call(functools.partial(attend_kernel, heads, chunk * column(hea...  58.7 us
    ppermute x14, waiting for transfers between devices, send_back(): piece = lax.ppermute(piece, 'tensor', pairs)  57.3 us
    ppermute x32, starting transfers between devices, partner(): lax.ppermute(values, axis, [(i, i ^ bit) for i in range(lax.axis_size(axi...  51.8 us
    ppermute x14, starting transfers between devices, to_slots(): piece = lax.ppermute(piece, 'tensor', pairs)  50.2 us
  transfers between devices with their start and end apart: 66, of which 24 were waited for; matrix products, arithmetic and copies ran while one was open for 42% of the time, Pallas kernels for 16%

profile of v2, /device:TPU:0, one launch (start us, length us, event | category | flops | bytes accessed | tf_op | source)
XLA Modules:
  0.0 904.7 jit_solution(1623740559941761389)
XLA Ops:
  19.7 7.3 collective-permute-start.4
  34.7 16.1 %collective-permute-done.8 = f32[2,6192]{1,0:T(2,128)S(1)} collective-permute-done((f32[2,6192]{1,0:T(2,128)S(1)}, f32[2,6192]{1,0:T(2,128)S(1)}, u32[]{:S(2)}, u32[]{:S(2)}) %collective-permute-start.8) | collective-permute-done | bytes 49568 | tf_op jit(solution)/shard_map/ppermute | solution.py:165
  55.2 4.8 collective-permute-done.9
  60.7 6.2 collective-permute-start
  77.8 4.1 collective-permute-start.2
  83.5 5.5 collective-permute-start.5
  102.2 33.0 %all-gather.4.cloned.1.call-done = bf16[4608,1152]{1,0:T(8,128)(2,1)} async-done(((bf16[144,1152]{1,0:T(8,128)(2,1)}), bf16[4608,1152]{1,0:T(8,128)(2,1)}) %all-gather.4.cloned.1.call-update) | async-done | bytes 10616848 | tf_op jit(solution)/shard_map/all_gather | solution.py:201
  135.2 5.6 copy.44
  145.1 8.0 slice.166
  153.1 15.6 %add_convert_fusion.projected = bf16[1024,3456]{1,0:T(8,128)(2,1)} fusion(bf16[3456,1152]{1,0:T(8,128)(2,1)} %bitcast.173, f32[3456]{0:T(1024)S(1)} %copy-done.52, bf16[1024,1152]{1,0:T(8,128)(2,1)S(1)} %copy-done.12, f32[1152]{0:T(1024)S(1)} %get-tuple-element.46, f32[1152]{0:T(1024)S(1)} %get-tuple-element.47, f32[1024]{0:T(1024)S(1)} %add_rsqrt_fusion.1, ...), kind=kOutput, calls=%fused_computation.13 | convolution fusion | flops 8167882752 | bytes 17431040 | tf_op jit(solution)/shard_map/dot_general | solution.py:22
  171.0 7.4 collective-permute-start.15
  182.4 4.1 collective-permute-start.10
  186.6 29.3 %shard_map.238 = bf16[1024,576]{1,0:T(8,128)(2,1)S(1)} custom-call(bf16[1024,3456]{1,0:T(8,128)(2,1)} %add_convert_fusion.projected), custom_call_target="tpu_custom_call" | custom-call | flops 17179869184 | bytes 4718592 | tf_op jit(solution)/shard_map/pallas_call | solution.py:77
  215.8 29.5 %shard_map.237 = bf16[1024,576]{1,0:T(8,128)(2,1)S(1)} custom-call(bf16[1024,3456]{1,0:T(8,128)(2,1)} %add_convert_fusion.projected), custom_call_target="tpu_custom_call" | custom-call | flops 17179869184 | bytes 4718592 | tf_op jit(solution)/shard_map/pallas_call | solution.py:77
  245.4 5.5 fusion.57
  253.7 21.1 %fusion.53 = f32[1024,4608]{1,0:T(8,128)} fusion(bf16[4608,1152]{1,0:T(8,128)(2,1)} %all-gather.6.cloned.1.call-done, f32[1024,1152]{1,0:T(8,128)} %copy-done.23, f32[1152]{0:T(1024)S(1)} %copy-done.61, f32[1152]{0:T(1024)S(1)} %copy-done.58, f32[1024]{0:T(1024)S(1)} %add_rsqrt_fusion, f32[1024]{0:T(1024)S(1)} %broadcast_multiply_fusion.4), kind=kOutput, calls=%fused_computation.262 | convolution fusion | flops 10877534208 | bytes 34227200 | tf_op jit(solution)/shard_map/dot_general | solution.py:22
  280.9 9.7 %collective-permute-done.12 = bf16[128,1152]{1,0:T(8,128)(2,1)S(1)} collective-permute-done((bf16[128,1152]{1,0:T(8,128)(2,1)S(1)}, bf16[128,1152]{1,0:T(8,128)(2,1)S(1)}, u32[]{:S(2)}, u32[]{:S(2)}) %collective-permute-start.12) | collective-permute-done | bytes 294944 | tf_op jit(solution)/shard_map/ppermute | solution.py:245
  290.7 6.0 collective-permute-done.13
  302.5 23.0 %convolution_convert_fusion.1 = bf16[4608,1152]{1,0:T(8,128)(2,1)} fusion(bf16[1024,1152]{1,0:T(8,128)(2,1)S(1)} %get-tuple-element.25, f32[1024,4608]{1,0:T(8,128)} %fusion.53, f32[4608]{0:T(1024)S(1)} %copy-done.51), kind=kOutput, calls=%fused_computation.3 | convolution fusion | flops 10924130304 | bytes 31868928 | tf_op jit(solution)/shard_map/dot_general | solution.py:22
  325.5 5.5 constant_dynamic-slice_fusion.6
  331.0 9.1 %collective-permute-done.17 = bf16[8,288,1152]{2,1,0:T(8,128)(2,1)} collective-permute-done((bf16[8,288,1152]{2,1,0:T(8,128)(2,1)}, bf16[8,288,1152]{2,1,0:T(8,128)(2,1)}, u32[]{:S(2)}, u32[]{:S(2)}) %collective-permute-start.17) | collective-permute-done | bytes 5308448 | tf_op jit(solution)/shard_map/ppermute | solution.py:165
  340.1 5.8 add_convert_fusion.2
  351.4 29.0 %fusion.6 = bf16[1024,4608]{1,0:T(8,128)(2,1)} fusion(f32[1024,4608]{1,0:T(8,128)} %fusion.53, f32[4608]{0:T(1024)S(1)} %copy-done.51, bf16[1024,1152]{1,0:T(8,128)(2,1)} %copy-done.29, bf16[4608,1152]{1,0:T(8,128)(2,1)} %all-gather.8.cloned.1.call-done), kind=kOutput, calls=%fused_computation.10 | convolution fusion | flops 10970726400 | bytes 41306112 | tf_op jit(solution)/shard_map/dot_general | solution.py:22
  380.4 17.1 %convolution_convert_fusion = bf16[4608,1152]{1,0:T(8,128)(2,1)S(1)} fusion(bf16[1024,4608]{1,0:T(8,128)(2,1)} %fusion.6, f32[1024,1152]{1,0:T(8,128)} %copy-done.23, f32[1152]{0:T(1024)S(1)} %copy-done.61, f32[1152]{0:T(1024)S(1)} %copy-done.58, f32[1024]{0:T(1024)S(1)} %add_rsqrt_fusion, f32[1024]{0:T(1024)S(1)} %broadcast_multiply_fusion.4), kind=kOutput, calls=%fused_computation.2 | convolution fusion | flops 10882842624 | bytes 24790016 | tf_op jit(solution)/shard_map/dot_general | solution.py:22
  400.5 4.1 copy-done.19
  404.5 5.1 collective-permute-done.18
  413.7 5.8 convert_reduce_fusion
  419.5 21.7 %multiply_reduce_fusion.1 = (bf16[1152]{0:T(1024)(128)(2,1)}, f32[1024]{0:T(1024)S(1)}, f32[1024]{0:T(1024)S(1)}, bf16[1152]{0:T(1024)(128)(2,1)}, f32[1024,1152]{1,0:T(8,128)}) fusion(f32[1024,1152]{1,0:T(8,128)} %copy-done.23, f32[1024]{0:T(1024)S(1)} %add_rsqrt_fusion, f32[1024]{0:T(1024)S(1)} %broadcast_multiply_fusion.4, f32[1152]{0:T(1024)S(1)} %copy-done.58, ...), kind=kOutput, calls=%fused_computation.60 | convolution fusion | flops 10882248704 | bytes 29516800 | tf_op jit(solution)/shard_map/dot_general | solution.py:22
  441.3 26.2 %multiply_reduce_fusion = (bf16[1152]{0:T(1024)(128)(2,1)}, bf16[1024,1152]{1,0:T(8,128)(2,1)}, f32[1152]{0:T(1024)}, bf16[1024,1152]{1,0:T(8,128)(2,1)}, f32[1024,1152]{1,0:T(8,128)}) fusion(bf16[1024,1152]{1,0:T(8,128)(2,1)} %copy-done.25, f32[]{:T(128)S(6)} %convert_element_type.198, f32[1024,1152]{1,0:T(8,128)S(1)} %bitcast.176, ...), kind=kOutput, calls=%fused_computation.59 | convolution fusion | flops 10943592448 | bytes 50785028 | tf_op jit(solution)/shard_map/dot_general | solution.py:22
  467.5 5.2 convolution_convert_fusion.4
  475.6 4.8 convolution_convert_fusion.5.attended_grad
  480.5 5.5 add_convert_fusion.1
  501.4 44.0 %shard_map.239 = bf16[1024,1728]{1,0:T(8,128)(2,1)S(1)} custom-call(bf16[1024,3456]{1,0:T(8,128)(2,1)} %add_convert_fusion.projected, bf16[1024,1152]{1,0:T(8,128)(2,1)S(1)} %copy-done.5), custom_call_target="tpu_custom_call" | custom-call | flops 34359738368 | bytes 8257536 | tf_op jit(solution)/shard_map/pallas_call | solution.py:138
  553.4 7.9 convolution_convert_fusion.3
  566.5 6.0 collective-permute-done.58
  579.8 44.1 %shard_map.240 = bf16[1024,1728]{1,0:T(8,128)(2,1)S(1)} custom-call(bf16[1024,3456]{1,0:T(8,128)(2,1)} %add_convert_fusion.projected, bf16[1024,1152]{1,0:T(8,128)(2,1)S(1)} %copy-done.6), custom_call_target="tpu_custom_call" | custom-call | flops 34359738368 | bytes 8257536 | tf_op jit(solution)/shard_map/pallas_call | solution.py:138
  630.8 6.0 convolution_convert_fusion.2
  637.9 32.4 %collective-permute-done.25 = bf16[128,1152]{1,0:T(8,128)(2,1)S(1)} collective-permute-done((bf16[128,1152]{1,0:T(8,128)(2,1)S(1)}, bf16[128,1152]{1,0:T(8,128)(2,1)S(1)}, u32[]{:S(2)}, u32[]{:S(2)}) %collective-permute-start.25) | collective-permute-done | bytes 294944 | tf_op jit(solution)/shard_map/ppermute | solution.py:260
  689.3 15.3 %fusion.24 = (bf16[1152]{0:T(1024)(128)(2,1)S(1)}, f32[1024]{0:T(1024)S(1)}, f32[1024]{0:T(1024)S(1)}, bf16[1152]{0:T(1024)(128)(2,1)S(1)}, f32[1024,1152]{1,0:T(8,128)}) fusion(bf16[1024,1152]{1,0:T(8,128)(2,1)S(1)} %copy-done.13, f32[1024]{0:T(1024)S(1)} %copy-done.54, f32[1024]{0:T(1024)S(1)} %copy-done.45, f32[1152]{0:T(1024)S(1)} %copy-done.47, ...), kind=kOutput, calls=%fused_computation.55 | convolution fusion | flops 8179675136 | bytes 22144000 | tf_op jit(solution)/shard_map/dot_general | solution.py:22
  705.0 8.4 multiply_reduce_fusion.2
  718.8 11.6 %collective-permute-start.40 = (bf16[2,8,864]{2,1,0:T(8,128)(2,1)S(1)}, bf16[2,8,864]{2,1,0:T(8,128)(2,1)S(1)}, u32[]{:S(2)}, u32[]{:S(2)}) collective-permute-start(bf16[2,8,864]{2,1,0:T(8,128)(2,1)S(1)} %pad_maximum_fusion.13), channel_id=1, source_target_pairs={{0,2},{1,3},{2,0},{3,1},{4,6},{5,7},{6,4},{7,5},{8,10},{9,11},{10,... | collective-permute-start | bytes 82952 | tf_op jit(solution)/shard_map/ppermute | solution.py:165
  745.7 5.0 collective-permute-start.53
  752.7 5.1 collective-permute-done.43
  757.8 8.1 collective-permute-start.44
  765.9 6.5 collective-permute-done.53
  791.9 18.5 %collective-permute-done.30 = bf16[128,1152]{1,0:T(8,128)(2,1)S(1)} collective-permute-done((bf16[128,1152]{1,0:T(8,128)(2,1)S(1)}, bf16[128,1152]{1,0:T(8,128)(2,1)S(1)}, u32[]{:S(2)}, u32[]{:S(2)}) %collective-permute-start.30) | collective-permute-done | bytes 294944 | tf_op jit(solution)/shard_map/ppermute | solution.py:260
  821.6 45.8 %reduce-scatter.8.cloned.1.call-done = bf16[144,1152]{1,0:T(8,128)(2,1)} async-done(((bf16[1152,1152]{1,0:T(8,128)(2,1)}), bf16[144,1152]{1,0:T(8,128)(2,1)}) %reduce-scatter.8.cloned.1.call-update) | async-done | bytes 331792 | tf_op jit(solution)/shard_map/reduce_scatter | solution.py:219
  873.8 5.9 collective-permute-done.37
  (443 shorter events, 230.9 us)
Async XLA Ops:
  7.2 127.9 %all-gather.4.cloned.1.call-start = ((), (), s32[]{:S(2)}) async-start(), calls=%async_computation.3 | async-start | bytes 10948608 | tf_op jit(solution)/shard_map/all_gather | solution.py:201
  9.8 243.9 %all-gather.6.cloned.1.call-start = ((), (), s32[]{:S(2)}) async-start(), calls=%async_computation.4 | async-start | bytes 10948608 | tf_op jit(solution)/shard_map/all_gather | solution.py:201
  11.6 339.9 %all-gather.8.cloned.1.call-start = ((), (), s32[]{:S(2)}) async-start(), calls=%async_computation.5 | async-start | bytes 10948608 | tf_op jit(solution)/shard_map/all_gather | solution.py:201
  12.8 19.8 %collective-permute-start.7 = (f32[1,6192]{1,0:T(1,128)S(1)}, f32[1,6192]{1,0:T(1,128)S(1)}, u32[]{:S(2)}, u32[]{:S(2)}) collective-permute-start(f32[1,6192]{1,0:T(1,128)S(1)} %broadcast_in_dim.6), channel_id=1, source_target_pairs={{0,1},{1,0},{2,3},{3,2},{4,5},{5,4},{6,7},{7,6},{8,9},{9,8},{10,11... | collective-permute-start | bytes 74312 | tf_op jit(solution)/shard_map/ppermute | solution.py:165
  18.3 77.3 %collective-permute-start.6 = (bf16[128,1152]{1,0:T(8,128)(2,1)S(1)}, bf16[128,1152]{1,0:T(8,128)(2,1)}, u32[]{:S(2)}, u32[]{:S(2)}) collective-permute-start(bf16[128,1152]{1,0:T(8,128)(2,1)S(1)} %get-tuple-element.88), channel_id=1, source_target_pairs={{2,1},{3,2},{4,3},{5,4},{6,5},{7,6},{10,9},{11,10},{12,11},{13,12}... | collective-permute-start | bytes 884744 | tf_op jit(solution)/shard_map/ppermute | solution.py:245
  19.7 73.5 %collective-permute-start.4 = (bf16[128,1152]{1,0:T(8,128)(2,1)S(1)}, bf16[128,1152]{1,0:T(8,128)(2,1)}, u32[]{:S(2)}, u32[]{:S(2)}) collective-permute-start(bf16[128,1152]{1,0:T(8,128)(2,1)S(1)} %get-tuple-element.89), channel_id=1, source_target_pairs={{0,5},{1,6},{4,1},{5,2},{6,3},{7,4},{8,13},{9,14},{12,9},{13,10},{... | collective-permute-start | bytes 884744 | tf_op jit(solution)/shard_map/ppermute | solution.py:245
  27.0 64.5 %collective-permute-start.3 = (bf16[128,1152]{1,0:T(8,128)(2,1)S(1)}, bf16[128,1152]{1,0:T(8,128)(2,1)}, u32[]{:S(2)}, u32[]{:S(2)}) collective-permute-start(bf16[128,1152]{1,0:T(8,128)(2,1)S(1)} %get-tuple-element.90), channel_id=1, source_target_pairs={{0,4},{1,5},{2,6},{5,1},{6,2},{7,3},{8,12},{9,13},{10,14},{13,9},{... | collective-permute-start | bytes 884744 | tf_op jit(solution)/shard_map/ppermute | solution.py:245
  29.0 54.6 %collective-permute-start.1 = (bf16[128,1152]{1,0:T(8,128)(2,1)}, bf16[128,1152]{1,0:T(8,128)(2,1)}, u32[]{:S(2)}, u32[]{:S(2)}) collective-permute-start(bf16[128,1152]{1,0:T(8,128)(2,1)} %get-tuple-element.92), channel_id=1, source_target_pairs={{0,2},{1,3},{2,4},{3,5},{4,6},{7,1},{8,10},{9,11},{10,12},{11,13},... | collective-permute-start | bytes 884744 | tf_op jit(solution)/shard_map/ppermute | solution.py:245
  32.8 18.0 %collective-permute-start.8 = (f32[2,6192]{1,0:T(2,128)S(1)}, f32[2,6192]{1,0:T(2,128)S(1)}, u32[]{:S(2)}, u32[]{:S(2)}) collective-permute-start(f32[2,6192]{1,0:T(2,128)S(1)} %pad_maximum_fusion.10), channel_id=1, source_target_pairs={{0,2},{1,3},{2,0},{3,1},{4,6},{5,7},{6,4},{7,5},{8,10},{9,11},{10,... | collective-permute-start | bytes 148616 | tf_op jit(solution)/shard_map/ppermute | solution.py:165
  34.6 459.2 %reduce-scatter.4.cloned.1.call-start = ((), (), s32[]{:S(2)}) async-start(), calls=%async_computation.6 | async-start | bytes 2985984 | tf_op jit(solution)/shard_map/reduce_scatter | solution.py:219
  60.7 17.1 %collective-permute-start = (bf16[128,1152]{1,0:T(8,128)(2,1)}, bf16[128,1152]{1,0:T(8,128)(2,1)}, u32[]{:S(2)}, u32[]{:S(2)}) collective-permute-start(bf16[128,1152]{1,0:T(8,128)(2,1)} %get-tuple-element.93), channel_id=1, source_target_pairs={{0,1},{1,2},{2,3},{3,4},{4,5},{5,6},{8,9},{9,10},{10,11},{11,12},{... | collective-permute-start | bytes 884744 | tf_op jit(solution)/shard_map/ppermute | solution.py:245
  77.8 13.0 %collective-permute-start.2 = (bf16[128,1152]{1,0:T(8,128)(2,1)}, bf16[128,1152]{1,0:T(8,128)(2,1)S(1)}, u32[]{:S(2)}, u32[]{:S(2)}) collective-permute-start(bf16[128,1152]{1,0:T(8,128)(2,1)} %get-tuple-element.91), channel_id=1, source_target_pairs={{0,3},{1,4},{2,5},{3,6},{6,1},{7,2},{8,11},{9,12},{10,13},{11,14},... | collective-permute-start | bytes 884744 | tf_op jit(solution)/shard_map/ppermute | solution.py:245
  83.5 11.3 %collective-permute-start.5 = (bf16[128,1152]{1,0:T(8,128)(2,1)S(1)}, bf16[128,1152]{1,0:T(8,128)(2,1)S(1)}, u32[]{:S(2)}, u32[]{:S(2)}) collective-permute-start(bf16[128,1152]{1,0:T(8,128)(2,1)S(1)} %get-tuple-element.94), channel_id=1, source_target_pairs={{0,6},{3,1},{4,2},{5,3},{6,4},{7,5},{8,14},{11,9},{12,10},{13,11},... | collective-permute-start | bytes 884744 | tf_op jit(solution)/shard_map/ppermute | solution.py:245
  169.6 129.0 %collective-permute-start.16 = (bf16[128,1152]{1,0:T(8,128)(2,1)S(1)}, bf16[128,1152]{1,0:T(8,128)(2,1)}, u32[]{:S(2)}, u32[]{:S(2)}) collective-permute-start(bf16[128,1152]{1,0:T(8,128)(2,1)S(1)} %get-tuple-element.81), channel_id=1, source_target_pairs={{2,1},{3,2},{4,3},{5,4},{6,5},{7,6},{10,9},{11,10},{12,11},{13,12}... | collective-permute-start | bytes 884744 | tf_op jit(solution)/shard_map/ppermute | solution.py:245
  171.0 126.7 %collective-permute-start.15 = (bf16[128,1152]{1,0:T(8,128)(2,1)S(1)}, bf16[128,1152]{1,0:T(8,128)(2,1)}, u32[]{:S(2)}, u32[]{:S(2)}) collective-permute-start(bf16[128,1152]{1,0:T(8,128)(2,1)S(1)} %get-tuple-element.82), channel_id=1, source_target_pairs={{0,6},{3,1},{4,2},{5,3},{6,4},{7,5},{8,14},{11,9},{12,10},{13,11},... | collective-permute-start | bytes 884744 | tf_op jit(solution)/shard_map/ppermute | solution.py:245
  178.4 118.3 %collective-permute-start.14 = (bf16[128,1152]{1,0:T(8,128)(2,1)S(1)}, bf16[128,1152]{1,0:T(8,128)(2,1)}, u32[]{:S(2)}, u32[]{:S(2)}) collective-permute-start(bf16[128,1152]{1,0:T(8,128)(2,1)S(1)} %get-tuple-element.83), channel_id=1, source_target_pairs={{0,5},{1,6},{4,1},{5,2},{6,3},{7,4},{8,13},{9,14},{12,9},{13,10},{... | collective-permute-start | bytes 884744 | tf_op jit(solution)/shard_map/ppermute | solution.py:245
  180.4 98.2 %collective-permute-start.11 = (bf16[128,1152]{1,0:T(8,128)(2,1)}, bf16[128,1152]{1,0:T(8,128)(2,1)}, u32[]{:S(2)}, u32[]{:S(2)}) collective-permute-start(bf16[128,1152]{1,0:T(8,128)(2,1)} %get-tuple-element.86), channel_id=1, source_target_pairs={{0,2},{1,3},{2,4},{3,5},{4,6},{7,1},{8,10},{9,11},{10,12},{11,13},... | collective-permute-start | bytes 884744 | tf_op jit(solution)/shard_map/ppermute | solution.py:245
  182.4 93.4 %collective-permute-start.10 = (bf16[128,1152]{1,0:T(8,128)(2,1)}, bf16[128,1152]{1,0:T(8,128)(2,1)}, u32[]{:S(2)}, u32[]{:S(2)}) collective-permute-start(bf16[128,1152]{1,0:T(8,128)(2,1)} %get-tuple-element.87), channel_id=1, source_target_pairs={{0,1},{1,2},{2,3},{3,4},{4,5},{5,6},{8,9},{9,10},{10,11},{11,12},{... | collective-permute-start | bytes 884744 | tf_op jit(solution)/shard_map/ppermute | solution.py:245
  275.8 14.8 %collective-permute-start.12 = (bf16[128,1152]{1,0:T(8,128)(2,1)S(1)}, bf16[128,1152]{1,0:T(8,128)(2,1)S(1)}, u32[]{:S(2)}, u32[]{:S(2)}) collective-permute-start(bf16[128,1152]{1,0:T(8,128)(2,1)S(1)} %copy-done.39), channel_id=1, source_target_pairs={{0,3},{1,4},{2,5},{3,6},{6,1},{7,2},{8,11},{9,12},{10,13},{11,14},... | collective-permute-start | bytes 884744 | tf_op jit(solution)/shard_map/ppermute | solution.py:245
  278.6 18.0 %collective-permute-start.13 = (bf16[128,1152]{1,0:T(8,128)(2,1)S(1)}, bf16[128,1152]{1,0:T(8,128)(2,1)S(1)}, u32[]{:S(2)}, u32[]{:S(2)}) collective-permute-start(bf16[128,1152]{1,0:T(8,128)(2,1)S(1)} %get-tuple-element.84), channel_id=1, source_target_pairs={{0,4},{1,5},{2,6},{5,1},{6,2},{7,3},{8,12},{9,13},{10,14},{13,9},{... | collective-permute-start | bytes 884744 | tf_op jit(solution)/shard_map/ppermute | solution.py:245
  349.9 59.8 %collective-permute-start.18 = (bf16[8,144,1152]{2,1,0:T(8,128)(2,1)}, bf16[8,144,1152]{2,1,0:T(8,128)(2,1)}, u32[]{:S(2)}, u32[]{:S(2)}) collective-permute-start(bf16[8,144,1152]{2,1,0:T(8,128)(2,1)} %constant_dynamic-slice_fusion.5), channel_id=1, source_target_pairs={{0,16},{8,24},{16,0},{24,8},{1,17},{9,25},{17,1},{25,9},{2,18},{10... | collective-permute-start | bytes 7962632 | tf_op jit(solution)/shard_map/ppermute | solution.py:165
  404.5 75.9 %collective-permute-start.19 = (bf16[8,288,1152]{2,1,0:T(8,128)(2,1)}, bf16[8,288,1152]{2,1,0:T(8,128)(2,1)}, u32[]{:S(2)}, u32[]{:S(2)}) collective-permute-start(bf16[8,288,1152]{2,1,0:T(8,128)(2,1)} %constant_dynamic-slice_fusion.4), channel_id=1, source_target_pairs={{0,8},{8,0},{16,24},{24,16},{1,9},{9,1},{17,25},{25,17},{2,10},{10... | collective-permute-start | bytes 15925256 | tf_op jit(solution)/shard_map/ppermute | solution.py:165
  413.6 316.8 %reduce-scatter.6.cloned.1.call-start = ((), (), s32[]{:S(2)}) async-start(), calls=%async_computation.7 | async-start | bytes 2985984 | tf_op jit(solution)/shard_map/reduce_scatter | solution.py:219
  490.0 59.0 %collective-permute-start.24 = (bf16[8,144,1152]{2,1,0:T(8,128)(2,1)}, bf16[8,144,1152]{2,1,0:T(8,128)(2,1)}, u32[]{:S(2)}, u32[]{:S(2)}) collective-permute-start(bf16[8,144,1152]{2,1,0:T(8,128)(2,1)} %constant_dynamic-slice_fusion.3), channel_id=1, source_target_pairs={{0,16},{8,24},{16,0},{24,8},{1,17},{9,25},{17,1},{25,9},{2,18},{10... | collective-permute-start | bytes 7962632 | tf_op jit(solution)/shard_map/ppermute | solution.py:165
  495.9 78.6 %collective-permute-start.22 = (bf16[128,1152]{1,0:T(8,128)(2,1)}, bf16[128,1152]{1,0:T(8,128)(2,1)}, u32[]{:S(2)}, u32[]{:S(2)}) collective-permute-start(bf16[128,1152]{1,0:T(8,128)(2,1)} %get-tuple-element.78), channel_id=1, source_target_pairs={{3,0},{4,1},{5,2},{6,3},{1,6},{2,7},{11,8},{12,9},{13,10},{14,11},... | collective-permute-start | bytes 884744 | tf_op jit(solution)/shard_map/ppermute | solution.py:260
  497.2 75.6 %collective-permute-start.21 = (bf16[128,1152]{1,0:T(8,128)(2,1)}, bf16[128,1152]{1,0:T(8,128)(2,1)}, u32[]{:S(2)}, u32[]{:S(2)}) collective-permute-start(bf16[128,1152]{1,0:T(8,128)(2,1)} %get-tuple-element.79), channel_id=1, source_target_pairs={{2,0},{3,1},{4,2},{5,3},{6,4},{1,7},{10,8},{11,9},{12,10},{13,11},... | collective-permute-start | bytes 884744 | tf_op jit(solution)/shard_map/ppermute | solution.py:260
  498.5 66.3 %collective-permute-start.20 = (bf16[128,1152]{1,0:T(8,128)(2,1)}, bf16[128,1152]{1,0:T(8,128)(2,1)}, u32[]{:S(2)}, u32[]{:S(2)}) collective-permute-start(bf16[128,1152]{1,0:T(8,128)(2,1)} %get-tuple-element.80), channel_id=1, source_target_pairs={{1,0},{2,1},{3,2},{4,3},{5,4},{6,5},{9,8},{10,9},{11,10},{12,11},{... | collective-permute-start | bytes 884744 | tf_op jit(solution)/shard_map/ppermute | solution.py:260
  552.9 314.5 %reduce-scatter.8.cloned.1.call-start = ((), (), s32[]{:S(2)}) async-start(), calls=%async_computation.8 | async-start | bytes 2985984 | tf_op jit(solution)/shard_map/reduce_scatter | solution.py:219
  562.2 15.9 %collective-permute-start.23 = (bf16[8,144,1152]{2,1,0:T(8,128)(2,1)S(1)}, bf16[8,144,1152]{2,1,0:T(8,128)(2,1)S(1)}, u32[]{:S(2)}, u32[]{:S(2)}) collective-permute-start(bf16[8,144,1152]{2,1,0:T(8,128)(2,1)S(1)} %fusion.28), channel_id=1, source_target_pairs={{0,8},{8,0},{16,24},{24,16},{1,9},{9,1},{17,25},{25,17},{2,10},{10... | collective-permute-start | bytes 7962632 | tf_op jit(solution)/shard_map/ppermute | solution.py:165
  562.3 10.2 %collective-permute-start.58 = (bf16[144,1152]{1,0:T(8,128)(2,1)S(1)}, bf16[144,1152]{1,0:T(8,128)(2,1)S(1)}, u32[]{:S(2)}, u32[]{:S(2)}) collective-permute-start(bf16[144,1152]{1,0:T(8,128)(2,1)S(1)} %copy-done.36), channel_id=1, source_target_pairs={{0,16},{8,24},{16,0},{24,8},{1,17},{9,25},{17,1},{25,9},{2,18},{10... | collective-permute-start | bytes 995336 | tf_op jit(solution)/shard_map/ppermute | solution.py:165
  624.0 48.6 %collective-permute-start.28 = (bf16[128,1152]{1,0:T(8,128)(2,1)S(1)}, bf16[128,1152]{1,0:T(8,128)(2,1)S(1)}, u32[]{:S(2)}, u32[]{:S(2)}) collective-permute-start(bf16[128,1152]{1,0:T(8,128)(2,1)S(1)} %get-tuple-element.74), channel_id=1, source_target_pairs={{1,2},{2,3},{3,4},{4,5},{5,6},{6,7},{9,10},{10,11},{11,12},{12,13}... | collective-permute-start | bytes 884744 | tf_op jit(solution)/shard_map/ppermute | solution.py:260
  624.8 47.0 %collective-permute-start.27 = (bf16[128,1152]{1,0:T(8,128)(2,1)S(1)}, bf16[128,1152]{1,0:T(8,128)(2,1)S(1)}, u32[]{:S(2)}, u32[]{:S(2)}) collective-permute-start(bf16[128,1152]{1,0:T(8,128)(2,1)S(1)} %get-tuple-element.75), channel_id=1, source_target_pairs={{6,0},{1,3},{2,4},{3,5},{4,6},{5,7},{14,8},{9,11},{10,12},{11,13},... | collective-permute-start | bytes 884744 | tf_op jit(solution)/shard_map/ppermute | solution.py:260
  626.4 44.7 %collective-permute-start.26 = (bf16[128,1152]{1,0:T(8,128)(2,1)S(1)}, bf16[128,1152]{1,0:T(8,128)(2,1)S(1)}, u32[]{:S(2)}, u32[]{:S(2)}) collective-permute-start(bf16[128,1152]{1,0:T(8,128)(2,1)S(1)} %get-tuple-element.76), channel_id=1, source_target_pairs={{5,0},{6,1},{1,4},{2,5},{3,6},{4,7},{13,8},{14,9},{9,12},{10,13},{... | collective-permute-start | bytes 884744 | tf_op jit(solution)/shard_map/ppermute | solution.py:260
  627.7 42.6 %collective-permute-start.25 = (bf16[128,1152]{1,0:T(8,128)(2,1)S(1)}, bf16[128,1152]{1,0:T(8,128)(2,1)S(1)}, u32[]{:S(2)}, u32[]{:S(2)}) collective-permute-start(bf16[128,1152]{1,0:T(8,128)(2,1)S(1)} %get-tuple-element.77), channel_id=1, source_target_pairs={{4,0},{5,1},{6,2},{1,5},{2,6},{3,7},{12,8},{13,9},{14,10},{9,13},{... | collective-permute-start | bytes 884744 | tf_op jit(solution)/shard_map/ppermute | solution.py:260
  629.1 55.9 %collective-permute-start.35 = (bf16[8,72,1152]{2,1,0:T(8,128)(2,1)S(1)}, bf16[8,72,1152]{2,1,0:T(8,128)(2,1)S(1)}, u32[]{:S(2)}, u32[]{:S(2)}) collective-permute-start(bf16[8,72,1152]{2,1,0:T(8,128)(2,1)S(1)} %constant_dynamic-slice_fusion.2), channel_id=1, source_target_pairs={{0,16},{8,24},{16,0},{24,8},{1,17},{9,25},{17,1},{25,9},{2,18},{10... | collective-permute-start | bytes 3981320 | tf_op jit(solution)/shard_map/ppermute | solution.py:165
  670.3 16.1 %collective-permute-start.29 = (bf16[8,144,1152]{2,1,0:T(8,128)(2,1)S(1)}, bf16[8,144,1152]{2,1,0:T(8,128)(2,1)S(1)}, u32[]{:S(2)}, u32[]{:S(2)}) collective-permute-start(bf16[8,144,1152]{2,1,0:T(8,128)(2,1)S(1)} %fusion.26), channel_id=1, source_target_pairs={{0,8},{8,0},{16,24},{24,16},{1,9},{9,1},{17,25},{25,17},{2,10},{10... | collective-permute-start | bytes 7962632 | tf_op jit(solution)/shard_map/ppermute | solution.py:165
  718.8 13.4 %collective-permute-start.40 = (bf16[2,8,864]{2,1,0:T(8,128)(2,1)S(1)}, bf16[2,8,864]{2,1,0:T(8,128)(2,1)S(1)}, u32[]{:S(2)}, u32[]{:S(2)}) collective-permute-start(bf16[2,8,864]{2,1,0:T(8,128)(2,1)S(1)} %pad_maximum_fusion.13), channel_id=1, source_target_pairs={{0,2},{1,3},{2,0},{3,1},{4,6},{5,7},{6,4},{7,5},{8,10},{9,11},{10,... | collective-permute-start | bytes 82952 | tf_op jit(solution)/shard_map/ppermute | solution.py:165
  731.1 44.0 %collective-permute-start.36 = (bf16[8,72,1152]{2,1,0:T(8,128)(2,1)S(1)}, bf16[8,72,1152]{2,1,0:T(8,128)(2,1)S(1)}, u32[]{:S(2)}, u32[]{:S(2)}) collective-permute-start(bf16[8,72,1152]{2,1,0:T(8,128)(2,1)S(1)} %constant_dynamic-slice_fusion.1), channel_id=1, source_target_pairs={{0,16},{8,24},{16,0},{24,8},{1,17},{9,25},{17,1},{25,9},{2,18},{10... | collective-permute-start | bytes 3981320 | tf_op jit(solution)/shard_map/ppermute | solution.py:165
  740.7 10.0 %collective-permute-start.47 = (bf16[1,8,864]{2,1,0:T(8,128)(2,1)S(1)}, bf16[1,8,864]{2,1,0:T(8,128)(2,1)S(1)}, u32[]{:S(2)}, u32[]{:S(2)}) collective-permute-start(bf16[1,8,864]{2,1,0:T(8,128)(2,1)S(1)} %bitcast.185), channel_id=1, source_target_pairs={{0,8},{8,0},{16,24},{24,16},{1,9},{9,1},{17,25},{25,17},{2,10},{10... | collective-permute-start | bytes 41480 | tf_op jit(solution)/shard_map/ppermute | solution.py:165
  743.0 76.6 %collective-permute-start.34 = (bf16[128,1152]{1,0:T(8,128)(2,1)}, bf16[128,1152]{1,0:T(8,128)(2,1)}, u32[]{:S(2)}, u32[]{:S(2)}) collective-permute-start(bf16[128,1152]{1,0:T(8,128)(2,1)} %get-tuple-element.69), channel_id=1, source_target_pairs={{5,0},{6,1},{1,4},{2,5},{3,6},{4,7},{13,8},{14,9},{9,12},{10,13},{... | collective-permute-start | bytes 884744 | tf_op jit(solution)/shard_map/ppermute | solution.py:260
  744.3 73.6 %collective-permute-start.33 = (bf16[128,1152]{1,0:T(8,128)(2,1)}, bf16[128,1152]{1,0:T(8,128)(2,1)}, u32[]{:S(2)}, u32[]{:S(2)}) collective-permute-start(bf16[128,1152]{1,0:T(8,128)(2,1)} %get-tuple-element.70), channel_id=1, source_target_pairs={{4,0},{5,1},{6,2},{1,5},{2,6},{3,7},{12,8},{13,9},{14,10},{9,13},{... | collective-permute-start | bytes 884744 | tf_op jit(solution)/shard_map/ppermute | solution.py:260
  745.7 26.8 %collective-permute-start.53 = (f32[10368]{0:T(1024)S(1)}, f32[10368]{0:T(1024)S(1)}, u32[]{:S(2)}, u32[]{:S(2)}) collective-permute-start(f32[10368]{0:T(1024)S(1)} %add.354), channel_id=1, source_target_pairs={{0,4},{1,5},{2,6},{3,7},{4,0},{5,1},{6,2},{7,3},{8,12},{9,13},{10,... | collective-permute-start | bytes 124424 | tf_op jit(solution)/shard_map/ppermute | solution.py:165
  757.8 15.9 %collective-permute-start.44 = (f32[6,1152]{1,0:T(8,128)S(1)}, f32[6,1152]{1,0:T(8,128)S(1)}, u32[]{:S(2)}, u32[]{:S(2)}) collective-permute-start(f32[6,1152]{1,0:T(8,128)S(1)} %add.351), channel_id=1, source_target_pairs={{0,4},{1,5},{2,6},{3,7},{4,0},{5,1},{6,2},{7,3},{8,12},{9,13},{10,... | collective-permute-start | bytes 82952 | tf_op jit(solution)/shard_map/ppermute | solution.py:165
  772.4 41.1 %collective-permute-start.32 = (bf16[128,1152]{1,0:T(8,128)(2,1)}, bf16[128,1152]{1,0:T(8,128)(2,1)}, u32[]{:S(2)}, u32[]{:S(2)}) collective-permute-start(bf16[128,1152]{1,0:T(8,128)(2,1)} %get-tuple-element.71), channel_id=1, source_target_pairs={{3,0},{4,1},{5,2},{6,3},{1,6},{2,7},{11,8},{12,9},{13,10},{14,11},... | collective-permute-start | bytes 884744 | tf_op jit(solution)/shard_map/ppermute | solution.py:260
  778.5 34.2 %collective-permute-start.31 = (bf16[128,1152]{1,0:T(8,128)(2,1)S(1)}, bf16[128,1152]{1,0:T(8,128)(2,1)S(1)}, u32[]{:S(2)}, u32[]{:S(2)}) collective-permute-start(bf16[128,1152]{1,0:T(8,128)(2,1)S(1)} %copy-done.37), channel_id=1, source_target_pairs={{2,0},{3,1},{4,2},{5,3},{6,4},{1,7},{10,8},{11,9},{12,10},{13,11},... | collective-permute-start | bytes 884744 | tf_op jit(solution)/shard_map/ppermute | solution.py:260
  787.9 22.4 %collective-permute-start.30 = (bf16[128,1152]{1,0:T(8,128)(2,1)S(1)}, bf16[128,1152]{1,0:T(8,128)(2,1)S(1)}, u32[]{:S(2)}, u32[]{:S(2)}) collective-permute-start(bf16[128,1152]{1,0:T(8,128)(2,1)S(1)} %copy-done.38), channel_id=1, source_target_pairs={{1,0},{2,1},{3,2},{4,3},{5,4},{6,5},{9,8},{10,9},{11,10},{12,11},{... | collective-permute-start | bytes 884744 | tf_op jit(solution)/shard_map/ppermute | solution.py:260
  868.6 11.1 %collective-permute-start.37 = (bf16[128,1152]{1,0:T(8,128)(2,1)S(1)}, bf16[128,1152]{1,0:T(8,128)(2,1)S(1)}, u32[]{:S(2)}, u32[]{:S(2)}) collective-permute-start(bf16[128,1152]{1,0:T(8,128)(2,1)S(1)} %get-tuple-element.68), channel_id=1, source_target_pairs={{6,0},{1,3},{2,4},{3,5},{4,6},{5,7},{14,8},{9,11},{10,12},{11,13},... | collective-permute-start | bytes 884744 | tf_op jit(solution)/shard_map/ppermute | solution.py:260
  872.2 17.9 %collective-permute-start.49 = (bf16[144,1152]{1,0:T(8,128)(2,1)S(1)}, bf16[144,1152]{1,0:T(8,128)(2,1)S(1)}, u32[]{:S(2)}, u32[]{:S(2)}) collective-permute-start(bf16[144,1152]{1,0:T(8,128)(2,1)S(1)} %copy-done.35), channel_id=1, source_target_pairs={{0,16},{8,24},{16,0},{24,8},{1,17},{9,25},{17,1},{25,9},{2,18},{10... | collective-permute-start | bytes 995336 | tf_op jit(solution)/shard_map/ppermute | solution.py:165
  (93 other events, 1658.9 us)
Sparse Core Ops, SparseCore 0:
  11.5 123.5 all-gather.3
  138.6 100.7 all-gather.5
  242.4 102.4 all-gather.7
  413.8 80.0 reduce-scatter.3
  553.0 81.9 reduce-scatter.5
  777.5 89.8 reduce-scatter.7

commit v3 on v2

--- a/solution.py
+++ b/solution.py
@@ -379,12 +379,9 @@
         if not chunk:
             attended_grad = after(attended_grad, part, fc1_part, *early)
             fc1_part = scatter(fc1_part)
-            output = after(output, attended_grad)
-            late = send_back(output, slots, range(groups // 2, groups))
         else:
             projected_grad = after(projected_grad, part)
         first_parts.append(pair_reduce(part, SIDE))
-    output = jnp.transpose(from_slots(early + late, slots), (1, 0, 2))
     first_part = scatter(jnp.concatenate(first_parts, axis=1))
     fc2_weight_grad = spread(fc2_part).astype(FULL)
     fc1_weight_grad = spread(fc1_part).astype(FULL).T
@@ -395,18 +392,22 @@
     qkv_weight_grad = jnp.transpose(first_grad[:3], (2, 0, 1))
     out_weight_grad = first_grad[3]
     hidden_attn_grad = dot(jnp.concatenate(projected_grad, axis=1), qkv_full)
+    hidden_attn_grad = after(hidden_attn_grad, *first_parts)
     qkv_bias_part = jnp.concatenate([jnp.sum(part, axis=0, dtype=FULL) for part in projected_grad])
     shift_attn_grad = jnp.sum(hidden_attn_grad, axis=0)
     scale_attn_grad = jnp.sum(hidden_attn_grad * normed_attn, axis=0)
     tokens_grad = mixed_grad + norm_back(
         normed_attn, attn_scale, hidden_attn_grad * (1.0 + scale_attn)
     )
-    tokens_grad = after(tokens_grad.astype(LOW), fc1_part, *late)
-    cut = groups - 2
-    early = send_back(tokens_grad, slots, range(cut))
-    tokens_grad = after(tokens_grad, first_part)
-    late = send_back(tokens_grad, slots, range(cut, groups))
-    tokens_grad = from_slots(early + late, slots).astype(FULL)
+    tokens_grad = after(tokens_grad.astype(LOW), fc1_part)
+    tokens_parts = send_back(tokens_grad, slots, range(groups // 2))
+    both = jnp.concatenate([tokens_grad, output], axis=1)
+    late = send_back(both, slots, range(groups // 2, groups - 2))
+    late += send_back(after(both, first_part), slots, range(groups - 2, groups))
+    tokens_parts += [part[:, :width] for part in late]
+    output_parts = early + [part[:, width:] for part in late]
+    tokens_grad = from_slots(tokens_parts, slots).astype(FULL)
+    output = jnp.transpose(from_slots(output_parts, slots), (1, 0, 2))
     tokens_grad = jnp.transpose(tokens_grad, (1, 0, 2))
 
     mod_row = jnp.concatenate(

time: 918 us -> 969 us (1.056)
  starting transfers between devices: 120 us -> 138 us
  waiting for transfers between devices: 217 us -> 235 us
  other arithmetic: 69.1 us -> 82.4 us
    ppermute x32, waiting for transfers between devices: 60.7 us -> 129 us  [partner(): lax.ppermute(values, axis, [(i, i ^ bit) for i in range(lax.axis_size(axi...]
    reduce_scatter x3, waiting for transfers between devices: 48.1 us -> 10.2 us  [scatter(): return lax.psum_scatter(held, 'tensor', scatter_dimension=0, tiled=True)]
    ppermute x32, starting transfers between devices: 51.8 us -> 75.1 us  [partner(): lax.ppermute(values, axis, [(i, i ^ bit) for i in range(lax.axis_size(axi...]
    ppermute x14 -> x10, waiting for transfers between devices: 57.3 us -> 44.9 us  [send_back(): piece = lax.ppermute(piece, 'tensor', pairs)]
    unnamed x200 -> x205, local copies, waits for them, and re-layouts: 75.2 us -> 67.5 us
  transfers between devices with their start and end apart: 66 -> 62, of which waited for: 24 -> 26; matrix products, arithmetic and copies ran while one was open for 42% -> 39% of each run, Pallas kernels for 16% -> 15%
where the time goes in v3:
time: 969 us; the launch traced here: 951 us
  waiting for transfers between devices  235 us (24%)
  matrix products  199 us (21%)
  Pallas kernels  147 us (15%)
  starting transfers between devices  138 us (14%)
  local copies, waits for them, and re-layouts  133 us (14%)
  other arithmetic  82.4 us (9%)
  between operations  16.6 us (2%)
    dot_general x16, matrix products, dot(): return lax.dot_general(left, right, dims, preferred_element_type=FULL)  199 us
    ppermute x32, waiting for transfers between devices, partner(): lax.ppermute(values, axis, [(i, i ^ bit) for i in range(lax.axis_size(axi...  129 us
    pallas_call x2, Pallas kernels, attend_back(): pl.pallas_call(functools.partial(attend_back_kernel, heads, chunk * colum...  88.1 us
    ppermute x32, starting transfers between devices, partner(): lax.ppermute(values, axis, [(i, i ^ bit) for i in range(lax.axis_size(axi...  75.1 us
    unnamed x205, local copies, waits for them, and re-layouts  67.5 us
    pallas_call x2, Pallas kernels, attend(): pl.pallas_call(functools.partial(attend_kernel, heads, chunk * column(hea...  58.7 us
    ppermute x14, starting transfers between devices, to_slots(): piece = lax.ppermute(piece, 'tensor', pairs)  50.2 us
    ppermute x10, waiting for transfers between devices, send_back(): piece = lax.ppermute(piece, 'tensor', pairs)  44.9 us
  transfers between devices with their start and end apart: 62, of which 26 were waited for; matrix products, arithmetic and copies ran while one was open for 39% of the time, Pallas kernels for 15%

profile of v3, /device:TPU:0, one launch (start us, length us, event | category | flops | bytes accessed | tf_op | source)
XLA Modules:
  0.0 950.7 jit_solution(7548043507944703028)
XLA Ops:
  19.7 7.3 collective-permute-start.4
  34.7 16.1 %collective-permute-done.8 = f32[2,6192]{1,0:T(2,128)S(1)} collective-permute-done((f32[2,6192]{1,0:T(2,128)S(1)}, f32[2,6192]{1,0:T(2,128)S(1)}, u32[]{:S(2)}, u32[]{:S(2)}) %collective-permute-start.8) | collective-permute-done | bytes 49568 | tf_op jit(solution)/shard_map/ppermute | solution.py:165
  55.2 4.8 collective-permute-done.9
  60.7 6.2 collective-permute-start
  83.6 5.5 collective-permute-start.5
  102.2 33.0 %all-gather.4.cloned.1.call-done = bf16[4608,1152]{1,0:T(8,128)(2,1)} async-done(((bf16[144,1152]{1,0:T(8,128)(2,1)}), bf16[4608,1152]{1,0:T(8,128)(2,1)}) %all-gather.4.cloned.1.call-update) | async-done | bytes 10616848 | tf_op jit(solution)/shard_map/all_gather | solution.py:201
  135.2 5.6 copy.44
  145.1 8.0 slice.182
  153.1 15.6 %add_convert_fusion.projected = bf16[1024,3456]{1,0:T(8,128)(2,1)} fusion(bf16[3456,1152]{1,0:T(8,128)(2,1)} %bitcast.201, f32[3456]{0:T(1024)S(1)} %copy-done.59, bf16[1024,1152]{1,0:T(8,128)(2,1)S(1)} %copy-done.11, f32[1152]{0:T(1024)S(1)} %get-tuple-element.46, f32[1152]{0:T(1024)S(1)} %get-tuple-element.47, f32[1024]{0:T(1024)S(1)} %add_rsqrt_fusion.1, ...), kind=kOutput, calls=%fused_computation.13 | convolution fusion | flops 8167882752 | bytes 17431040 | tf_op jit(solution)/shard_map/dot_general | solution.py:22
  171.0 7.4 collective-permute-start.15
  182.5 4.1 collective-permute-start.10
  186.6 29.2 %shard_map.238 = bf16[1024,576]{1,0:T(8,128)(2,1)S(1)} custom-call(bf16[1024,3456]{1,0:T(8,128)(2,1)} %add_convert_fusion.projected), custom_call_target="tpu_custom_call" | custom-call | flops 17179869184 | bytes 4718592 | tf_op jit(solution)/shard_map/pallas_call | solution.py:77
  215.9 29.5 %shard_map.237 = bf16[1024,576]{1,0:T(8,128)(2,1)S(1)} custom-call(bf16[1024,3456]{1,0:T(8,128)(2,1)} %add_convert_fusion.projected), custom_call_target="tpu_custom_call" | custom-call | flops 17179869184 | bytes 4718592 | tf_op jit(solution)/shard_map/pallas_call | solution.py:77
  245.4 5.6 fusion.73
  253.8 21.1 %fusion.69 = f32[1024,4608]{1,0:T(8,128)} fusion(bf16[4608,1152]{1,0:T(8,128)(2,1)} %all-gather.6.cloned.1.call-done, f32[1024,1152]{1,0:T(8,128)} %copy-done.28, f32[1152]{0:T(1024)S(1)} %copy-done.65, f32[1152]{0:T(1024)S(1)} %copy-done.62, f32[1024]{0:T(1024)S(1)} %add_rsqrt_fusion, f32[1024]{0:T(1024)S(1)} %broadcast_multiply_fusion.4), kind=kOutput, calls=%fused_computation.272 | convolution fusion | flops 10877534208 | bytes 34227200 | tf_op jit(solution)/shard_map/dot_general | solution.py:22
  281.0 9.7 %collective-permute-done.12 = bf16[128,1152]{1,0:T(8,128)(2,1)S(1)} collective-permute-done((bf16[128,1152]{1,0:T(8,128)(2,1)S(1)}, bf16[128,1152]{1,0:T(8,128)(2,1)S(1)}, u32[]{:S(2)}, u32[]{:S(2)}) %collective-permute-start.12) | collective-permute-done | bytes 294944 | tf_op jit(solution)/shard_map/ppermute | solution.py:245
  290.8 5.9 collective-permute-done.13
  302.6 23.0 %convolution_convert_fusion.1 = bf16[4608,1152]{1,0:T(8,128)(2,1)} fusion(bf16[1024,1152]{1,0:T(8,128)(2,1)S(1)} %get-tuple-element.25, f32[1024,4608]{1,0:T(8,128)} %fusion.69, f32[4608]{0:T(1024)S(1)} %copy-done.58), kind=kOutput, calls=%fused_computation.3 | convolution fusion | flops 10924130304 | bytes 31868928 | tf_op jit(solution)/shard_map/dot_general | solution.py:22
  325.6 5.5 constant_dynamic-slice_fusion.6
  331.1 9.1 collective-permute-done.17
  340.2 5.8 add_convert_fusion.2
  351.6 28.9 %fusion.6 = bf16[1024,4608]{1,0:T(8,128)(2,1)} fusion(f32[1024,4608]{1,0:T(8,128)} %fusion.69, f32[4608]{0:T(1024)S(1)} %copy-done.58, bf16[1024,1152]{1,0:T(8,128)(2,1)} %copy-done.34, bf16[4608,1152]{1,0:T(8,128)(2,1)} %all-gather.8.cloned.1.call-done), kind=kOutput, calls=%fused_computation.10 | convolution fusion | flops 10970726400 | bytes 41306112 | tf_op jit(solution)/shard_map/dot_general | solution.py:22
  380.5 17.1 %convolution_convert_fusion = bf16[4608,1152]{1,0:T(8,128)(2,1)S(1)} fusion(bf16[1024,4608]{1,0:T(8,128)(2,1)} %fusion.6, f32[1024,1152]{1,0:T(8,128)} %copy-done.28, f32[1152]{0:T(1024)S(1)} %copy-done.65, f32[1152]{0:T(1024)S(1)} %copy-done.62, f32[1024]{0:T(1024)S(1)} %add_rsqrt_fusion, f32[1024]{0:T(1024)S(1)} %broadcast_multiply_fusion.4), kind=kOutput, calls=%fused_computation.2 | convolution fusion | flops 10882842624 | bytes 24790016 | tf_op jit(solution)/shard_map/dot_general | solution.py:22
  404.7 5.2 collective-permute-done.18
  413.9 21.9 %multiply_reduce_fusion.1 = (bf16[1152]{0:T(1024)(128)(2,1)}, f32[1024]{0:T(1024)S(1)}, f32[1024]{0:T(1024)S(1)}, bf16[1152]{0:T(1024)(128)(2,1)}, f32[1024,1152]{1,0:T(8,128)}) fusion(f32[1024,1152]{1,0:T(8,128)} %copy-done.28, f32[1024]{0:T(1024)S(1)} %add_rsqrt_fusion, f32[1024]{0:T(1024)S(1)} %broadcast_multiply_fusion.4, f32[1152]{0:T(1024)S(1)} %copy-done.62, ...), kind=kOutput, calls=%fused_computation.60 | convolution fusion | flops 10882248704 | bytes 29516800 | tf_op jit(solution)/shard_map/dot_general | solution.py:22
  435.9 25.9 %multiply_reduce_fusion = (bf16[1152]{0:T(1024)(128)(2,1)}, bf16[1024,1152]{1,0:T(8,128)(2,1)}, f32[1152]{0:T(1024)S(1)}, bf16[1024,1152]{1,0:T(8,128)(2,1)S(1)}, f32[1024,1152]{1,0:T(8,128)}) fusion(bf16[1024,1152]{1,0:T(8,128)(2,1)S(1)} %copy-done.31, f32[]{:T(128)S(6)} %convert_element_type.198, f32[1024,1152]{1,0:T(8,128)} %copy-done.28, ...), kind=kOutput, calls=%fused_computation.59 | convolution fusion | flops 10943592448 | bytes 50785028 | tf_op jit(solution)/shard_map/dot_general | solution.py:22
  468.0 4.8 convolution_convert_fusion.5.attended_grad
  472.8 5.4 add_convert_fusion.1
  483.8 10.0 %reduce-scatter.4.cloned.1.call-done = bf16[144,1152]{1,0:T(8,128)(2,1)} async-done(((bf16[1152,1152]{1,0:T(8,128)(2,1)}), bf16[144,1152]{1,0:T(8,128)(2,1)}) %reduce-scatter.4.cloned.1.call-update) | async-done | bytes 331792 | tf_op jit(solution)/shard_map/reduce_scatter | solution.py:219
  495.4 44.2 %shard_map.239 = bf16[1024,1728]{1,0:T(8,128)(2,1)S(1)} custom-call(bf16[1024,3456]{1,0:T(8,128)(2,1)} %add_convert_fusion.projected, bf16[1024,1152]{1,0:T(8,128)(2,1)S(1)} %copy-done.4), custom_call_target="tpu_custom_call" | custom-call | flops 34359738368 | bytes 8257536 | tf_op jit(solution)/shard_map/pallas_call | solution.py:138
  539.7 5.9 convolution_convert_fusion.3
  550.0 5.2 convert_reduce_fusion
  570.1 8.1 collective-permute-done.21
  578.1 43.9 %shard_map.240 = bf16[1024,1728]{1,0:T(8,128)(2,1)S(1)} custom-call(bf16[1024,3456]{1,0:T(8,128)(2,1)} %add_convert_fusion.projected, bf16[1024,1152]{1,0:T(8,128)(2,1)S(1)} %copy-done.5), custom_call_target="tpu_custom_call" | custom-call | flops 34359738368 | bytes 8257536 | tf_op jit(solution)/shard_map/pallas_call | solution.py:138
  622.1 6.1 convolution_convert_fusion.2
  635.9 5.3 collective-permute-done.54
  647.4 12.6 %collective-permute-start.47 = (f32[10368]{0:T(1024)S(1)}, f32[10368]{0:T(1024)S(1)}, u32[]{:S(2)}, u32[]{:S(2)}) collective-permute-start(f32[10368]{0:T(1024)S(1)} %concatenate.108), channel_id=1, source_target_pairs={{0,1},{1,0},{2,3},{3,2},{4,5},{5,4},{6,7},{7,6},{8,9},{9,8},{10,11... | collective-permute-start | bytes 124424 | tf_op jit(solution)/shard_map/ppermute | solution.py:165
  662.1 18.7 %collective-permute-start.48 = (f32[10368]{0:T(1024)S(1)}, f32[10368]{0:T(1024)S(1)}, u32[]{:S(2)}, u32[]{:S(2)}) collective-permute-start(f32[10368]{0:T(1024)S(1)} %add.353), channel_id=1, source_target_pairs={{0,2},{1,3},{2,0},{3,1},{4,6},{5,7},{6,4},{7,5},{8,10},{9,11},{10,... | collective-permute-start | bytes 124424 | tf_op jit(solution)/shard_map/ppermute | solution.py:165
  689.1 15.9 %fusion.7 = f32[1024,1152]{1,0:T(8,128)} fusion(bf16[3456,1152]{1,0:T(8,128)(2,1)} %bitcast.202, bf16[1024,1728]{1,0:T(8,128)(2,1)} %copy-done.3, bf16[1024,1728]{1,0:T(8,128)(2,1)} %copy-done.1), kind=kOutput, calls=%fused_computation.22 | convolution fusion | flops 8167882752 | bytes 19759104 | tf_op jit(solution)/shard_map/dot_general | solution.py:22
  714.8 24.9 %collective-permute-done.27 = bf16[8,72,1152]{2,1,0:T(8,128)(2,1)} collective-permute-done((bf16[8,72,1152]{2,1,0:T(8,128)(2,1)}, bf16[8,72,1152]{2,1,0:T(8,128)(2,1)}, u32[]{:S(2)}, u32[]{:S(2)}) %collective-permute-start.27) | collective-permute-done | bytes 1327136 | tf_op jit(solution)/shard_map/ppermute | solution.py:165
  746.0 8.5 multiply_reduce_fusion.2
  763.4 18.7 %collective-permute-start.36 = (bf16[2,8,864]{2,1,0:T(8,128)(2,1)S(1)}, bf16[2,8,864]{2,1,0:T(8,128)(2,1)S(1)}, u32[]{:S(2)}, u32[]{:S(2)}) collective-permute-start(bf16[2,8,864]{2,1,0:T(8,128)(2,1)S(1)} %pad_maximum_fusion.13), channel_id=1, source_target_pairs={{0,2},{1,3},{2,0},{3,1},{4,6},{5,7},{6,4},{7,5},{8,10},{9,11},{10,... | collective-permute-start | bytes 82952 | tf_op jit(solution)/shard_map/ppermute | solution.py:165
  790.2 12.8 %collective-permute-done.37 = bf16[4,8,864]{2,1,0:T(8,128)(2,1)S(1)} collective-permute-done((bf16[4,8,864]{2,1,0:T(8,128)(2,1)S(1)}, bf16[4,8,864]{2,1,0:T(8,128)(2,1)S(1)}, u32[]{:S(2)}, u32[]{:S(2)}) %collective-permute-start.37) | collective-permute-done | bytes 55328 | tf_op jit(solution)/shard_map/ppermute | solution.py:165
  814.8 4.4 collective-permute-start.40
  819.2 32.5 %collective-permute-done.40 = f32[6,1152]{1,0:T(8,128)S(1)} collective-permute-done((f32[6,1152]{1,0:T(8,128)S(1)}, f32[6,1152]{1,0:T(8,128)S(1)}, u32[]{:S(2)}, u32[]{:S(2)}) %collective-permute-start.40) | collective-permute-done | bytes 27680 | tf_op jit(solution)/shard_map/ppermute | solution.py:165
  867.8 26.1 %collective-permute-done.28 = bf16[128,2304]{1,0:T(8,128)(2,1)S(1)} collective-permute-done((bf16[128,2304]{1,0:T(8,128)(2,1)S(1)}, bf16[128,2304]{1,0:T(8,128)(2,1)S(1)}, u32[]{:S(2)}, u32[]{:S(2)}) %collective-permute-start.28) | collective-permute-done | bytes 589856 | tf_op jit(solution)/shard_map/ppermute | solution.py:260
  899.5 6.0 collective-permute-done.45
  906.6 10.0 %collective-permute-done.30 = bf16[128,2304]{1,0:T(8,128)(2,1)S(1)} collective-permute-done((bf16[128,2304]{1,0:T(8,128)(2,1)S(1)}, bf16[128,2304]{1,0:T(8,128)(2,1)S(1)}, u32[]{:S(2)}, u32[]{:S(2)}) %collective-permute-start.30) | collective-permute-done | bytes 589856 | tf_op jit(solution)/shard_map/ppermute | solution.py:260
  (443 shorter events, 247.1 us)
Async XLA Ops:
  7.2 127.9 %all-gather.4.cloned.1.call-start = ((), (), s32[]{:S(2)}) async-start(), calls=%async_computation.3 | async-start | bytes 10948608 | tf_op jit(solution)/shard_map/all_gather | solution.py:201
  9.8 244.0 %all-gather.6.cloned.1.call-start = ((), (), s32[]{:S(2)}) async-start(), calls=%async_computation.4 | async-start | bytes 10948608 | tf_op jit(solution)/shard_map/all_gather | solution.py:201
  11.6 340.0 %all-gather.8.cloned.1.call-start = ((), (), s32[]{:S(2)}) async-start(), calls=%async_computation.5 | async-start | bytes 10948608 | tf_op jit(solution)/shard_map/all_gather | solution.py:201
  12.8 19.8 %collective-permute-start.7 = (f32[1,6192]{1,0:T(1,128)S(1)}, f32[1,6192]{1,0:T(1,128)S(1)}, u32[]{:S(2)}, u32[]{:S(2)}) collective-permute-start(f32[1,6192]{1,0:T(1,128)S(1)} %broadcast_in_dim.6), channel_id=1, source_target_pairs={{0,1},{1,0},{2,3},{3,2},{4,5},{5,4},{6,7},{7,6},{8,9},{9,8},{10,11... | collective-permute-start | bytes 74312 | tf_op jit(solution)/shard_map/ppermute | solution.py:165
  18.3 77.3 %collective-permute-start.6 = (bf16[128,1152]{1,0:T(8,128)(2,1)S(1)}, bf16[128,1152]{1,0:T(8,128)(2,1)}, u32[]{:S(2)}, u32[]{:S(2)}) collective-permute-start(bf16[128,1152]{1,0:T(8,128)(2,1)S(1)} %get-tuple-element.84), channel_id=1, source_target_pairs={{2,1},{3,2},{4,3},{5,4},{6,5},{7,6},{10,9},{11,10},{12,11},{13,12}... | collective-permute-start | bytes 884744 | tf_op jit(solution)/shard_map/ppermute | solution.py:245
  19.7 73.5 %collective-permute-start.4 = (bf16[128,1152]{1,0:T(8,128)(2,1)S(1)}, bf16[128,1152]{1,0:T(8,128)(2,1)}, u32[]{:S(2)}, u32[]{:S(2)}) collective-permute-start(bf16[128,1152]{1,0:T(8,128)(2,1)S(1)} %get-tuple-element.85), channel_id=1, source_target_pairs={{0,5},{1,6},{4,1},{5,2},{6,3},{7,4},{8,13},{9,14},{12,9},{13,10},{... | collective-permute-start | bytes 884744 | tf_op jit(solution)/shard_map/ppermute | solution.py:245
  27.0 64.5 %collective-permute-start.3 = (bf16[128,1152]{1,0:T(8,128)(2,1)S(1)}, bf16[128,1152]{1,0:T(8,128)(2,1)}, u32[]{:S(2)}, u32[]{:S(2)}) collective-permute-start(bf16[128,1152]{1,0:T(8,128)(2,1)S(1)} %get-tuple-element.86), channel_id=1, source_target_pairs={{0,4},{1,5},{2,6},{5,1},{6,2},{7,3},{8,12},{9,13},{10,14},{13,9},{... | collective-permute-start | bytes 884744 | tf_op jit(solution)/shard_map/ppermute | solution.py:245
  29.0 54.6 %collective-permute-start.1 = (bf16[128,1152]{1,0:T(8,128)(2,1)}, bf16[128,1152]{1,0:T(8,128)(2,1)}, u32[]{:S(2)}, u32[]{:S(2)}) collective-permute-start(bf16[128,1152]{1,0:T(8,128)(2,1)} %get-tuple-element.88), channel_id=1, source_target_pairs={{0,2},{1,3},{2,4},{3,5},{4,6},{7,1},{8,10},{9,11},{10,12},{11,13},... | collective-permute-start | bytes 884744 | tf_op jit(solution)/shard_map/ppermute | solution.py:245
  32.8 18.0 %collective-permute-start.8 = (f32[2,6192]{1,0:T(2,128)S(1)}, f32[2,6192]{1,0:T(2,128)S(1)}, u32[]{:S(2)}, u32[]{:S(2)}) collective-permute-start(f32[2,6192]{1,0:T(2,128)S(1)} %pad_maximum_fusion.10), channel_id=1, source_target_pairs={{0,2},{1,3},{2,0},{3,1},{4,6},{5,7},{6,4},{7,5},{8,10},{9,11},{10,... | collective-permute-start | bytes 148616 | tf_op jit(solution)/shard_map/ppermute | solution.py:165
  34.6 459.2 %reduce-scatter.4.cloned.1.call-start = ((), (), s32[]{:S(2)}) async-start(), calls=%async_computation.6 | async-start | bytes 2985984 | tf_op jit(solution)/shard_map/reduce_scatter | solution.py:219
  60.7 17.1 %collective-permute-start = (bf16[128,1152]{1,0:T(8,128)(2,1)}, bf16[128,1152]{1,0:T(8,128)(2,1)}, u32[]{:S(2)}, u32[]{:S(2)}) collective-permute-start(bf16[128,1152]{1,0:T(8,128)(2,1)} %get-tuple-element.89), channel_id=1, source_target_pairs={{0,1},{1,2},{2,3},{3,4},{4,5},{5,6},{8,9},{9,10},{10,11},{11,12},{... | collective-permute-start | bytes 884744 | tf_op jit(solution)/shard_map/ppermute | solution.py:245
  77.8 13.0 %collective-permute-start.2 = (bf16[128,1152]{1,0:T(8,128)(2,1)}, bf16[128,1152]{1,0:T(8,128)(2,1)S(1)}, u32[]{:S(2)}, u32[]{:S(2)}) collective-permute-start(bf16[128,1152]{1,0:T(8,128)(2,1)} %get-tuple-element.87), channel_id=1, source_target_pairs={{0,3},{1,4},{2,5},{3,6},{6,1},{7,2},{8,11},{9,12},{10,13},{11,14},... | collective-permute-start | bytes 884744 | tf_op jit(solution)/shard_map/ppermute | solution.py:245
  83.6 11.3 %collective-permute-start.5 = (bf16[128,1152]{1,0:T(8,128)(2,1)S(1)}, bf16[128,1152]{1,0:T(8,128)(2,1)S(1)}, u32[]{:S(2)}, u32[]{:S(2)}) collective-permute-start(bf16[128,1152]{1,0:T(8,128)(2,1)S(1)} %get-tuple-element.90), channel_id=1, source_target_pairs={{0,6},{3,1},{4,2},{5,3},{6,4},{7,5},{8,14},{11,9},{12,10},{13,11},... | collective-permute-start | bytes 884744 | tf_op jit(solution)/shard_map/ppermute | solution.py:245
  169.7 129.1 %collective-permute-start.16 = (bf16[128,1152]{1,0:T(8,128)(2,1)S(1)}, bf16[128,1152]{1,0:T(8,128)(2,1)}, u32[]{:S(2)}, u32[]{:S(2)}) collective-permute-start(bf16[128,1152]{1,0:T(8,128)(2,1)S(1)} %get-tuple-element.77), channel_id=1, source_target_pairs={{2,1},{3,2},{4,3},{5,4},{6,5},{7,6},{10,9},{11,10},{12,11},{13,12}... | collective-permute-start | bytes 884744 | tf_op jit(solution)/shard_map/ppermute | solution.py:245
  171.0 126.8 %collective-permute-start.15 = (bf16[128,1152]{1,0:T(8,128)(2,1)S(1)}, bf16[128,1152]{1,0:T(8,128)(2,1)}, u32[]{:S(2)}, u32[]{:S(2)}) collective-permute-start(bf16[128,1152]{1,0:T(8,128)(2,1)S(1)} %get-tuple-element.78), channel_id=1, source_target_pairs={{0,6},{3,1},{4,2},{5,3},{6,4},{7,5},{8,14},{11,9},{12,10},{13,11},... | collective-permute-start | bytes 884744 | tf_op jit(solution)/shard_map/ppermute | solution.py:245
  178.4 118.4 %collective-permute-start.14 = (bf16[128,1152]{1,0:T(8,128)(2,1)S(1)}, bf16[128,1152]{1,0:T(8,128)(2,1)}, u32[]{:S(2)}, u32[]{:S(2)}) collective-permute-start(bf16[128,1152]{1,0:T(8,128)(2,1)S(1)} %get-tuple-element.79), channel_id=1, source_target_pairs={{0,5},{1,6},{4,1},{5,2},{6,3},{7,4},{8,13},{9,14},{12,9},{13,10},{... | collective-permute-start | bytes 884744 | tf_op jit(solution)/shard_map/ppermute | solution.py:245
  180.4 98.3 %collective-permute-start.11 = (bf16[128,1152]{1,0:T(8,128)(2,1)}, bf16[128,1152]{1,0:T(8,128)(2,1)}, u32[]{:S(2)}, u32[]{:S(2)}) collective-permute-start(bf16[128,1152]{1,0:T(8,128)(2,1)} %get-tuple-element.82), channel_id=1, source_target_pairs={{0,2},{1,3},{2,4},{3,5},{4,6},{7,1},{8,10},{9,11},{10,12},{11,13},... | collective-permute-start | bytes 884744 | tf_op jit(solution)/shard_map/ppermute | solution.py:245
  182.5 93.4 %collective-permute-start.10 = (bf16[128,1152]{1,0:T(8,128)(2,1)}, bf16[128,1152]{1,0:T(8,128)(2,1)}, u32[]{:S(2)}, u32[]{:S(2)}) collective-permute-start(bf16[128,1152]{1,0:T(8,128)(2,1)} %get-tuple-element.83), channel_id=1, source_target_pairs={{0,1},{1,2},{2,3},{3,4},{4,5},{5,6},{8,9},{9,10},{10,11},{11,12},{... | collective-permute-start | bytes 884744 | tf_op jit(solution)/shard_map/ppermute | solution.py:245
  275.9 14.9 %collective-permute-start.12 = (bf16[128,1152]{1,0:T(8,128)(2,1)S(1)}, bf16[128,1152]{1,0:T(8,128)(2,1)S(1)}, u32[]{:S(2)}, u32[]{:S(2)}) collective-permute-start(bf16[128,1152]{1,0:T(8,128)(2,1)S(1)} %copy-done.43), channel_id=1, source_target_pairs={{0,3},{1,4},{2,5},{3,6},{6,1},{7,2},{8,11},{9,12},{10,13},{11,14},... | collective-permute-start | bytes 884744 | tf_op jit(solution)/shard_map/ppermute | solution.py:245
  278.7 18.0 %collective-permute-start.13 = (bf16[128,1152]{1,0:T(8,128)(2,1)S(1)}, bf16[128,1152]{1,0:T(8,128)(2,1)S(1)}, u32[]{:S(2)}, u32[]{:S(2)}) collective-permute-start(bf16[128,1152]{1,0:T(8,128)(2,1)S(1)} %get-tuple-element.80), channel_id=1, source_target_pairs={{0,4},{1,5},{2,6},{5,1},{6,2},{7,3},{8,12},{9,13},{10,14},{13,9},{... | collective-permute-start | bytes 884744 | tf_op jit(solution)/shard_map/ppermute | solution.py:245
  350.0 59.8 %collective-permute-start.18 = (bf16[8,144,1152]{2,1,0:T(8,128)(2,1)}, bf16[8,144,1152]{2,1,0:T(8,128)(2,1)}, u32[]{:S(2)}, u32[]{:S(2)}) collective-permute-start(bf16[8,144,1152]{2,1,0:T(8,128)(2,1)} %constant_dynamic-slice_fusion.5), channel_id=1, source_target_pairs={{0,16},{8,24},{16,0},{24,8},{1,17},{9,25},{17,1},{25,9},{2,18},{10... | collective-permute-start | bytes 7962632 | tf_op jit(solution)/shard_map/ppermute | solution.py:165
  404.6 68.2 %collective-permute-start.19 = (bf16[8,288,1152]{2,1,0:T(8,128)(2,1)}, bf16[8,288,1152]{2,1,0:T(8,128)(2,1)}, u32[]{:S(2)}, u32[]{:S(2)}) collective-permute-start(bf16[8,288,1152]{2,1,0:T(8,128)(2,1)} %constant_dynamic-slice_fusion.4), channel_id=1, source_target_pairs={{0,8},{8,0},{16,24},{24,16},{1,9},{9,1},{17,25},{25,17},{2,10},{10... | collective-permute-start | bytes 15925256 | tf_op jit(solution)/shard_map/ppermute | solution.py:165
  413.8 273.4 %reduce-scatter.6.cloned.1.call-start = ((), (), s32[]{:S(2)}) async-start(), calls=%async_computation.7 | async-start | bytes 2985984 | tf_op jit(solution)/shard_map/reduce_scatter | solution.py:219
  482.3 79.0 %collective-permute-start.24 = (bf16[8,144,1152]{2,1,0:T(8,128)(2,1)}, bf16[8,144,1152]{2,1,0:T(8,128)(2,1)}, u32[]{:S(2)}, u32[]{:S(2)}) collective-permute-start(bf16[8,144,1152]{2,1,0:T(8,128)(2,1)} %constant_dynamic-slice_fusion.3), channel_id=1, source_target_pairs={{0,16},{8,24},{16,0},{24,8},{1,17},{9,25},{17,1},{25,9},{2,18},{10... | collective-permute-start | bytes 7962632 | tf_op jit(solution)/shard_map/ppermute | solution.py:165
  550.0 15.4 %collective-permute-start.23 = (bf16[8,144,1152]{2,1,0:T(8,128)(2,1)}, bf16[8,144,1152]{2,1,0:T(8,128)(2,1)}, u32[]{:S(2)}, u32[]{:S(2)}) collective-permute-start(bf16[8,144,1152]{2,1,0:T(8,128)(2,1)} %fusion.28), channel_id=1, source_target_pairs={{0,8},{8,0},{16,24},{24,16},{1,9},{9,1},{17,25},{25,17},{2,10},{10... | collective-permute-start | bytes 7962632 | tf_op jit(solution)/shard_map/ppermute | solution.py:165
  557.3 12.8 %collective-permute-start.22 = (bf16[128,1152]{1,0:T(8,128)(2,1)}, bf16[128,1152]{1,0:T(8,128)(2,1)S(1)}, u32[]{:S(2)}, u32[]{:S(2)}) collective-permute-start(bf16[128,1152]{1,0:T(8,128)(2,1)} %get-tuple-element.74), channel_id=1, source_target_pairs={{3,0},{4,1},{5,2},{6,3},{1,6},{2,7},{11,8},{12,9},{13,10},{14,11},... | collective-permute-start | bytes 884744 | tf_op jit(solution)/shard_map/ppermute | solution.py:260
  558.6 19.6 %collective-permute-start.21 = (bf16[128,1152]{1,0:T(8,128)(2,1)}, bf16[128,1152]{1,0:T(8,128)(2,1)}, u32[]{:S(2)}, u32[]{:S(2)}) collective-permute-start(bf16[128,1152]{1,0:T(8,128)(2,1)} %get-tuple-element.75), channel_id=1, source_target_pairs={{2,0},{3,1},{4,2},{5,3},{6,4},{1,7},{10,8},{11,9},{12,10},{13,11},... | collective-permute-start | bytes 884744 | tf_op jit(solution)/shard_map/ppermute | solution.py:260
  560.0 18.1 %collective-permute-start.20 = (bf16[128,1152]{1,0:T(8,128)(2,1)}, bf16[128,1152]{1,0:T(8,128)(2,1)}, u32[]{:S(2)}, u32[]{:S(2)}) collective-permute-start(bf16[128,1152]{1,0:T(8,128)(2,1)} %get-tuple-element.76), channel_id=1, source_target_pairs={{1,0},{2,1},{3,2},{4,3},{5,4},{6,5},{9,8},{10,9},{11,10},{12,11},{... | collective-permute-start | bytes 884744 | tf_op jit(solution)/shard_map/ppermute | solution.py:260
  565.4 330.3 %reduce-scatter.8.cloned.1.call-start = ((), (), s32[]{:S(2)}) async-start(), calls=%async_computation.8 | async-start | bytes 2985984 | tf_op jit(solution)/shard_map/reduce_scatter | solution.py:219
  629.2 14.1 %collective-permute-start.25 = (bf16[8,144,1152]{2,1,0:T(8,128)(2,1)S(1)}, bf16[8,144,1152]{2,1,0:T(8,128)(2,1)S(1)}, u32[]{:S(2)}, u32[]{:S(2)}) collective-permute-start(bf16[8,144,1152]{2,1,0:T(8,128)(2,1)S(1)} %fusion.26), channel_id=1, source_target_pairs={{0,8},{8,0},{16,24},{24,16},{1,9},{9,1},{17,25},{25,17},{2,10},{10... | collective-permute-start | bytes 7962632 | tf_op jit(solution)/shard_map/ppermute | solution.py:165
  641.3 18.8 %collective-permute-start.55 = (bf16[288,1152]{1,0:T(8,128)(2,1)S(1)}, bf16[288,1152]{1,0:T(8,128)(2,1)}, u32[]{:S(2)}, u32[]{:S(2)}) collective-permute-start(bf16[288,1152]{1,0:T(8,128)(2,1)S(1)} %pad_maximum_fusion.6), channel_id=1, source_target_pairs={{0,8},{8,0},{16,24},{24,16},{1,9},{9,1},{17,25},{25,17},{2,10},{10... | collective-permute-start | bytes 1990664 | tf_op jit(solution)/shard_map/ppermute | solution.py:165
  642.6 42.0 %collective-permute-start.26 = (bf16[8,72,1152]{2,1,0:T(8,128)(2,1)}, bf16[8,72,1152]{2,1,0:T(8,128)(2,1)}, u32[]{:S(2)}, u32[]{:S(2)}) collective-permute-start(bf16[8,72,1152]{2,1,0:T(8,128)(2,1)} %constant_dynamic-slice_fusion.2), channel_id=1, source_target_pairs={{0,16},{8,24},{16,0},{24,8},{1,17},{9,25},{17,1},{25,9},{2,18},{10... | collective-permute-start | bytes 3981320 | tf_op jit(solution)/shard_map/ppermute | solution.py:165
  647.4 14.7 %collective-permute-start.47 = (f32[10368]{0:T(1024)S(1)}, f32[10368]{0:T(1024)S(1)}, u32[]{:S(2)}, u32[]{:S(2)}) collective-permute-start(f32[10368]{0:T(1024)S(1)} %concatenate.108), channel_id=1, source_target_pairs={{0,1},{1,0},{2,3},{3,2},{4,5},{5,4},{6,7},{7,6},{8,9},{9,8},{10,11... | collective-permute-start | bytes 124424 | tf_op jit(solution)/shard_map/ppermute | solution.py:165
  662.1 20.7 %collective-permute-start.48 = (f32[10368]{0:T(1024)S(1)}, f32[10368]{0:T(1024)S(1)}, u32[]{:S(2)}, u32[]{:S(2)}) collective-permute-start(f32[10368]{0:T(1024)S(1)} %add.353), channel_id=1, source_target_pairs={{0,2},{1,3},{2,0},{3,1},{4,6},{5,7},{6,4},{7,5},{8,10},{9,11},{10,... | collective-permute-start | bytes 124424 | tf_op jit(solution)/shard_map/ppermute | solution.py:165
  687.2 18.5 %collective-permute-start.52 = (bf16[144,1152]{1,0:T(8,128)(2,1)}, bf16[144,1152]{1,0:T(8,128)(2,1)S(1)}, u32[]{:S(2)}, u32[]{:S(2)}) collective-permute-start(bf16[144,1152]{1,0:T(8,128)(2,1)} %reduce-scatter.6.cloned.1.call-done), channel_id=1, source_target_pairs={{0,16},{8,24},{16,0},{24,8},{1,17},{9,25},{17,1},{25,9},{2,18},{10... | collective-permute-start | bytes 995336 | tf_op jit(solution)/shard_map/ppermute | solution.py:165
  689.0 16.0 %collective-permute-start.50 = (f32[10368]{0:T(1024)S(1)}, f32[10368]{0:T(1024)S(1)}, u32[]{:S(2)}, u32[]{:S(2)}) collective-permute-start(f32[10368]{0:T(1024)S(1)} %add.355), channel_id=1, source_target_pairs={{0,8},{8,0},{16,24},{24,16},{1,9},{9,1},{17,25},{25,17},{2,10},{10... | collective-permute-start | bytes 124424 | tf_op jit(solution)/shard_map/ppermute | solution.py:165
  707.9 31.8 %collective-permute-start.27 = (bf16[8,72,1152]{2,1,0:T(8,128)(2,1)}, bf16[8,72,1152]{2,1,0:T(8,128)(2,1)}, u32[]{:S(2)}, u32[]{:S(2)}) collective-permute-start(bf16[8,72,1152]{2,1,0:T(8,128)(2,1)} %constant_dynamic-slice_fusion.1), channel_id=1, source_target_pairs={{0,16},{8,24},{16,0},{24,8},{1,17},{9,25},{17,1},{25,9},{2,18},{10... | collective-permute-start | bytes 3981320 | tf_op jit(solution)/shard_map/ppermute | solution.py:165
  763.4 21.7 %collective-permute-start.36 = (bf16[2,8,864]{2,1,0:T(8,128)(2,1)S(1)}, bf16[2,8,864]{2,1,0:T(8,128)(2,1)S(1)}, u32[]{:S(2)}, u32[]{:S(2)}) collective-permute-start(bf16[2,8,864]{2,1,0:T(8,128)(2,1)S(1)} %pad_maximum_fusion.13), channel_id=1, source_target_pairs={{0,2},{1,3},{2,0},{3,1},{4,6},{5,7},{6,4},{7,5},{8,10},{9,11},{10,... | collective-permute-start | bytes 82952 | tf_op jit(solution)/shard_map/ppermute | solution.py:165
  783.7 81.7 %collective-permute-start.32 = (bf16[128,1152]{1,0:T(8,128)(2,1)}, bf16[128,1152]{1,0:T(8,128)(2,1)S(1)}, u32[]{:S(2)}, u32[]{:S(2)}) collective-permute-start(bf16[128,1152]{1,0:T(8,128)(2,1)} %get-tuple-element.73), channel_id=1, source_target_pairs={{1,0},{2,1},{3,2},{4,3},{5,4},{6,5},{9,8},{10,9},{11,10},{12,11},{... | collective-permute-start | bytes 884744 | tf_op jit(solution)/shard_map/ppermute | solution.py:260
  785.2 17.9 %collective-permute-start.37 = (bf16[4,8,864]{2,1,0:T(8,128)(2,1)S(1)}, bf16[4,8,864]{2,1,0:T(8,128)(2,1)S(1)}, u32[]{:S(2)}, u32[]{:S(2)}) collective-permute-start(bf16[4,8,864]{2,1,0:T(8,128)(2,1)S(1)} %pad_maximum_fusion.8), channel_id=1, source_target_pairs={{0,4},{1,5},{2,6},{3,7},{4,0},{5,1},{6,2},{7,3},{8,12},{9,13},{10,... | collective-permute-start | bytes 165896 | tf_op jit(solution)/shard_map/ppermute | solution.py:165
  809.9 57.1 %collective-permute-start.34 = (bf16[128,1152]{1,0:T(8,128)(2,1)S(1)}, bf16[128,1152]{1,0:T(8,128)(2,1)S(1)}, u32[]{:S(2)}, u32[]{:S(2)}) collective-permute-start(bf16[128,1152]{1,0:T(8,128)(2,1)S(1)} %copy-done.44), channel_id=1, source_target_pairs={{3,0},{4,1},{5,2},{6,3},{1,6},{2,7},{11,8},{12,9},{13,10},{14,11},... | collective-permute-start | bytes 884744 | tf_op jit(solution)/shard_map/ppermute | solution.py:260
  811.2 55.0 %collective-permute-start.33 = (bf16[128,1152]{1,0:T(8,128)(2,1)S(1)}, bf16[128,1152]{1,0:T(8,128)(2,1)S(1)}, u32[]{:S(2)}, u32[]{:S(2)}) collective-permute-start(bf16[128,1152]{1,0:T(8,128)(2,1)S(1)} %copy-done.45), channel_id=1, source_target_pairs={{2,0},{3,1},{4,2},{5,3},{6,4},{1,7},{10,8},{11,9},{12,10},{13,11},... | collective-permute-start | bytes 884744 | tf_op jit(solution)/shard_map/ppermute | solution.py:260
  813.5 81.2 %collective-permute-start.29 = (bf16[128,2304]{1,0:T(8,128)(2,1)S(1)}, bf16[128,2304]{1,0:T(8,128)(2,1)S(1)}, u32[]{:S(2)}, u32[]{:S(2)}) collective-permute-start(bf16[128,2304]{1,0:T(8,128)(2,1)S(1)} %get-tuple-element.67), channel_id=1, source_target_pairs={{5,0},{6,1},{1,4},{2,5},{3,6},{4,7},{13,8},{14,9},{9,12},{10,13},{... | collective-permute-start | bytes 1769480 | tf_op jit(solution)/shard_map/ppermute | solution.py:260
  814.8 37.0 %collective-permute-start.40 = (f32[6,1152]{1,0:T(8,128)S(1)}, f32[6,1152]{1,0:T(8,128)S(1)}, u32[]{:S(2)}, u32[]{:S(2)}) collective-permute-start(f32[6,1152]{1,0:T(8,128)S(1)} %add.351), channel_id=1, source_target_pairs={{0,4},{1,5},{2,6},{3,7},{4,0},{5,1},{6,2},{7,3},{8,12},{9,13},{10,... | collective-permute-start | bytes 82952 | tf_op jit(solution)/shard_map/ppermute | solution.py:165
  861.5 32.4 %collective-permute-start.28 = (bf16[128,2304]{1,0:T(8,128)(2,1)S(1)}, bf16[128,2304]{1,0:T(8,128)(2,1)S(1)}, u32[]{:S(2)}, u32[]{:S(2)}) collective-permute-start(bf16[128,2304]{1,0:T(8,128)(2,1)S(1)} %get-tuple-element.68), channel_id=1, source_target_pairs={{4,0},{5,1},{6,2},{1,5},{2,6},{3,7},{12,8},{13,9},{14,10},{9,13},{... | collective-permute-start | bytes 1769480 | tf_op jit(solution)/shard_map/ppermute | solution.py:260
  897.5 19.9 %collective-permute-start.31 = (bf16[128,2304]{1,0:T(8,128)(2,1)S(1)}, bf16[128,2304]{1,0:T(8,128)(2,1)S(1)}, u32[]{:S(2)}, u32[]{:S(2)}) collective-permute-start(bf16[128,2304]{1,0:T(8,128)(2,1)S(1)} %get-tuple-element.65), channel_id=1, source_target_pairs={{1,2},{2,3},{3,4},{4,5},{5,6},{6,7},{9,10},{10,11},{11,12},{12,13}... | collective-permute-start | bytes 1769480 | tf_op jit(solution)/shard_map/ppermute | solution.py:260
  898.2 18.4 %collective-permute-start.30 = (bf16[128,2304]{1,0:T(8,128)(2,1)S(1)}, bf16[128,2304]{1,0:T(8,128)(2,1)S(1)}, u32[]{:S(2)}, u32[]{:S(2)}) collective-permute-start(bf16[128,2304]{1,0:T(8,128)(2,1)S(1)} %get-tuple-element.66), channel_id=1, source_target_pairs={{6,0},{1,3},{2,4},{3,5},{4,6},{5,7},{14,8},{9,11},{10,12},{11,13},... | collective-permute-start | bytes 1769480 | tf_op jit(solution)/shard_map/ppermute | solution.py:260
  906.6 34.1 %collective-permute-start.46 = (bf16[288,1152]{1,0:T(8,128)(2,1)S(1)}, bf16[288,1152]{1,0:T(8,128)(2,1)S(1)}, u32[]{:S(2)}, u32[]{:S(2)}) collective-permute-start(bf16[288,1152]{1,0:T(8,128)(2,1)S(1)} %pad_maximum_fusion.4), channel_id=1, source_target_pairs={{0,8},{8,0},{16,24},{24,16},{1,9},{9,1},{17,25},{25,17},{2,10},{10... | collective-permute-start | bytes 1990664 | tf_op jit(solution)/shard_map/ppermute | solution.py:165
  (93 other events, 2167.6 us)
Sparse Core Ops, SparseCore 0:
  11.5 123.5 all-gather.3
  138.6 100.8 all-gather.5
  242.4 102.4 all-gather.7
  413.9 79.7 reduce-scatter.3
  565.5 81.7 reduce-scatter.5
  785.2 110.4 reduce-scatter.7

commit v4 on v2

--- a/solution.py
+++ b/solution.py
@@ -395,6 +395,7 @@
     qkv_weight_grad = jnp.transpose(first_grad[:3], (2, 0, 1))
     out_weight_grad = first_grad[3]
     hidden_attn_grad = dot(jnp.concatenate(projected_grad, axis=1), qkv_full)
+    hidden_attn_grad = after(hidden_attn_grad, *first_parts)
     qkv_bias_part = jnp.concatenate([jnp.sum(part, axis=0, dtype=FULL) for part in projected_grad])
     shift_attn_grad = jnp.sum(hidden_attn_grad, axis=0)
     scale_attn_grad = jnp.sum(hidden_attn_grad * normed_attn, axis=0)
@@ -402,7 +403,7 @@
         normed_attn, attn_scale, hidden_attn_grad * (1.0 + scale_attn)
     )
     tokens_grad = after(tokens_grad.astype(LOW), fc1_part, *late)
-    cut = groups - 2
+    cut = groups // 2
     early = send_back(tokens_grad, slots, range(cut))
     tokens_grad = after(tokens_grad, first_part)
     late = send_back(tokens_grad, slots, range(cut, groups))
@@ -419,6 +420,7 @@
             gate_mlp_grad,
         ]
     ).astype(LOW)
+    mod_row = after(mod_row, first_part)
     mod_mine = pair_gather(mod_row.reshape(groups, mod_width), "tensor")
     mod_mine = lax.dynamic_index_in_dim(mod_mine, here, 1, False)
     mod_grad = pair_gather(mod_mine, "dp").reshape(-1, mod_width)

time: 918 us -> 941 us (1.025)
  waiting for transfers between devices: 217 us -> 252 us
  local copies, waits for them, and re-layouts: 134 us -> 116 us
    ppermute x32, waiting for transfers between devices: 60.7 us -> 127 us  [partner(): lax.ppermute(values, axis, [(i, i ^ bit) for i in range(lax.axis_size(axi...]
    ppermute x14, waiting for transfers between devices: 57.3 us -> 38.3 us  [send_back(): piece = lax.ppermute(piece, 'tensor', pairs)]
    unnamed x200 -> x190, local copies, waits for them, and re-layouts: 75.2 us -> 57.6 us
    reduce_scatter x3, waiting for transfers between devices: 48.1 us -> 35.6 us  [scatter(): return lax.psum_scatter(held, 'tensor', scatter_dimension=0, tiled=True)]
  transfers between devices with their start and end apart: 66 -> 66, of which waited for: 24 -> 24; matrix products, arithmetic and copies ran while one was open for 42% -> 39% of each run, Pallas kernels for 16% -> 16%
where the time goes in v4:
time: 941 us; the launch traced here: 924 us
  waiting for transfers between devices  252 us (27%)
  matrix products  202 us (21%)
  Pallas kernels  148 us (16%)
  starting transfers between devices  117 us (12%)
  local copies, waits for them, and re-layouts  116 us (12%)
  other arithmetic  71.8 us (8%)
  between operations  16.8 us (2%)
    dot_general x16, matrix products, dot(): return lax.dot_general(left, right, dims, preferred_element_type=FULL)  202 us
    ppermute x32, waiting for transfers between devices, partner(): lax.ppermute(values, axis, [(i, i ^ bit) for i in range(lax.axis_size(axi...  127 us
    pallas_call x2, Pallas kernels, attend_back(): pl.pallas_call(functools.partial(attend_back_kernel, heads, chunk * colum...  89.1 us
    pallas_call x2, Pallas kernels, attend(): pl.pallas_call(functools.partial(attend_kernel, heads, chunk * column(hea...  58.7 us
    unnamed x190, local copies, waits for them, and re-layouts  57.6 us
    ppermute x14, starting transfers between devices, to_slots(): piece = lax.ppermute(piece, 'tensor', pairs)  50.1 us
    ppermute x32, starting transfers between devices, partner(): lax.ppermute(values, axis, [(i, i ^ bit) for i in range(lax.axis_size(axi...  49 us
    ppermute x14, waiting for transfers between devices, send_back(): piece = lax.ppermute(piece, 'tensor', pairs)  38.3 us
  transfers between devices with their start and end apart: 66, of which 24 were waited for; matrix products, arithmetic and copies ran while one was open for 39% of the time, Pallas kernels for 16%

profile of v4, /device:TPU:0, one launch (start us, length us, event | category | flops | bytes accessed | tf_op | source)
XLA Modules:
  0.0 924.1 jit_solution(14630947647731314840)
XLA Ops:
  19.7 7.3 collective-permute-start.4
  34.6 16.1 %collective-permute-done.8 = f32[2,6192]{1,0:T(2,128)S(1)} collective-permute-done((f32[2,6192]{1,0:T(2,128)S(1)}, f32[2,6192]{1,0:T(2,128)S(1)}, u32[]{:S(2)}, u32[]{:S(2)}) %collective-permute-start.8) | collective-permute-done | bytes 49568 | tf_op jit(solution)/shard_map/ppermute | solution.py:165
  55.2 4.8 collective-permute-done.9
  60.7 6.2 collective-permute-start
  83.6 5.5 collective-permute-start.5
  102.2 33.0 %all-gather.4.cloned.1.call-done = bf16[4608,1152]{1,0:T(8,128)(2,1)} async-done(((bf16[144,1152]{1,0:T(8,128)(2,1)}), bf16[4608,1152]{1,0:T(8,128)(2,1)}) %all-gather.4.cloned.1.call-update) | async-done | bytes 10616848 | tf_op jit(solution)/shard_map/all_gather | solution.py:201
  135.1 5.6 copy.44
  145.1 8.0 slice.166
  153.1 15.5 %add_convert_fusion.projected = bf16[1024,3456]{1,0:T(8,128)(2,1)} fusion(bf16[3456,1152]{1,0:T(8,128)(2,1)} %bitcast.173, f32[3456]{0:T(1024)S(1)} %copy-done.50, bf16[1024,1152]{1,0:T(8,128)(2,1)S(1)} %copy-done.11, f32[1152]{0:T(1024)S(1)} %get-tuple-element.50, f32[1152]{0:T(1024)S(1)} %get-tuple-element.51, f32[1024]{0:T(1024)S(1)} %add_rsqrt_fusion.1, ...), kind=kOutput, calls=%fused_computation.13 | convolution fusion | flops 8167882752 | bytes 17431040 | tf_op jit(solution)/shard_map/dot_general | solution.py:22
  171.0 7.4 collective-permute-start.15
  182.4 4.1 collective-permute-start.10
  186.5 29.2 %shard_map.238 = bf16[1024,576]{1,0:T(8,128)(2,1)S(1)} custom-call(bf16[1024,3456]{1,0:T(8,128)(2,1)} %add_convert_fusion.projected), custom_call_target="tpu_custom_call" | custom-call | flops 17179869184 | bytes 4718592 | tf_op jit(solution)/shard_map/pallas_call | solution.py:77
  215.8 29.5 %shard_map.237 = bf16[1024,576]{1,0:T(8,128)(2,1)S(1)} custom-call(bf16[1024,3456]{1,0:T(8,128)(2,1)} %add_convert_fusion.projected), custom_call_target="tpu_custom_call" | custom-call | flops 17179869184 | bytes 4718592 | tf_op jit(solution)/shard_map/pallas_call | solution.py:77
  245.4 5.5 fusion.57
  253.7 21.1 %fusion.53 = f32[1024,4608]{1,0:T(8,128)} fusion(bf16[4608,1152]{1,0:T(8,128)(2,1)} %all-gather.6.cloned.1.call-done, f32[1024,1152]{1,0:T(8,128)} %copy-done.25, f32[1152]{0:T(1024)S(1)} %copy-done.57, f32[1152]{0:T(1024)S(1)} %copy-done.54, f32[1024]{0:T(1024)S(1)} %add_rsqrt_fusion, f32[1024]{0:T(1024)S(1)} %broadcast_multiply_fusion.4), kind=kOutput, calls=%fused_computation.262 | convolution fusion | flops 10877534208 | bytes 34227200 | tf_op jit(solution)/shard_map/dot_general | solution.py:22
  280.9 9.7 %collective-permute-done.12 = bf16[128,1152]{1,0:T(8,128)(2,1)S(1)} collective-permute-done((bf16[128,1152]{1,0:T(8,128)(2,1)S(1)}, bf16[128,1152]{1,0:T(8,128)(2,1)S(1)}, u32[]{:S(2)}, u32[]{:S(2)}) %collective-permute-start.12) | collective-permute-done | bytes 294944 | tf_op jit(solution)/shard_map/ppermute | solution.py:245
  290.6 6.0 collective-permute-done.13
  302.5 23.0 %convolution_convert_fusion.1 = bf16[4608,1152]{1,0:T(8,128)(2,1)} fusion(bf16[1024,1152]{1,0:T(8,128)(2,1)S(1)} %get-tuple-element.27, f32[1024,4608]{1,0:T(8,128)} %fusion.53, f32[4608]{0:T(1024)S(1)} %copy-done.49), kind=kOutput, calls=%fused_computation.3 | convolution fusion | flops 10924130304 | bytes 31868928 | tf_op jit(solution)/shard_map/dot_general | solution.py:22
  325.5 5.5 constant_dynamic-slice_fusion.6
  331.0 9.8 %collective-permute-done.17 = bf16[8,288,1152]{2,1,0:T(8,128)(2,1)} collective-permute-done((bf16[8,288,1152]{2,1,0:T(8,128)(2,1)}, bf16[8,288,1152]{2,1,0:T(8,128)(2,1)}, u32[]{:S(2)}, u32[]{:S(2)}) %collective-permute-start.17) | collective-permute-done | bytes 5308448 | tf_op jit(solution)/shard_map/ppermute | solution.py:165
  340.7 5.8 add_convert_fusion.2
  351.4 28.9 %fusion.6 = bf16[1024,4608]{1,0:T(8,128)(2,1)} fusion(f32[1024,4608]{1,0:T(8,128)} %fusion.53, f32[4608]{0:T(1024)S(1)} %copy-done.49, bf16[1024,1152]{1,0:T(8,128)(2,1)} %copy-done.31, bf16[4608,1152]{1,0:T(8,128)(2,1)} %all-gather.8.cloned.1.call-done), kind=kOutput, calls=%fused_computation.10 | convolution fusion | flops 10970726400 | bytes 41306112 | tf_op jit(solution)/shard_map/dot_general | solution.py:22
  380.3 17.1 %convolution_convert_fusion = bf16[4608,1152]{1,0:T(8,128)(2,1)S(1)} fusion(bf16[1024,4608]{1,0:T(8,128)(2,1)} %fusion.6, f32[1024,1152]{1,0:T(8,128)} %copy-done.25, f32[1152]{0:T(1024)S(1)} %copy-done.57, f32[1152]{0:T(1024)S(1)} %copy-done.54, f32[1024]{0:T(1024)S(1)} %add_rsqrt_fusion, f32[1024]{0:T(1024)S(1)} %broadcast_multiply_fusion.4), kind=kOutput, calls=%fused_computation.2 | convolution fusion | flops 10882842624 | bytes 24790016 | tf_op jit(solution)/shard_map/dot_general | solution.py:22
  404.5 6.0 collective-permute-done.18
  414.6 5.8 convert_reduce_fusion
  420.3 21.7 %multiply_reduce_fusion.1 = (bf16[1152]{0:T(1024)(128)(2,1)}, f32[1024]{0:T(1024)S(1)}, f32[1024]{0:T(1024)S(1)}, bf16[1152]{0:T(1024)(128)(2,1)}, f32[1024,1152]{1,0:T(8,128)}) fusion(f32[1024,1152]{1,0:T(8,128)} %copy-done.25, f32[1024]{0:T(1024)S(1)} %add_rsqrt_fusion, f32[1024]{0:T(1024)S(1)} %broadcast_multiply_fusion.4, f32[1152]{0:T(1024)S(1)} %copy-done.54, ...), kind=kOutput, calls=%fused_computation.60 | convolution fusion | flops 10882248704 | bytes 29516800 | tf_op jit(solution)/shard_map/dot_general | solution.py:22
  442.1 26.2 %multiply_reduce_fusion = (bf16[1152]{0:T(1024)(128)(2,1)}, bf16[1024,1152]{1,0:T(8,128)(2,1)}, f32[1152]{0:T(1024)S(1)}, bf16[1024,1152]{1,0:T(8,128)(2,1)}, f32[1024,1152]{1,0:T(8,128)}) fusion(bf16[1024,1152]{1,0:T(8,128)(2,1)} %copy-done.27, f32[]{:T(128)S(6)} %convert_element_type.188, f32[1024,1152]{1,0:T(8,128)S(1)} %bitcast.176, ...), kind=kOutput, calls=%fused_computation.59 | convolution fusion | flops 10943592448 | bytes 50785028 | tf_op jit(solution)/shard_map/dot_general | solution.py:22
  468.3 5.2 convolution_convert_fusion.4
  476.5 4.8 convolution_convert_fusion.5.attended_grad
  481.3 5.5 add_convert_fusion.1
  501.5 44.0 %shard_map.239 = bf16[1024,1728]{1,0:T(8,128)(2,1)S(1)} custom-call(bf16[1024,3456]{1,0:T(8,128)(2,1)} %add_convert_fusion.projected, bf16[1024,1152]{1,0:T(8,128)(2,1)S(1)} %copy-done.4), custom_call_target="tpu_custom_call" | custom-call | flops 34359738368 | bytes 8257536 | tf_op jit(solution)/shard_map/pallas_call | solution.py:138
  554.4 7.9 convolution_convert_fusion.3
  566.5 7.1 collective-permute-done.58
  580.8 45.0 %shard_map.240 = bf16[1024,1728]{1,0:T(8,128)(2,1)S(1)} custom-call(bf16[1024,3456]{1,0:T(8,128)(2,1)} %add_convert_fusion.projected, bf16[1024,1152]{1,0:T(8,128)(2,1)S(1)} %copy-done.5), custom_call_target="tpu_custom_call" | custom-call | flops 34359738368 | bytes 8257536 | tf_op jit(solution)/shard_map/pallas_call | solution.py:138
  632.6 5.9 convolution_convert_fusion.2
  639.5 31.7 %collective-permute-done.25 = bf16[128,1152]{1,0:T(8,128)(2,1)S(1)} collective-permute-done((bf16[128,1152]{1,0:T(8,128)(2,1)S(1)}, bf16[128,1152]{1,0:T(8,128)(2,1)S(1)}, u32[]{:S(2)}, u32[]{:S(2)}) %collective-permute-start.25) | collective-permute-done | bytes 294944 | tf_op jit(solution)/shard_map/ppermute | solution.py:260
  690.6 10.3 %collective-permute-start.52 = (f32[10368]{0:T(1024)S(1)}, f32[10368]{0:T(1024)S(1)}, u32[]{:S(2)}, u32[]{:S(2)}) collective-permute-start(f32[10368]{0:T(1024)S(1)} %add.353), channel_id=1, source_target_pairs={{0,2},{1,3},{2,0},{3,1},{4,6},{5,7},{6,4},{7,5},{8,10},{9,11},{10,... | collective-permute-start | bytes 124424 | tf_op jit(solution)/shard_map/ppermute | solution.py:165
  713.3 33.2 %collective-permute-done.56 = bf16[144,1152]{1,0:T(8,128)(2,1)S(1)} collective-permute-done((bf16[144,1152]{1,0:T(8,128)(2,1)}, bf16[144,1152]{1,0:T(8,128)(2,1)S(1)}, u32[]{:S(2)}, u32[]{:S(2)}) %collective-permute-start.56) | collective-permute-done | bytes 331808 | tf_op jit(solution)/shard_map/ppermute | solution.py:165
  751.1 16.0 %fusion.7 = f32[1024,1152]{1,0:T(8,128)} fusion(bf16[3456,1152]{1,0:T(8,128)(2,1)} %bitcast.174, bf16[1024,1728]{1,0:T(8,128)(2,1)} %copy-done.3, bf16[1024,1728]{1,0:T(8,128)(2,1)} %copy-done.1), kind=kOutput, calls=%fused_computation.22 | convolution fusion | flops 8167882752 | bytes 19759104 | tf_op jit(solution)/shard_map/dot_general | solution.py:22
  772.5 4.8 fusion.24
  777.4 6.0 multiply_reduce_fusion.2
  786.2 33.1 %reduce-scatter.8.cloned.1.call-done = bf16[144,1152]{1,0:T(8,128)(2,1)} async-done(((bf16[1152,1152]{1,0:T(8,128)(2,1)}), bf16[144,1152]{1,0:T(8,128)(2,1)}) %reduce-scatter.8.cloned.1.call-update) | async-done | bytes 331792 | tf_op jit(solution)/shard_map/reduce_scatter | solution.py:219
  825.2 6.7 collective-permute-start.40
  831.9 6.6 collective-permute-done.32
  838.5 8.1 collective-permute-done.40
  846.6 5.3 collective-permute-start.41
  867.0 4.6 collective-permute-start.44
  871.6 22.8 %collective-permute-done.44 = f32[6,1152]{1,0:T(8,128)S(1)} collective-permute-done((f32[6,1152]{1,0:T(8,128)S(1)}, f32[6,1152]{1,0:T(8,128)S(1)}, u32[]{:S(2)}, u32[]{:S(2)}) %collective-permute-start.44) | collective-permute-done | bytes 27680 | tf_op jit(solution)/shard_map/ppermute | solution.py:165
  (434 shorter events, 228.3 us)
Async XLA Ops:
  7.2 127.9 %all-gather.4.cloned.1.call-start = ((), (), s32[]{:S(2)}) async-start(), calls=%async_computation.3 | async-start | bytes 10948608 | tf_op jit(solution)/shard_map/all_gather | solution.py:201
  9.8 243.9 %all-gather.6.cloned.1.call-start = ((), (), s32[]{:S(2)}) async-start(), calls=%async_computation.4 | async-start | bytes 10948608 | tf_op jit(solution)/shard_map/all_gather | solution.py:201
  11.6 339.8 %all-gather.8.cloned.1.call-start = ((), (), s32[]{:S(2)}) async-start(), calls=%async_computation.5 | async-start | bytes 10948608 | tf_op jit(solution)/shard_map/all_gather | solution.py:201
  12.8 19.8 %collective-permute-start.7 = (f32[1,6192]{1,0:T(1,128)S(1)}, f32[1,6192]{1,0:T(1,128)S(1)}, u32[]{:S(2)}, u32[]{:S(2)}) collective-permute-start(f32[1,6192]{1,0:T(1,128)S(1)} %broadcast_in_dim.6), channel_id=1, source_target_pairs={{0,1},{1,0},{2,3},{3,2},{4,5},{5,4},{6,7},{7,6},{8,9},{9,8},{10,11... | collective-permute-start | bytes 74312 | tf_op jit(solution)/shard_map/ppermute | solution.py:165
  18.3 77.3 %collective-permute-start.6 = (bf16[128,1152]{1,0:T(8,128)(2,1)S(1)}, bf16[128,1152]{1,0:T(8,128)(2,1)}, u32[]{:S(2)}, u32[]{:S(2)}) collective-permute-start(bf16[128,1152]{1,0:T(8,128)(2,1)S(1)} %get-tuple-element.92), channel_id=1, source_target_pairs={{2,1},{3,2},{4,3},{5,4},{6,5},{7,6},{10,9},{11,10},{12,11},{13,12}... | collective-permute-start | bytes 884744 | tf_op jit(solution)/shard_map/ppermute | solution.py:245
  19.7 73.5 %collective-permute-start.4 = (bf16[128,1152]{1,0:T(8,128)(2,1)S(1)}, bf16[128,1152]{1,0:T(8,128)(2,1)}, u32[]{:S(2)}, u32[]{:S(2)}) collective-permute-start(bf16[128,1152]{1,0:T(8,128)(2,1)S(1)} %get-tuple-element.93), channel_id=1, source_target_pairs={{0,5},{1,6},{4,1},{5,2},{6,3},{7,4},{8,13},{9,14},{12,9},{13,10},{... | collective-permute-start | bytes 884744 | tf_op jit(solution)/shard_map/ppermute | solution.py:245
  27.0 64.5 %collective-permute-start.3 = (bf16[128,1152]{1,0:T(8,128)(2,1)S(1)}, bf16[128,1152]{1,0:T(8,128)(2,1)}, u32[]{:S(2)}, u32[]{:S(2)}) collective-permute-start(bf16[128,1152]{1,0:T(8,128)(2,1)S(1)} %get-tuple-element.94), channel_id=1, source_target_pairs={{0,4},{1,5},{2,6},{5,1},{6,2},{7,3},{8,12},{9,13},{10,14},{13,9},{... | collective-permute-start | bytes 884744 | tf_op jit(solution)/shard_map/ppermute | solution.py:245
  29.0 54.6 %collective-permute-start.1 = (bf16[128,1152]{1,0:T(8,128)(2,1)}, bf16[128,1152]{1,0:T(8,128)(2,1)}, u32[]{:S(2)}, u32[]{:S(2)}) collective-permute-start(bf16[128,1152]{1,0:T(8,128)(2,1)} %get-tuple-element.96), channel_id=1, source_target_pairs={{0,2},{1,3},{2,4},{3,5},{4,6},{7,1},{8,10},{9,11},{10,12},{11,13},... | collective-permute-start | bytes 884744 | tf_op jit(solution)/shard_map/ppermute | solution.py:245
  32.7 18.0 %collective-permute-start.8 = (f32[2,6192]{1,0:T(2,128)S(1)}, f32[2,6192]{1,0:T(2,128)S(1)}, u32[]{:S(2)}, u32[]{:S(2)}) collective-permute-start(f32[2,6192]{1,0:T(2,128)S(1)} %pad_maximum_fusion.10), channel_id=1, source_target_pairs={{0,2},{1,3},{2,0},{3,1},{4,6},{5,7},{6,4},{7,5},{8,10},{9,11},{10,... | collective-permute-start | bytes 148616 | tf_op jit(solution)/shard_map/ppermute | solution.py:165
  34.6 459.3 %reduce-scatter.4.cloned.1.call-start = ((), (), s32[]{:S(2)}) async-start(), calls=%async_computation.6 | async-start | bytes 2985984 | tf_op jit(solution)/shard_map/reduce_scatter | solution.py:219
  60.7 17.1 %collective-permute-start = (bf16[128,1152]{1,0:T(8,128)(2,1)}, bf16[128,1152]{1,0:T(8,128)(2,1)}, u32[]{:S(2)}, u32[]{:S(2)}) collective-permute-start(bf16[128,1152]{1,0:T(8,128)(2,1)} %get-tuple-element.97), channel_id=1, source_target_pairs={{0,1},{1,2},{2,3},{3,4},{4,5},{5,6},{8,9},{9,10},{10,11},{11,12},{... | collective-permute-start | bytes 884744 | tf_op jit(solution)/shard_map/ppermute | solution.py:245
  77.7 13.0 %collective-permute-start.2 = (bf16[128,1152]{1,0:T(8,128)(2,1)}, bf16[128,1152]{1,0:T(8,128)(2,1)S(1)}, u32[]{:S(2)}, u32[]{:S(2)}) collective-permute-start(bf16[128,1152]{1,0:T(8,128)(2,1)} %get-tuple-element.95), channel_id=1, source_target_pairs={{0,3},{1,4},{2,5},{3,6},{6,1},{7,2},{8,11},{9,12},{10,13},{11,14},... | collective-permute-start | bytes 884744 | tf_op jit(solution)/shard_map/ppermute | solution.py:245
  169.6 129.0 %collective-permute-start.16 = (bf16[128,1152]{1,0:T(8,128)(2,1)S(1)}, bf16[128,1152]{1,0:T(8,128)(2,1)}, u32[]{:S(2)}, u32[]{:S(2)}) collective-permute-start(bf16[128,1152]{1,0:T(8,128)(2,1)S(1)} %get-tuple-element.85), channel_id=1, source_target_pairs={{2,1},{3,2},{4,3},{5,4},{6,5},{7,6},{10,9},{11,10},{12,11},{13,12}... | collective-permute-start | bytes 884744 | tf_op jit(solution)/shard_map/ppermute | solution.py:245
  171.0 126.6 %collective-permute-start.15 = (bf16[128,1152]{1,0:T(8,128)(2,1)S(1)}, bf16[128,1152]{1,0:T(8,128)(2,1)}, u32[]{:S(2)}, u32[]{:S(2)}) collective-permute-start(bf16[128,1152]{1,0:T(8,128)(2,1)S(1)} %get-tuple-element.86), channel_id=1, source_target_pairs={{0,6},{3,1},{4,2},{5,3},{6,4},{7,5},{8,14},{11,9},{12,10},{13,11},... | collective-permute-start | bytes 884744 | tf_op jit(solution)/shard_map/ppermute | solution.py:245
  178.4 118.2 %collective-permute-start.14 = (bf16[128,1152]{1,0:T(8,128)(2,1)S(1)}, bf16[128,1152]{1,0:T(8,128)(2,1)}, u32[]{:S(2)}, u32[]{:S(2)}) collective-permute-start(bf16[128,1152]{1,0:T(8,128)(2,1)S(1)} %get-tuple-element.87), channel_id=1, source_target_pairs={{0,5},{1,6},{4,1},{5,2},{6,3},{7,4},{8,13},{9,14},{12,9},{13,10},{... | collective-permute-start | bytes 884744 | tf_op jit(solution)/shard_map/ppermute | solution.py:245
  180.4 98.2 %collective-permute-start.11 = (bf16[128,1152]{1,0:T(8,128)(2,1)}, bf16[128,1152]{1,0:T(8,128)(2,1)}, u32[]{:S(2)}, u32[]{:S(2)}) collective-permute-start(bf16[128,1152]{1,0:T(8,128)(2,1)} %get-tuple-element.90), channel_id=1, source_target_pairs={{0,2},{1,3},{2,4},{3,5},{4,6},{7,1},{8,10},{9,11},{10,12},{11,13},... | collective-permute-start | bytes 884744 | tf_op jit(solution)/shard_map/ppermute | solution.py:245
  182.4 93.3 %collective-permute-start.10 = (bf16[128,1152]{1,0:T(8,128)(2,1)}, bf16[128,1152]{1,0:T(8,128)(2,1)}, u32[]{:S(2)}, u32[]{:S(2)}) collective-permute-start(bf16[128,1152]{1,0:T(8,128)(2,1)} %get-tuple-element.91), channel_id=1, source_target_pairs={{0,1},{1,2},{2,3},{3,4},{4,5},{5,6},{8,9},{9,10},{10,11},{11,12},{... | collective-permute-start | bytes 884744 | tf_op jit(solution)/shard_map/ppermute | solution.py:245
  275.8 14.8 %collective-permute-start.12 = (bf16[128,1152]{1,0:T(8,128)(2,1)S(1)}, bf16[128,1152]{1,0:T(8,128)(2,1)S(1)}, u32[]{:S(2)}, u32[]{:S(2)}) collective-permute-start(bf16[128,1152]{1,0:T(8,128)(2,1)S(1)} %copy-done.35), channel_id=1, source_target_pairs={{0,3},{1,4},{2,5},{3,6},{6,1},{7,2},{8,11},{9,12},{10,13},{11,14},... | collective-permute-start | bytes 884744 | tf_op jit(solution)/shard_map/ppermute | solution.py:245
  278.6 18.0 %collective-permute-start.13 = (bf16[128,1152]{1,0:T(8,128)(2,1)S(1)}, bf16[128,1152]{1,0:T(8,128)(2,1)S(1)}, u32[]{:S(2)}, u32[]{:S(2)}) collective-permute-start(bf16[128,1152]{1,0:T(8,128)(2,1)S(1)} %get-tuple-element.88), channel_id=1, source_target_pairs={{0,4},{1,5},{2,6},{5,1},{6,2},{7,3},{8,12},{9,13},{10,14},{13,9},{... | collective-permute-start | bytes 884744 | tf_op jit(solution)/shard_map/ppermute | solution.py:245
  350.5 60.0 %collective-permute-start.18 = (bf16[8,144,1152]{2,1,0:T(8,128)(2,1)}, bf16[8,144,1152]{2,1,0:T(8,128)(2,1)}, u32[]{:S(2)}, u32[]{:S(2)}) collective-permute-start(bf16[8,144,1152]{2,1,0:T(8,128)(2,1)} %constant_dynamic-slice_fusion.5), channel_id=1, source_target_pairs={{0,16},{8,24},{16,0},{24,8},{1,17},{9,25},{17,1},{25,9},{2,18},{10... | collective-permute-start | bytes 7962632 | tf_op jit(solution)/shard_map/ppermute | solution.py:165
  404.5 76.8 %collective-permute-start.19 = (bf16[8,288,1152]{2,1,0:T(8,128)(2,1)}, bf16[8,288,1152]{2,1,0:T(8,128)(2,1)}, u32[]{:S(2)}, u32[]{:S(2)}) collective-permute-start(bf16[8,288,1152]{2,1,0:T(8,128)(2,1)} %constant_dynamic-slice_fusion.4), channel_id=1, source_target_pairs={{0,8},{8,0},{16,24},{24,16},{1,9},{9,1},{17,25},{25,17},{2,10},{10... | collective-permute-start | bytes 15925256 | tf_op jit(solution)/shard_map/ppermute | solution.py:165
  414.5 294.5 %reduce-scatter.6.cloned.1.call-start = ((), (), s32[]{:S(2)}) async-start(), calls=%async_computation.7 | async-start | bytes 2985984 | tf_op jit(solution)/shard_map/reduce_scatter | solution.py:219
  490.8 59.2 %collective-permute-start.24 = (bf16[8,144,1152]{2,1,0:T(8,128)(2,1)}, bf16[8,144,1152]{2,1,0:T(8,128)(2,1)}, u32[]{:S(2)}, u32[]{:S(2)}) collective-permute-start(bf16[8,144,1152]{2,1,0:T(8,128)(2,1)} %constant_dynamic-slice_fusion.3), channel_id=1, source_target_pairs={{0,16},{8,24},{16,0},{24,8},{1,17},{9,25},{17,1},{25,9},{2,18},{10... | collective-permute-start | bytes 7962632 | tf_op jit(solution)/shard_map/ppermute | solution.py:165
  495.9 79.6 %collective-permute-start.22 = (bf16[128,1152]{1,0:T(8,128)(2,1)}, bf16[128,1152]{1,0:T(8,128)(2,1)}, u32[]{:S(2)}, u32[]{:S(2)}) collective-permute-start(bf16[128,1152]{1,0:T(8,128)(2,1)} %get-tuple-element.82), channel_id=1, source_target_pairs={{3,0},{4,1},{5,2},{6,3},{1,6},{2,7},{11,8},{12,9},{13,10},{14,11},... | collective-permute-start | bytes 884744 | tf_op jit(solution)/shard_map/ppermute | solution.py:260
  497.2 76.6 %collective-permute-start.21 = (bf16[128,1152]{1,0:T(8,128)(2,1)}, bf16[128,1152]{1,0:T(8,128)(2,1)}, u32[]{:S(2)}, u32[]{:S(2)}) collective-permute-start(bf16[128,1152]{1,0:T(8,128)(2,1)} %get-tuple-element.83), channel_id=1, source_target_pairs={{2,0},{3,1},{4,2},{5,3},{6,4},{1,7},{10,8},{11,9},{12,10},{13,11},... | collective-permute-start | bytes 884744 | tf_op jit(solution)/shard_map/ppermute | solution.py:260
  498.5 66.3 %collective-permute-start.20 = (bf16[128,1152]{1,0:T(8,128)(2,1)}, bf16[128,1152]{1,0:T(8,128)(2,1)}, u32[]{:S(2)}, u32[]{:S(2)}) collective-permute-start(bf16[128,1152]{1,0:T(8,128)(2,1)} %get-tuple-element.84), channel_id=1, source_target_pairs={{1,0},{2,1},{3,2},{4,3},{5,4},{6,5},{9,8},{10,9},{11,10},{12,11},{... | collective-permute-start | bytes 884744 | tf_op jit(solution)/shard_map/ppermute | solution.py:260
  553.9 265.4 %reduce-scatter.8.cloned.1.call-start = ((), (), s32[]{:S(2)}) async-start(), calls=%async_computation.8 | async-start | bytes 2985984 | tf_op jit(solution)/shard_map/reduce_scatter | solution.py:219
  563.3 15.9 %collective-permute-start.23 = (bf16[8,144,1152]{2,1,0:T(8,128)(2,1)S(1)}, bf16[8,144,1152]{2,1,0:T(8,128)(2,1)S(1)}, u32[]{:S(2)}, u32[]{:S(2)}) collective-permute-start(bf16[8,144,1152]{2,1,0:T(8,128)(2,1)S(1)} %fusion.28), channel_id=1, source_target_pairs={{0,8},{8,0},{16,24},{24,16},{1,9},{9,1},{17,25},{25,17},{2,10},{10... | collective-permute-start | bytes 7962632 | tf_op jit(solution)/shard_map/ppermute | solution.py:165
  626.0 47.5 %collective-permute-start.28 = (bf16[128,1152]{1,0:T(8,128)(2,1)S(1)}, bf16[128,1152]{1,0:T(8,128)(2,1)S(1)}, u32[]{:S(2)}, u32[]{:S(2)}) collective-permute-start(bf16[128,1152]{1,0:T(8,128)(2,1)S(1)} %get-tuple-element.78), channel_id=1, source_target_pairs={{1,2},{2,3},{3,4},{4,5},{5,6},{6,7},{9,10},{10,11},{11,12},{12,13}... | collective-permute-start | bytes 884744 | tf_op jit(solution)/shard_map/ppermute | solution.py:260
  626.8 46.0 %collective-permute-start.27 = (bf16[128,1152]{1,0:T(8,128)(2,1)S(1)}, bf16[128,1152]{1,0:T(8,128)(2,1)S(1)}, u32[]{:S(2)}, u32[]{:S(2)}) collective-permute-start(bf16[128,1152]{1,0:T(8,128)(2,1)S(1)} %get-tuple-element.79), channel_id=1, source_target_pairs={{6,0},{1,3},{2,4},{3,5},{4,6},{5,7},{14,8},{9,11},{10,12},{11,13},... | collective-permute-start | bytes 884744 | tf_op jit(solution)/shard_map/ppermute | solution.py:260
  628.3 43.6 %collective-permute-start.26 = (bf16[128,1152]{1,0:T(8,128)(2,1)S(1)}, bf16[128,1152]{1,0:T(8,128)(2,1)S(1)}, u32[]{:S(2)}, u32[]{:S(2)}) collective-permute-start(bf16[128,1152]{1,0:T(8,128)(2,1)S(1)} %get-tuple-element.80), channel_id=1, source_target_pairs={{5,0},{6,1},{1,4},{2,5},{3,6},{4,7},{13,8},{14,9},{9,12},{10,13},{... | collective-permute-start | bytes 884744 | tf_op jit(solution)/shard_map/ppermute | solution.py:260
  629.6 41.5 %collective-permute-start.25 = (bf16[128,1152]{1,0:T(8,128)(2,1)S(1)}, bf16[128,1152]{1,0:T(8,128)(2,1)S(1)}, u32[]{:S(2)}, u32[]{:S(2)}) collective-permute-start(bf16[128,1152]{1,0:T(8,128)(2,1)S(1)} %get-tuple-element.81), channel_id=1, source_target_pairs={{4,0},{5,1},{6,2},{1,5},{2,6},{3,7},{12,8},{13,9},{14,10},{9,13},{... | collective-permute-start | bytes 884744 | tf_op jit(solution)/shard_map/ppermute | solution.py:260
  632.2 78.3 %collective-permute-start.30 = (bf16[8,72,1152]{2,1,0:T(8,128)(2,1)}, bf16[8,72,1152]{2,1,0:T(8,128)(2,1)}, u32[]{:S(2)}, u32[]{:S(2)}) collective-permute-start(bf16[8,72,1152]{2,1,0:T(8,128)(2,1)} %constant_dynamic-slice_fusion.2), channel_id=1, source_target_pairs={{0,16},{8,24},{16,0},{24,8},{1,17},{9,25},{17,1},{25,9},{2,18},{10... | collective-permute-start | bytes 3981320 | tf_op jit(solution)/shard_map/ppermute | solution.py:165
  690.6 13.1 %collective-permute-start.52 = (f32[10368]{0:T(1024)S(1)}, f32[10368]{0:T(1024)S(1)}, u32[]{:S(2)}, u32[]{:S(2)}) collective-permute-start(f32[10368]{0:T(1024)S(1)} %add.353), channel_id=1, source_target_pairs={{0,2},{1,3},{2,0},{3,1},{4,6},{5,7},{6,4},{7,5},{8,10},{9,11},{10,... | collective-permute-start | bytes 124424 | tf_op jit(solution)/shard_map/ppermute | solution.py:165
  708.3 39.4 %collective-permute-start.31 = (bf16[8,72,1152]{2,1,0:T(8,128)(2,1)}, bf16[8,72,1152]{2,1,0:T(8,128)(2,1)}, u32[]{:S(2)}, u32[]{:S(2)}) collective-permute-start(bf16[8,72,1152]{2,1,0:T(8,128)(2,1)} %constant_dynamic-slice_fusion.1), channel_id=1, source_target_pairs={{0,16},{8,24},{16,0},{24,8},{1,17},{9,25},{17,1},{25,9},{2,18},{10... | collective-permute-start | bytes 3981320 | tf_op jit(solution)/shard_map/ppermute | solution.py:165
  709.0 37.5 %collective-permute-start.56 = (bf16[144,1152]{1,0:T(8,128)(2,1)}, bf16[144,1152]{1,0:T(8,128)(2,1)S(1)}, u32[]{:S(2)}, u32[]{:S(2)}) collective-permute-start(bf16[144,1152]{1,0:T(8,128)(2,1)} %reduce-scatter.6.cloned.1.call-done), channel_id=1, source_target_pairs={{0,16},{8,24},{16,0},{24,8},{1,17},{9,25},{17,1},{25,9},{2,18},{10... | collective-permute-start | bytes 995336 | tf_op jit(solution)/shard_map/ppermute | solution.py:165
  712.5 54.6 %collective-permute-start.55 = (f32[10368]{0:T(1024)S(1)}, f32[10368]{0:T(1024)S(1)}, u32[]{:S(2)}, u32[]{:S(2)}) collective-permute-start(f32[10368]{0:T(1024)S(1)} %add.356), channel_id=1, source_target_pairs={{0,16},{8,24},{16,0},{24,8},{1,17},{9,25},{17,1},{25,9},{2,18},{10... | collective-permute-start | bytes 124424 | tf_op jit(solution)/shard_map/ppermute | solution.py:165
  747.7 21.8 %collective-permute-start.57 = (bf16[288,1152]{1,0:T(8,128)(2,1)S(1)}, bf16[288,1152]{1,0:T(8,128)(2,1)}, u32[]{:S(2)}, u32[]{:S(2)}) collective-permute-start(bf16[288,1152]{1,0:T(8,128)(2,1)S(1)} %pad_maximum_fusion.5), channel_id=1, source_target_pairs={{0,8},{8,0},{16,24},{24,16},{1,9},{9,1},{17,25},{25,17},{2,10},{10... | collective-permute-start | bytes 1990664 | tf_op jit(solution)/shard_map/ppermute | solution.py:165
  821.3 33.3 %collective-permute-start.34 = (bf16[128,1152]{1,0:T(8,128)(2,1)S(1)}, bf16[128,1152]{1,0:T(8,128)(2,1)S(1)}, u32[]{:S(2)}, u32[]{:S(2)}) collective-permute-start(bf16[128,1152]{1,0:T(8,128)(2,1)S(1)} %get-tuple-element.75), channel_id=1, source_target_pairs={{3,0},{4,1},{5,2},{6,3},{1,6},{2,7},{11,8},{12,9},{13,10},{14,11},... | collective-permute-start | bytes 884744 | tf_op jit(solution)/shard_map/ppermute | solution.py:260
  822.6 29.4 %collective-permute-start.33 = (bf16[128,1152]{1,0:T(8,128)(2,1)S(1)}, bf16[128,1152]{1,0:T(8,128)(2,1)S(1)}, u32[]{:S(2)}, u32[]{:S(2)}) collective-permute-start(bf16[128,1152]{1,0:T(8,128)(2,1)S(1)} %get-tuple-element.76), channel_id=1, source_target_pairs={{2,0},{3,1},{4,2},{5,3},{6,4},{1,7},{10,8},{11,9},{12,10},{13,11},... | collective-permute-start | bytes 884744 | tf_op jit(solution)/shard_map/ppermute | solution.py:260
  823.9 14.6 %collective-permute-start.32 = (bf16[128,1152]{1,0:T(8,128)(2,1)S(1)}, bf16[128,1152]{1,0:T(8,128)(2,1)S(1)}, u32[]{:S(2)}, u32[]{:S(2)}) collective-permute-start(bf16[128,1152]{1,0:T(8,128)(2,1)S(1)} %get-tuple-element.77), channel_id=1, source_target_pairs={{1,0},{2,1},{3,2},{4,3},{5,4},{6,5},{9,8},{10,9},{11,10},{12,11},{... | collective-permute-start | bytes 884744 | tf_op jit(solution)/shard_map/ppermute | solution.py:260
  825.2 21.4 %collective-permute-start.40 = (bf16[2,8,864]{2,1,0:T(8,128)(2,1)S(1)}, bf16[2,8,864]{2,1,0:T(8,128)(2,1)S(1)}, u32[]{:S(2)}, u32[]{:S(2)}) collective-permute-start(bf16[2,8,864]{2,1,0:T(8,128)(2,1)S(1)} %pad_maximum_fusion.13), channel_id=1, source_target_pairs={{0,2},{1,3},{2,0},{3,1},{4,6},{5,7},{6,4},{7,5},{8,10},{9,11},{10,... | collective-permute-start | bytes 82952 | tf_op jit(solution)/shard_map/ppermute | solution.py:165
  854.7 12.3 %collective-permute-start.47 = (bf16[1,8,864]{2,1,0:T(8,128)(2,1)S(1)}, bf16[1,8,864]{2,1,0:T(8,128)(2,1)S(1)}, u32[]{:S(2)}, u32[]{:S(2)}) collective-permute-start(bf16[1,8,864]{2,1,0:T(8,128)(2,1)S(1)} %bitcast.185), channel_id=1, source_target_pairs={{0,8},{8,0},{16,24},{24,16},{1,9},{9,1},{17,25},{25,17},{2,10},{10... | collective-permute-start | bytes 41480 | tf_op jit(solution)/shard_map/ppermute | solution.py:165
  862.1 46.3 %collective-permute-start.38 = (bf16[128,1152]{1,0:T(8,128)(2,1)S(1)}, bf16[128,1152]{1,0:T(8,128)(2,1)S(1)}, u32[]{:S(2)}, u32[]{:S(2)}) collective-permute-start(bf16[128,1152]{1,0:T(8,128)(2,1)S(1)} %get-tuple-element.71), channel_id=1, source_target_pairs={{1,2},{2,3},{3,4},{4,5},{5,6},{6,7},{9,10},{10,11},{11,12},{12,13}... | collective-permute-start | bytes 884744 | tf_op jit(solution)/shard_map/ppermute | solution.py:260
  862.8 45.6 %collective-permute-start.37 = (bf16[128,1152]{1,0:T(8,128)(2,1)S(1)}, bf16[128,1152]{1,0:T(8,128)(2,1)S(1)}, u32[]{:S(2)}, u32[]{:S(2)}) collective-permute-start(bf16[128,1152]{1,0:T(8,128)(2,1)S(1)} %get-tuple-element.72), channel_id=1, source_target_pairs={{6,0},{1,3},{2,4},{3,5},{4,6},{5,7},{14,8},{9,11},{10,12},{11,13},... | collective-permute-start | bytes 884744 | tf_op jit(solution)/shard_map/ppermute | solution.py:260
  864.1 44.2 %collective-permute-start.36 = (bf16[128,1152]{1,0:T(8,128)(2,1)S(1)}, bf16[128,1152]{1,0:T(8,128)(2,1)S(1)}, u32[]{:S(2)}, u32[]{:S(2)}) collective-permute-start(bf16[128,1152]{1,0:T(8,128)(2,1)S(1)} %get-tuple-element.73), channel_id=1, source_target_pairs={{5,0},{6,1},{1,4},{2,5},{3,6},{4,7},{13,8},{14,9},{9,12},{10,13},{... | collective-permute-start | bytes 884744 | tf_op jit(solution)/shard_map/ppermute | solution.py:260
  865.4 42.9 %collective-permute-start.35 = (bf16[128,1152]{1,0:T(8,128)(2,1)S(1)}, bf16[128,1152]{1,0:T(8,128)(2,1)S(1)}, u32[]{:S(2)}, u32[]{:S(2)}) collective-permute-start(bf16[128,1152]{1,0:T(8,128)(2,1)S(1)} %get-tuple-element.74), channel_id=1, source_target_pairs={{4,0},{5,1},{6,2},{1,5},{2,6},{3,7},{12,8},{13,9},{14,10},{9,13},{... | collective-permute-start | bytes 884744 | tf_op jit(solution)/shard_map/ppermute | solution.py:260
  867.0 27.4 %collective-permute-start.44 = (f32[6,1152]{1,0:T(8,128)S(1)}, f32[6,1152]{1,0:T(8,128)S(1)}, u32[]{:S(2)}, u32[]{:S(2)}) collective-permute-start(f32[6,1152]{1,0:T(8,128)S(1)} %add.351), channel_id=1, source_target_pairs={{0,4},{1,5},{2,6},{3,7},{4,0},{5,1},{6,2},{7,3},{8,12},{9,13},{10,... | collective-permute-start | bytes 82952 | tf_op jit(solution)/shard_map/ppermute | solution.py:165
  (88 other events, 1716.4 us)
Sparse Core Ops, SparseCore 0:
  11.5 123.5 all-gather.3
  138.6 100.7 all-gather.5
  242.3 102.5 all-gather.7
  414.6 79.1 reduce-scatter.3
  554.0 80.5 reduce-scatter.5
  751.2 68.0 reduce-scatter.7
